TPU v7x, 512 devices: a whole 4x8x8 slice. The times are simulated.
512 devices in a mesh: ctx: 64 (over x, y, core), sess: 8 (over z).
Axes of the slice: x: 4, y: 8, z: 8, core: 2. Of those that a mesh axis runs over, the one named last changes fastest.
Arguments:
- hidden_slab: bfloat16 [8, 4096, 5120], P('sess', 'ctx'), may hold values from -6 to 6
- projection: bfloat16 [5120, 1024], P(('ctx', 'sess')), may hold values from -0.078125 to 0.078125
- adapter_down: bfloat16 [8, 5120, 64], P('sess'), may hold values from -0.078125 to 0.078125
- adapter_up: bfloat16 [8, 2, 32, 512], P('sess'), may hold values from -1 to 1
- key_gain: float32 [128], replicated, may hold values from 0.5 to 2
- cache_keys: bfloat16 [8, 8192, 512], P('sess', 'ctx'), may hold values from -4 to 4
- cache_values: bfloat16 [8, 8192, 512], P('sess', 'ctx'), may hold values from -6 to 6
- fresh_keys: bfloat16 [8, 64, 512], P('sess', 'ctx'), may hold values from -4 to 4
- fresh_values: bfloat16 [8, 64, 512], P('sess', 'ctx'), may hold values from -6 to 6
- queries: bfloat16 [8, 64, 4096], P('sess', 'ctx'), may hold values from -24 to 24
- slab_length: int32 [8], P('sess'), may hold values from 512 to 4096, as said below
- cache_length: int32 [8, 64], P('sess', 'ctx'), may hold values from 1 to 128, as said below
Outputs:
- slab_cache: bfloat16 [8, 4096, 1024], P('sess', 'ctx')
- attended: bfloat16 [8, 64, 4096], P('sess', 'ctx')
Inputs may be any that keep to these rules, and one draw needn't show every extreme that they name: `slab_length`: some session has exactly 4096 live prefix rows. `cache_length`: in every session some context shard has all 128 slots filled.
All inputs are finite; a program needn't handle non-finite values.
Results may differ from a plain program's by a relative error of at most 0.012.
Values may be sent and summed in bfloat16 or wider, within the bound.
No kernel may reach another device: no remote copies, remote signals or barrier semaphores. Data moves between devices by JAX's collectives and lax.ppermute only.
A program may use at most 128 MiB of HBM per device.

v0:
```python
import math

import jax
import jax.numpy as jnp
from jax import lax
from jax.sharding import PartitionSpec as P

adapter_scale = 0.5
norm_epsilon = 1e-06


def finish_rows(base_part, slab_rows, down_part, up_part, key_gain):
    row_count = slab_rows.shape[0]
    low_rank = up_part.shape[1]
    half_width = base_part.shape[1] // 2
    head_size = key_gain.shape[0]
    low_part = jnp.dot(slab_rows, down_part, preferred_element_type=jnp.float32).astype(
        jnp.bfloat16
    )
    delta_keys = jnp.dot(low_part[:, :low_rank], up_part[0], preferred_element_type=jnp.float32)
    delta_values = jnp.dot(low_part[:, low_rank:], up_part[1], preferred_element_type=jnp.float32)
    projected = base_part + adapter_scale * jnp.concatenate([delta_keys, delta_values], axis=1)
    raw_keys = projected[:, :half_width].reshape(row_count, half_width // head_size, head_size)
    normed = (
        raw_keys
        * lax.rsqrt(jnp.mean(raw_keys * raw_keys, axis=-1, keepdims=True) + norm_epsilon)
        * key_gain
    )
    new_keys = normed.reshape(row_count, half_width).astype(jnp.bfloat16)
    new_values = projected[:, half_width:].astype(jnp.bfloat16)
    return jnp.concatenate([new_keys, new_values], axis=1)


def body(
    hidden_slab,
    projection,
    adapter_down,
    adapter_up,
    key_gain,
    cache_keys,
    cache_values,
    fresh_keys,
    fresh_values,
    queries,
    slab_length,
    cache_length,
):
    shards = lax.axis_size("ctx")
    shard_id = lax.axis_index("ctx")
    head_size = key_gain.shape[0]
    half_width = cache_keys.shape[2]
    key_heads = half_width // head_size
    query_heads = queries.shape[2] // head_size
    group_size = query_heads // key_heads
    slab_dev = hidden_slab.shape[1]
    model_width = hidden_slab.shape[2]
    block_rows = slab_dev // shards
    new_dev = queries.shape[1]
    cache_dev = cache_keys.shape[1]
    arrived = lax.all_to_all(
        hidden_slab.reshape(1, shards, block_rows, model_width),
        "ctx",
        split_axis=1,
        concat_axis=1,
        tiled=True,
    )
    slab_rows = arrived.reshape(slab_dev, model_width)
    whole_weight = lax.all_gather(projection, ("ctx", "sess"), axis=0, tiled=True)
    base_part = jnp.dot(slab_rows, whole_weight, preferred_element_type=jnp.float32)
    local_cache = finish_rows(base_part, slab_rows, adapter_down[0], adapter_up[0], key_gain)
    position = jnp.arange(slab_dev)
    initial = position // block_rows * slab_dev + shard_id * block_rows + position % block_rows
    slab_usable = initial < slab_length[0]
    all_queries = lax.all_gather(queries[0], "ctx", axis=0, tiled=True)
    new_tok = all_queries.shape[0]
    query_grid = all_queries.reshape(new_tok, key_heads, group_size, head_size)
    all_keys = jnp.concatenate([cache_keys[0], local_cache[:, :half_width], fresh_keys[0]], axis=0)
    all_values = jnp.concatenate(
        [cache_values[0], local_cache[:, half_width:], fresh_values[0]], axis=0
    )
    all_keys = all_keys.reshape(-1, key_heads, head_size)
    all_values = all_values.reshape(-1, key_heads, head_size)
    scores = jnp.einsum(
        "qkgd,nkd->kgqn", query_grid, all_keys, preferred_element_type=jnp.float32
    ) * (1.0 / math.sqrt(head_size))
    cache_ok = jnp.arange(cache_dev) < cache_length[0, 0]
    fresh_pos = shard_id * new_dev + jnp.arange(new_dev)
    query_pos = jnp.arange(new_tok)
    usable = jnp.concatenate(
        [
            jnp.broadcast_to(cache_ok[None, :], (new_tok, cache_dev)),
            jnp.broadcast_to(slab_usable[None, :], (new_tok, slab_dev)),
            fresh_pos[None, :] <= query_pos[:, None],
        ],
        axis=1,
    )
    masked = jnp.where(usable[None, None], scores, -jnp.inf)
    row_max = jnp.max(masked, axis=-1)
    weights = jnp.exp(masked - row_max[..., None]).astype(jnp.bfloat16)
    row_total = jnp.sum(weights, axis=-1, dtype=jnp.float32)
    row_output = jnp.einsum(
        "kgqn,nkd->kgqd", weights, all_values, preferred_element_type=jnp.float32
    )
    largest = lax.pmax(row_max, "ctx")
    factor = jnp.exp(row_max - largest)
    merged_total, merged_output = (
        lax.psum_scatter(row_total * factor, "ctx", scatter_dimension=2, tiled=True),
        lax.psum_scatter(row_output * factor[..., None], "ctx", scatter_dimension=2, tiled=True),
    )
    result = merged_output / merged_total[..., None]
    result = (
        result.transpose(2, 0, 1, 3)
        .reshape(1, new_dev, query_heads * head_size)
        .astype(jnp.bfloat16)
    )
    return (local_cache[None], result)


def solution(mesh):
    return jax.shard_map(
        body,
        mesh=mesh,
        in_specs=(
            P("sess", "ctx", None),
            P(("ctx", "sess"), None),
            P("sess", None, None),
            P("sess", None, None, None),
            P(),
            P("sess", "ctx", None),
            P("sess", "ctx", None),
            P("sess", "ctx", None),
            P("sess", "ctx", None),
            P("sess", "ctx", None),
            P("sess"),
            P("sess", "ctx"),
        ),
        out_specs=(P("sess", "ctx", None), P("sess", "ctx", None)),
        check_vma=False,
    )
```

profile of v0, /device:TPU:1, one launch (start us, length us, event | category | flops | bytes accessed | tf_op | source)
XLA Modules:
  0.0 685.8 jit_solution(1746942993819960809)
XLA Ops:
  7.2 0.0 copy-start
  7.2 0.0 all-gather.4.cloned.1.call-start
  7.2 0.7 all-gather.4.cloned.1.call-update
  7.9 2.1 copy.93
  10.0 0.5 broadcast.93
  10.5 4.6 reduce.1
  15.1 1.3 reshape.96
  16.4 11.6 %all-to-all-start = ((bf16[64,2,2560]{2,1,0:T(2,128)(2,1)}), bf16[64,2,2560]{2,1,0:T(2,128)(2,1)S(1)}, u32[]{:S(2)}, u32[]{:S(2)}) async-start(bf16[64,2,2560]{2,1,0:T(2,128)(2,1)} %reshape.96), calls=%async_computation | async-start | bytes 1310720 | tf_op jit(solution)/shard_map/all_to_all | solution.py:60
  28.1 0.0 copy-start.1
  28.1 0.0 reduce-scatter.2.cloned.1.call-start
  29.5 0.0 copy-done.4
  29.5 0.0 copy-start.2
  29.5 59.9 %all-gather = bf16[64,1,4096]{2,1,0:T(2,128)(2,1)S(1)} all-gather(bf16[1,1,4096]{2,1,0:T(2,128)(2,1)S(1)} %copy-done.4), channel_id=2, replica_groups=mesh['ctx'=64,'sess'=8] {'ctx'}, dimensions={0}, use_global_device_ids=true | all-gather | bytes 532480 | tf_op jit(solution)/shard_map/all_gather | solution.py:74
  89.4 3.2 reduce
  92.6 0.9 copy.75
  93.5 0.0 copy-done.1
  93.5 0.1 copy.60
  93.6 0.0 copy-start.3
  93.6 0.1 copy.61
  93.8 0.0 copy-done.2
  93.8 0.1 copy.64
  93.9 0.1 copy.65
  94.1 0.0 copy-done.5
  94.1 0.1 pad_add_fusion
  94.2 0.0 all-to-all-done
  94.2 0.6 reshape.97
  94.8 0.4 convolution_convert_fusion
  95.2 0.2 fusion.18
  95.4 0.2 fusion.20
  95.6 59.3 %all-gather.4.cloned.1.call-done = bf16[512,10,1024]{2,1,0:T(8,128)(2,1)} async-done(((bf16[1,10,1024]{2,1,0:T(8,128)(2,1)}), bf16[512,10,1024]{2,1,0:T(8,128)(2,1)}) %all-gather.4.cloned.1.call-update) | async-done | bytes 10485776 | tf_op jit(solution)/shard_map/all_gather | solution.py:68
  154.9 20.0 %reshape.89 = bf16[5120,1024]{1,0:T(8,128)(2,1)} reshape(bf16[512,10,1024]{2,1,0:T(8,128)(2,1)} %all-gather.4.cloned.1.call-done) | data formatting | bytes 20971520
  174.8 5.9 convolution_add_fusion
  180.8 0.1 reduce_sum.18
  181.0 0.1 mul.70
  181.2 0.0 copy-start.7
  181.2 1.7 fusion
  182.9 242.6 %pmax.7 = f32[4,8,64]{2,1,0:T(8,128)S(1)} all-reduce(f32[4,8,64]{2,1,0:T(8,128)S(1)} %get-tuple-element.4), channel_id=1, replica_groups=mesh['ctx'=64,'sess'=8] {'ctx'}, use_global_device_ids=true, to_apply=%region_2.3 | all-reduce | flops 2048 | bytes 16384 | tf_op jit(solution)/shard_map/pmax | solution.py:104
  425.5 0.8 convert_reduce_fusion
  426.3 0.7 convolution_multiply_fusion
  427.0 1.6 copy.67
  428.6 0.0 reduce-scatter.2.cloned.1.call-update
  428.7 1.3 dynamic-slice
  429.9 0.1 copy.68
  430.1 246.2 %all-reduce = f32[4,8,64]{1,0,2:T(4,128)S(1)} all-reduce(f32[4,8,64]{1,0,2:T(4,128)S(1)} %copy.68), channel_id=4, replica_groups=mesh['ctx'=64,'sess'=8] {'ctx'}, use_global_device_ids=true, to_apply=%region_5.6.clone | all-reduce | flops 2048 | bytes 16384
  676.2 0.6 dynamic-slice_bitcast_fusion
  676.9 0.7 maximum_bitcast_fusion.4
  677.6 0.8 divide_convert_fusion
  678.4 0.6 convert_element_type.32
  (21 shorter events, 0.2 us)
Async XLA Ops:
  7.2 87.6 %copy-start = (bf16[1,5120,64]{1,2,0:T(8,128)(2,1)S(1)}, bf16[1,5120,64]{1,2,0:T(8,128)(2,1)}, u32[]{:S(2)}) copy-start(bf16[1,5120,64]{1,2,0:T(8,128)(2,1)} %param.14) | copy-start | bytes 1966084
  7.2 147.7 %all-gather.4.cloned.1.call-start = ((), (), s32[]{:S(2)}) async-start(), calls=%async_computation.3 | async-start | bytes 16809984 | tf_op jit(solution)/shard_map/all_gather | solution.py:68
  10.5 18.9 %copy-start.4 = (bf16[1,1,4096]{2,1,0:T(2,128)(2,1)S(1)}, bf16[1,1,4096]{2,1,0:T(2,128)(2,1)}, u32[]{:S(2)}) copy-start(bf16[1,1,4096]{2,1,0:T(2,128)(2,1)} %param.21) | copy-start | bytes 24580
  16.4 77.8 %all-to-all-start = ((bf16[64,2,2560]{2,1,0:T(2,128)(2,1)}), bf16[64,2,2560]{2,1,0:T(2,128)(2,1)S(1)}, u32[]{:S(2)}, u32[]{:S(2)}) async-start(bf16[64,2,2560]{2,1,0:T(2,128)(2,1)} %reshape.96), calls=%async_computation | async-start | bytes 1310720 | tf_op jit(solution)/shard_map/all_to_all | solution.py:60
  28.1 65.4 %copy-start.1 = (bf16[1,128,512]{2,1,0:T(8,128)(2,1)S(1)}, bf16[1,128,512]{2,1,0:T(8,128)(2,1)}, u32[]{:S(2)}) copy-start(bf16[1,128,512]{2,1,0:T(8,128)(2,1)} %param.17) | copy-start | bytes 393220
  28.1 649.5 %reduce-scatter.2.cloned.1.call-start = ((), (), s32[]{:S(2)}) async-start(), calls=%async_computation.2 | async-start | bytes 1064960 | tf_op jit(solution)/shard_map/reduce_scatter | solution.py:108
  29.5 64.3 %copy-start.2 = (bf16[1,128,512]{2,1,0:T(8,128)(2,1)S(1)}, bf16[1,128,512]{2,1,0:T(8,128)(2,1)}, u32[]{:S(2)}) copy-start(bf16[1,128,512]{2,1,0:T(8,128)(2,1)} %param.18) | copy-start | bytes 393220
  89.4 4.7 copy-start.5
  93.6 1.6 copy-start.3
  174.8 6.4 copy-start.6
  181.2 245.1 %copy-start.7 = (bf16[1,1,512]{2,1,0:T(2,128)(2,1)S(1)}, bf16[1,1,512]{2,1,0:T(2,128)(2,1)}, u32[]{:S(2)}) copy-start(bf16[1,1,512]{2,1,0:T(2,128)(2,1)} %param.20) | copy-start | bytes 3076
Sparse Core Ops, SparseCore 0:
  12.5 142.3 all-gather.3
  428.8 138.7 reduce-scatter.1
where the time goes:
time: 690 us; the launch traced here: 686 us
  blocking collectives  549 us (80%)
  waiting for transfers between devices  60 us (9%)
  local copies, waits for them, and re-layouts  30.4 us (4%)
  between operations  15.7 us (2%)
  starting transfers between devices  11.7 us (2%)
  other arithmetic  10.4 us (2%)
  matrix products  9.05 us (1%)
    unnamed x1, blocking collectives  246 us
    pmax x1, blocking collectives, body(): largest = lax.pmax(row_max, 'ctx')  243 us
    all_gather x1, blocking collectives, body(): all_queries = lax.all_gather(queries[0], 'ctx', axis=0, tiled=True)  59.9 us
    all_gather x1, waiting for transfers between devices, body(): lax.all_gather(projection, ('ctx', 'sess'), axis=0, tiled=True)  59.3 us
    unnamed x24, local copies, waits for them, and re-layouts  24.8 us
  transfers between devices with their start and end apart: 3, of which 1 were waited for; matrix products, arithmetic and copies ran while one was open for 3% of the time, Pallas kernels for 0%

commit v1 on v0

v1 whole, which is shorter than its diff:
```python
import functools
import math

import jax
import jax.numpy as jnp
from jax import lax
from jax.experimental import pallas as pl
from jax.experimental.pallas import tpu as pltpu
from jax.sharding import Mesh, PartitionSpec as P

adapter_scale = 0.5
norm_epsilon = 1e-06
masked_score = -1e30
HD = 128
NX, NY, NC, NZ = 4, 8, 2, 8
CTX = ("x", "y", "c")
bf16 = jnp.bfloat16
f32 = jnp.float32


def dot_nt(a, b):
    return lax.dot_general(a, b, (((1,), (1,)), ((), ())), preferred_element_type=f32)


def dot_nn(a, b):
    return lax.dot_general(a, b, (((1,), (0,)), ((), ())), preferred_element_type=f32)


def rebuild_attend(
    place, weight, hidden, down, up, gain, context, out, base, low, asked
):
    step = pl.program_id(0)

    @pl.when(step == 0)
    def _():
        base[...] = jnp.zeros_like(base)
        low[...] = jnp.zeros_like(low)

    rows = hidden[...].reshape(NX * 64, 1280)
    key_weight = weight[:, :, 0:80, :].reshape(1280, HD)
    value_weight = weight[:, :, 80:160, :].reshape(1280, HD)
    base[:, 0:HD] += dot_nn(rows, key_weight)
    base[:, HD:] += dot_nn(rows, value_weight)
    low[...] += dot_nt(rows, down[...])
    tail = weight[:, :, 160:176, :].astype(f32)
    asked[step] = tail[:, :, 0:8, :].reshape(NY * NC * 8, HD)

    @pl.when(step == NX - 1)
    def _():
        slab_length = place[0]
        y = place[1]
        c = place[2]
        projected = base[...] + adapter_scale * dot_nn(low[...].astype(bf16), up[...])
        raw_keys = projected[:, 0:HD]
        mean = jnp.mean(raw_keys * raw_keys, axis=-1, keepdims=True)
        new_keys = (raw_keys * lax.rsqrt(mean + norm_epsilon) * gain[...]).astype(bf16)
        new_values = projected[:, HD:].astype(bf16)
        queries = asked[...].reshape(512, HD).astype(bf16)

        column = lax.broadcasted_iota(jnp.int32, (1, 256), 1)
        initial = (column >> 6) * 1024 + (y * 2 + c) * 64 + (column & 63)
        slab_scores = jnp.where(
            initial < slab_length, dot_nt(queries, new_keys), masked_score
        )
        cache_keys = context[:, 0:128, :].reshape(512, HD)
        cache_values = context[:, 128:256, :].reshape(512, HD)
        lane = lax.broadcasted_iota(jnp.int32, (1, HD), 1).astype(f32)
        filled = jnp.concatenate(
            [
                jnp.where(lane < context[i, 256:272, :].astype(f32)[1:2, :], 1.0, 0.0)
                for i in range(NX)
            ],
            axis=1,
        )
        cache_scores = jnp.where(
            filled > 0.5, dot_nt(queries, cache_keys), masked_score
        )
        fresh_keys = context[:, 256:272, :].reshape(64, HD)
        fresh_values = context[:, 272:288, :].reshape(64, HD)
        token = lax.broadcasted_iota(jnp.int32, (512, 64), 0) >> 3
        fresh = lax.broadcasted_iota(jnp.int32, (512, 64), 1)
        fresh_pos = (fresh >> 4) * 16 + y * 2 + c
        fresh_ok = ((fresh & 15) == 0) & (fresh_pos <= token)
        fresh_scores = jnp.where(fresh_ok, dot_nt(queries, fresh_keys), masked_score)

        scale = 1.0 / math.sqrt(HD)
        row_max = jnp.maximum(
            jnp.maximum(
                jnp.max(slab_scores, axis=-1, keepdims=True),
                jnp.max(cache_scores, axis=-1, keepdims=True),
            ),
            jnp.max(fresh_scores, axis=-1, keepdims=True),
        )
        shift = (row_max * scale).astype(bf16).astype(f32)

        def weigh(scores, values):
            weights = jnp.exp(scores * scale - shift).astype(bf16)
            wide = jnp.concatenate([values, jnp.ones_like(values)], axis=1)
            return dot_nn(weights, wide)

        merged = (
            weigh(slab_scores, new_values)
            + weigh(cache_scores, cache_values)
            + weigh(fresh_scores, fresh_values)
        )
        total = merged[:, HD:]
        high = total.astype(bf16).astype(f32)
        lanes = lax.broadcasted_iota(jnp.int32, (512, HD), 1)
        stats = jnp.where(
            lanes == 0, shift, jnp.where(lanes == 1, high, total - high)
        )
        target = lax.broadcasted_iota(jnp.int32, (512, 1), 0)
        origin = (target & 1) * 256 + ((target >> 1) & 3) * 64 + (target >> 3)
        pick = jnp.where(
            lax.broadcasted_iota(jnp.int32, (512, 512), 1) == origin, 1.0, 0.0
        ).astype(bf16)
        spread = dot_nn(pick, jnp.concatenate([new_keys, new_values], axis=0))
        out[:, 0:HD] = merged[:, 0:HD].astype(bf16)
        out[:, HD : 2 * HD] = stats.astype(bf16)
        out[:, 2 * HD :] = spread.astype(bf16)


def merge(parts, slab, attended):
    heads = []
    rebuilt = []
    for h in range(NX):
        block = parts[h * 128 : (h + 1) * 128, :]
        output = block[:, 0:HD].astype(f32).reshape(16, 8, HD)
        stats = block[:, HD : 2 * HD].astype(f32).reshape(16, 8, HD)
        rebuilt.append(block[:, 2 * HD :])
        shift = stats[:, :, 0:1]
        total = stats[:, :, 1:2] + stats[:, :, 2:3]
        largest = jnp.max(shift, axis=0, keepdims=True)
        factor = jnp.exp(shift - largest)
        merged_total = jnp.sum(factor * total, axis=0)
        merged_output = jnp.sum(factor * output, axis=0)
        heads.append(merged_output / merged_total)
    attended[...] = jnp.concatenate(heads, axis=0).astype(bf16)
    target = lax.broadcasted_iota(jnp.int32, (128, 1), 0)
    origin = (target & 15) * 8 + ((target >> 4) & 3) * 2 + (target >> 6)
    pick = jnp.where(
        lax.broadcasted_iota(jnp.int32, (128, 128), 1) == origin, 1.0, 0.0
    ).astype(bf16)
    placed = dot_nn(pick, jnp.concatenate(rebuilt, axis=1)).astype(bf16)
    slab[:, 0:512] = placed[0:64, :]
    slab[:, 512:1024] = placed[64:128, :]


def broadcast_over(value, axis):
    size = lax.axis_size(axis)
    return lax.all_to_all(
        jnp.broadcast_to(value[None], (size,) + value.shape), axis, 0, 0, tiled=True
    )


def body(
    hidden_slab,
    projection,
    adapter_down,
    adapter_up,
    key_gain,
    cache_keys,
    cache_values,
    fresh_keys,
    fresh_values,
    queries,
    slab_length,
    cache_length,
):
    head = lax.axis_index("x")
    y = lax.axis_index("y")
    c = lax.axis_index("c")

    weight_rows = broadcast_over(projection, "z").reshape(80, 2, NX, HD)
    weight_rows = weight_rows.transpose(2, 1, 0, 3).reshape(NX, 160, HD)
    asked = queries.reshape(NX, 8, HD)
    bundle = jnp.concatenate(
        [weight_rows, asked, jnp.zeros((NX, 8, HD), bf16)], axis=1
    )
    bundle = jnp.broadcast_to(bundle[:, None], (NX, NC, 176, HD)).reshape(
        NX * NC, 176, HD
    )
    bundle = lax.all_to_all(bundle, ("x", "c"), 0, 0, tiled=True)
    weight = lax.all_gather(bundle, "y", axis=0, tiled=False)

    def by_head(value):
        return value.reshape(-1, NX, HD).transpose(1, 0, 2)

    count = jnp.broadcast_to(
        cache_length.astype(f32).astype(bf16).reshape(1, 1, 1), (NX, 1, HD)
    )
    context = jnp.concatenate(
        [
            by_head(cache_keys[0]),
            by_head(cache_values[0]),
            by_head(fresh_keys[0]),
            count,
            jnp.zeros((NX, 14, HD), bf16),
            by_head(fresh_values[0]),
            jnp.zeros((NX, 15, HD), bf16),
        ],
        axis=1,
    )
    context = lax.all_to_all(context, "x", 0, 0, tiled=True)
    hidden = broadcast_over(hidden_slab[0], "x")

    up = lax.dynamic_slice(adapter_up[0], (0, 0, head * HD), (2, 32, HD))
    empty = jnp.zeros((32, HD), bf16)
    up = jnp.concatenate(
        [
            jnp.concatenate([up[0], empty], axis=1),
            jnp.concatenate([empty, up[1]], axis=1),
        ],
        axis=0,
    )
    place = jnp.stack([slab_length[0], y, c]).astype(jnp.int32)
    parts = pl.pallas_call(
        rebuild_attend,
        grid=(NX,),
        in_specs=[
            pl.BlockSpec(memory_space=pltpu.SMEM),
            pl.BlockSpec((NY, NC, 176, HD), lambda k: (0, k, 0, 0)),
            pl.BlockSpec((NX, 64, 1280), lambda k: (0, 0, k)),
            pl.BlockSpec((64, 1280), lambda k: (0, k)),
            pl.BlockSpec((64, 256), lambda k: (0, 0)),
            pl.BlockSpec((1, HD), lambda k: (0, 0)),
            pl.BlockSpec((NX, 288, HD), lambda k: (0, 0, 0)),
        ],
        out_specs=pl.BlockSpec((512, 384), lambda k: (0, 0)),
        out_shape=jax.ShapeDtypeStruct((512, 384), bf16),
        scratch_shapes=[
            pltpu.VMEM((256, 256), f32),
            pltpu.VMEM((256, 64), f32),
            pltpu.VMEM((NX, 128, HD), f32),
        ],
        compiler_params=pltpu.CompilerParams(vmem_limit_bytes=48 * 1024 * 1024),
    )(
        place,
        weight,
        hidden,
        adapter_down[0].T,
        up,
        key_gain.reshape(1, HD),
        context,
    )
    parts = lax.all_to_all(parts.reshape(64, 8, 384), CTX, 0, 0, tiled=True)
    slab, attended = pl.pallas_call(
        merge,
        out_shape=[
            jax.ShapeDtypeStruct((64, 1024), bf16),
            jax.ShapeDtypeStruct((32, HD), bf16),
        ],
        compiler_params=pltpu.CompilerParams(vmem_limit_bytes=32 * 1024 * 1024),
    )(parts.reshape(512, 384))
    return slab[None], attended.reshape(1, 1, 32 * HD)


def solution(mesh):
    fine = Mesh(mesh.devices.reshape(NX, NY, NC, NZ), ("x", "y", "c", "z"))
    return jax.shard_map(
        body,
        mesh=fine,
        in_specs=(
            P("z", CTX, None),
            P(CTX + ("z",), None),
            P("z", None, None),
            P("z", None, None, None),
            P(),
            P("z", CTX, None),
            P("z", CTX, None),
            P("z", CTX, None),
            P("z", CTX, None),
            P("z", CTX, None),
            P("z"),
            P("z", CTX),
        ),
        out_specs=(P("z", CTX, None), P("z", CTX, None)),
        check_vma=False,
    )
```

time: 690 us -> 132 us (0.19)
  blocking collectives: 549 us -> 48.4 us
  local copies, waits for them, and re-layouts: 30.4 us -> 6.95 us
  waiting for transfers between devices: 60 us -> 37.9 us
  other arithmetic: 10.4 us -> 1.01 us
  matrix products: 9.05 us -> 0 us
    unnamed x1 -> x0, blocking collectives: 246 us -> none
    pmax x1 -> x0, blocking collectives: 243 us -> none  [body(): largest = lax.pmax(row_max, 'ctx')]
    all_gather x1 -> x0, blocking collectives: 59.9 us -> none  [body(): all_queries = lax.all_gather(queries[0], 'ctx', axis=0, tiled=True)]
    all_gather x1, waiting for transfers between devices: 59.3 us -> 0.01 us  [body(): weight = lax.all_gather(bundle, 'y', axis=0, tiled=False)]
    all_to_all x0 -> x3, blocking collectives: none -> 48.4 us  [the longest x1 25.6 us: body(): parts = lax.all_to_all(parts.reshape(64, 8, 384), CTX, 0, 0, tiled=True)]
    all_to_all x1 -> x2, waiting for transfers between devices: 0.01 us -> 37.9 us  [broadcast_over(): lax.all_to_all(jnp.broadcast_to(value[None], (size,) + value.shape), axis...]
    unnamed x24 -> x16, local copies, waits for them, and re-layouts: 24.8 us -> 1.35 us
    dot_general x6 -> x0, matrix products: 9.05 us -> none  [the longest x1 5.92 us: body(): jnp.dot(slab_rows, whole_weight, preferred_element_type=jnp.float32)]
  transfers between devices with their start and end apart: 3 -> 3, of which waited for: 1 -> 2; matrix products, arithmetic and copies ran while one was open for 3% -> 3% of each run, Pallas kernels for 0% -> 0%
where the time goes in v1:
time: 132 us; the launch traced here: 131 us
  blocking collectives  48.4 us (37%)
  waiting for transfers between devices  37.9 us (29%)
  between operations  15.5 us (12%)
  starting transfers between devices  14.7 us (11%)
  local copies, waits for them, and re-layouts  6.95 us (5%)
  Pallas kernels  6.72 us (5%)
    all_to_all x2, waiting for transfers between devices, broadcast_over(): lax.all_to_all(jnp.broadcast_to(value[None], (size,) + value.shape), axis...  37.9 us
    all_to_all x1, blocking collectives, body(): parts = lax.all_to_all(parts.reshape(64, 8, 384), CTX, 0, 0, tiled=True)  25.6 us
    all_to_all x2, starting transfers between devices, broadcast_over(): lax.all_to_all(jnp.broadcast_to(value[None], (size,) + value.shape), axis...  14.7 us
    all_to_all x1, blocking collectives, body(): bundle = lax.all_to_all(bundle, ('x', 'c'), 0, 0, tiled=True)  14.4 us
    all_to_all x1, blocking collectives, body(): context = lax.all_to_all(context, 'x', 0, 0, tiled=True)  8.33 us
    pallas_call x1, Pallas kernels, body(): pl.pallas_call(rebuild_attend, grid=(NX,), in_specs=[pl.BlockSpec(memory_...  5.72 us
    broadcast_in_dim x2, local copies, waits for them, and re-layouts, broadcast_over(): jnp.broadcast_to(value[None], (size,) + value.shape)  3.38 us
  transfers between devices with their start and end apart: 3, of which 2 were waited for; matrix products, arithmetic and copies ran while one was open for 3% of the time, Pallas kernels for 0%

profile of v1, /device:TPU:1, one launch (start us, length us, event | category | flops | bytes accessed | tf_op | source)
XLA Modules:
  0.0 131.2 jit_solution(13559141930746666114)
XLA Ops:
  7.2 0.0 copy-start.3
  7.2 0.0 copy-start.4
  7.2 0.0 copy-start.5
  7.2 0.0 copy-start.6
  7.2 1.5 %broadcast_in_dim.39 = bf16[8,10,1024]{2,1,0:T(8,128)(2,1)} broadcast(bf16[10,1024]{1,0:T(8,128)(2,1)} %param.13), dimensions={1,2} | broadcast | bytes 184320 | tf_op jit(solution)/shard_map/broadcast_in_dim | solution.py:152
  8.7 10.9 %all-to-all-start = ((bf16[8,10,1024]{2,1,0:T(8,128)(2,1)}), bf16[8,10,1024]{2,1,0:T(8,128)(2,1)S(1)}, u32[]{:S(2)}, u32[]{:S(2)}) async-start(bf16[8,10,1024]{2,1,0:T(8,128)(2,1)} %broadcast_in_dim.39), calls=%async_computation | async-start | bytes 524288 | tf_op jit(solution)/shard_map/all_to_all | solution.py:151
  19.6 0.0 copy-start.2
  19.6 0.0 all-gather.3.cloned.1.call-start
  19.7 0.8 reduce
  20.5 0.1 pad.6.clone
  20.6 9.4 %all-to-all-done = bf16[8,10,1024]{2,1,0:T(8,128)(2,1)S(1)} async-done(((bf16[8,10,1024]{2,1,0:T(8,128)(2,1)}), bf16[8,10,1024]{2,1,0:T(8,128)(2,1)S(1)}, u32[]{:S(2)}, u32[]{:S(2)}) %all-to-all-start) | async-done | bytes 163872 | tf_op jit(solution)/shard_map/all_to_all | solution.py:151
  30.0 0.1 reshape.39
  30.1 0.1 maximum_maximum_fusion
  30.3 14.4 %all_to_all.25 = bf16[8,176,128]{2,1,0:T(8,128)(2,1)} all-to-all(bf16[8,176,128]{2,1,0:T(8,128)(2,1)S(1)} %bitcast.31), channel_id=1, replica_groups=mesh['x'=4,'y'=8,'c'=2,'z'=8] {'x','c'}, dimensions={0} | all-to-all | bytes 720896 | tf_op jit(solution)/shard_map/all_to_all | solution.py:183
  44.7 0.0 all-gather.3.cloned.1.call-update
  44.7 0.0 copy-done.3
  44.7 0.1 copy.24
  44.9 0.1 copy.25
  45.0 0.0 copy-done.4
  45.0 0.1 copy.26
  45.1 0.1 copy.27
  46.0 0.0 copy-done.5
  46.0 0.0 copy-done.6
  46.0 0.4 concatenate.19
  46.4 8.3 %all_to_all.26.context = bf16[4,288,128]{2,1,0:T(8,128)(2,1)S(1)} all-to-all(bf16[4,288,128]{2,1,0:T(8,128)(2,1)S(1)} %concatenate.19), channel_id=1, replica_groups=mesh['x'=4,'y'=8,'c'=2,'z'=8] {'x'}, dimensions={0} | all-to-all | bytes 589824 | tf_op jit(solution)/shard_map/all_to_all | solution.py:204
  54.7 0.0 copy-done.2
  54.7 1.8 %broadcast_in_dim.43 = bf16[4,64,5120]{2,1,0:T(8,128)(2,1)} broadcast(bf16[64,5120]{1,0:T(8,128)(2,1)S(1)} %bitcast.34), dimensions={1,2} | broadcast | bytes 3276800 | tf_op jit(solution)/shard_map/broadcast_in_dim | solution.py:152
  56.5 0.0 copy-start.1
  56.5 3.8 %all-to-all-start.2 = ((bf16[4,64,5120]{2,1,0:T(8,128)(2,1)}), bf16[4,64,5120]{2,1,0:T(8,128)(2,1)S(1)}, u32[]{:S(2)}, u32[]{:S(2)}) async-start(bf16[4,64,5120]{2,1,0:T(8,128)(2,1)} %broadcast_in_dim.43), calls=%async_computation.2 | async-start | bytes 5242880 | tf_op jit(solution)/shard_map/all_to_all | solution.py:151
  61.0 0.1 pad_add_fusion.place
  61.1 0.7 dynamic-slice_bitcast_fusion.1
  61.8 28.5 %all-to-all-done.2.hidden = bf16[4,64,5120]{2,1,0:T(8,128)(2,1)S(1)} async-done(((bf16[4,64,5120]{2,1,0:T(8,128)(2,1)}), bf16[4,64,5120]{2,1,0:T(8,128)(2,1)S(1)}, u32[]{:S(2)}, u32[]{:S(2)}) %all-to-all-start.2) | async-done | bytes 2621472 | tf_op jit(solution)/shard_map/all_to_all | solution.py:151
  90.3 0.0 all-gather.3.cloned.1.call-done
  90.3 0.0 copy-done.1
  90.3 0.0 copy-start
  90.3 1.1 copy-done
  91.4 5.7 %shard_map.131 = bf16[512,384]{1,0:T(8,128)(2,1)S(1)} custom-call(s32[3]{0:T(128)S(1)} %pad_add_fusion.place, bf16[8,8,176,128]{3,2,1,0:T(8,128)(2,1)} %bitcast.30, bf16[4,64,5120]{2,1,0:T(8,128)(2,1)S(1)} %all-to-all-done.2.hidden, bf16[64,5120]{1,0:T(8,128)(2,1)S(1)} %bitcast.28, bf16[64,256]{1,0:T(8,128)(2,1)S(1)} %fusion.2.up, f32[1,128]{1,0:T(1,128)S(1)} %bitcast.29, ...), custom_call_target="tpu_custom_call" | custom-call | tf_op jit(solution)/shard_map/pallas_call | solution.py:217
  97.1 25.6 %all_to_all.27 = bf16[64,8,384]{2,1,0:T(8,128)(2,1)S(1)} all-to-all(bf16[64,8,384]{2,1,0:T(8,128)(2,1)S(1)} %bitcast.26), channel_id=1, replica_groups=mesh['x'=4,'y'=8,'c'=2,'z'=8] {'x','y','c'}, dimensions={0} | all-to-all | bytes 786432 | tf_op jit(solution)/shard_map/all_to_all | solution.py:246
  122.7 1.0 shard_map.132
  123.7 0.6 reshape.46
  (7 shorter events, 0.1 us)
Async XLA Ops:
  7.2 37.6 %copy-start.3 = (bf16[1,128,512]{2,1,0:T(8,128)(2,1)S(1)}, bf16[1,128,512]{2,1,0:T(8,128)(2,1)}, u32[]{:S(2)}) copy-start(bf16[1,128,512]{2,1,0:T(8,128)(2,1)} %param.17) | copy-start | bytes 393220
  7.2 37.8 %copy-start.4 = (bf16[1,128,512]{2,1,0:T(8,128)(2,1)S(1)}, bf16[1,128,512]{2,1,0:T(8,128)(2,1)}, u32[]{:S(2)}) copy-start(bf16[1,128,512]{2,1,0:T(8,128)(2,1)} %param.18) | copy-start | bytes 393220
  7.2 38.8 %copy-start.5 = (bf16[1,1,512]{2,1,0:T(2,128)(2,1)S(1)}, bf16[1,1,512]{2,1,0:T(2,128)(2,1)}, u32[]{:S(2)}) copy-start(bf16[1,1,512]{2,1,0:T(2,128)(2,1)} %param.19) | copy-start | bytes 3076
  7.2 38.8 %copy-start.6 = (bf16[1,1,512]{2,1,0:T(2,128)(2,1)S(1)}, bf16[1,1,512]{2,1,0:T(2,128)(2,1)}, u32[]{:S(2)}) copy-start(bf16[1,1,512]{2,1,0:T(2,128)(2,1)} %param.20) | copy-start | bytes 3076
  8.7 21.2 %all-to-all-start = ((bf16[8,10,1024]{2,1,0:T(8,128)(2,1)}), bf16[8,10,1024]{2,1,0:T(8,128)(2,1)S(1)}, u32[]{:S(2)}, u32[]{:S(2)}) async-start(bf16[8,10,1024]{2,1,0:T(8,128)(2,1)} %broadcast_in_dim.39), calls=%async_computation | async-start | bytes 524288 | tf_op jit(solution)/shard_map/all_to_all | solution.py:151
  19.6 35.1 %copy-start.2 = (bf16[1,64,5120]{2,1,0:T(8,128)(2,1)S(1)}, bf16[1,64,5120]{2,1,0:T(8,128)(2,1)}, u32[]{:S(2)}) copy-start(bf16[1,64,5120]{2,1,0:T(8,128)(2,1)} %param.12) | copy-start | bytes 1966084
  19.6 70.7 %all-gather.3.cloned.1.call-start = ((), (), s32[]{:S(2)}) async-start(), calls=%async_computation.5 | async-start | bytes 3244032 | tf_op jit(solution)/shard_map/all_gather | solution.py:184
  56.5 33.7 %copy-start.1 = (f32[128]{0:T(128)S(1)}, f32[128]{0:T(128)}, u32[]{:S(2)}) copy-start(f32[128]{0:T(128)} %param.16) | copy-start | bytes 1540
  56.5 33.7 %all-to-all-start.2 = ((bf16[4,64,5120]{2,1,0:T(8,128)(2,1)}), bf16[4,64,5120]{2,1,0:T(8,128)(2,1)S(1)}, u32[]{:S(2)}, u32[]{:S(2)}) async-start(bf16[4,64,5120]{2,1,0:T(8,128)(2,1)} %broadcast_in_dim.43), calls=%async_computation.2 | async-start | bytes 5242880 | tf_op jit(solution)/shard_map/all_to_all | solution.py:151
  90.3 1.1 copy-start
Sparse Core Ops, SparseCore 0:
  44.8 38.6 all-gather.2

commit v2 on v1

v2 whole, which is shorter than its diff:
```python
import math

import jax
import jax.numpy as jnp
from jax import lax
from jax.experimental import pallas as pl
from jax.experimental.pallas import tpu as pltpu
from jax.sharding import Mesh, PartitionSpec as P

adapter_scale = 0.5
norm_epsilon = 1e-06
masked_score = -1e30
HD = 128
NX, NY, NC, NZ = 4, 8, 2, 8
HALF = 2560
CTX = ("x", "y", "c")
bf16 = jnp.bfloat16
f32 = jnp.float32


def dot_nt(a, b):
    return lax.dot_general(a, b, (((1,), (1,)), ((), ())), preferred_element_type=f32)


def dot_nn(a, b):
    return lax.dot_general(a, b, (((1,), (0,)), ((), ())), preferred_element_type=f32)


def one_hot(origin, columns):
    lane = lax.broadcasted_iota(jnp.int32, (origin.shape[0], columns), 1)
    return jnp.where(lane == origin, 1.0, 0.0).astype(bf16)


def project(mine, left, right, far_a, far_b, gathered, down, up, keep, send, weight):
    target = lax.broadcasted_iota(jnp.int32, (320, 1), 0)
    s = (target >= 80).astype(jnp.int32)
    s = s + (target >= 160).astype(jnp.int32) + (target >= 240).astype(jnp.int32)
    within = target - 80 * s
    z = (within * 205) >> 11
    pick = one_hot(z * 40 + s * 10 + (within - 10 * z), 320)
    for y in range(NY):
        rows = dot_nn(pick, gathered[y * 320 : (y + 1) * 320, :]).astype(bf16)
        for x in range(2):
            start = x * 1280 + y * 160
            weight[start : start + 160, :] = rows[x * 160 : (x + 1) * 160, :]
    blocks = [mine[...], left[...], right[...]]
    blocks.append(jnp.concatenate([far_a[...], far_b[...]], axis=0))
    for b, rows in enumerate(blocks):
        low = dot_nn(rows, down[...]).astype(bf16)
        part = dot_nn(rows, weight[...]) + adapter_scale * dot_nn(low, up[...])
        keep[b * 64 : (b + 1) * 64, :] = part[0:64, :]
        send[b * 64 : (b + 1) * 64, :] = part[64:128, :].astype(bf16)


def attend(
    place, keep, taken, gain, mine, left, right, far_a, far_b, fresh, *rest
):
    asked, out, ordered = rest[0:NY], rest[NY], rest[NY + 1]
    slab_length = place[0]
    head = place[1]
    y = place[2]
    c = place[3]
    for d in range(NY):
        ordered[(y + NY - d) & 7] = asked[d][...].astype(f32).reshape(NX, 16, HD)
    queries = jnp.stack([ordered[i] for i in range(NY)], axis=1)
    queries = queries.reshape(512, HD).astype(bf16)

    projected = keep[...] + taken[...].astype(f32)
    raw_keys = projected[:, 0:HD]
    mean = jnp.mean(raw_keys * raw_keys, axis=-1, keepdims=True)
    new_keys = (raw_keys * lax.rsqrt(mean + norm_epsilon) * gain[...]).astype(bf16)
    new_values = projected[:, HD:].astype(bf16)

    shards = [head, (head + 3) & 3, (head + 1) & 3, (head + 2) & 3]
    column = lax.broadcasted_iota(jnp.int32, (1, 256), 1)
    block = column >> 6
    source = jnp.where(
        block == 0,
        shards[0],
        jnp.where(block == 1, shards[1], jnp.where(block == 2, shards[2], shards[3])),
    )
    initial = source * 1024 + (y * 2 + c) * 64 + (column & 63)
    slab_scores = jnp.where(
        initial < slab_length, dot_nt(queries, new_keys), masked_score
    )
    key_lanes = pl.ds(pl.multiple_of(head * HD, HD), HD)
    value_lanes = pl.ds(pl.multiple_of(512 + head * HD, HD), HD)
    arrays = [mine, left, right, far_a, far_b]
    cache_keys = jnp.concatenate([a[:, key_lanes] for a in arrays], axis=0)
    cache_values = jnp.concatenate([a[:, value_lanes] for a in arrays], axis=0)
    lane = lax.broadcasted_iota(jnp.int32, (1, HD), 1).astype(f32)
    news = [fresh[2 * shard + c].astype(f32) for shard in shards]
    filled = jnp.concatenate(
        [jnp.where(lane < new[10:11, :], 1.0, 0.0) for new in news], axis=1
    )
    cache_scores = jnp.where(filled > 0.5, dot_nt(queries, cache_keys), masked_score)
    fresh_keys = jnp.concatenate([new[8:9, :] for new in news] * 2, axis=0)
    fresh_values = jnp.concatenate([new[9:10, :] for new in news] * 2, axis=0)
    fresh_keys = fresh_keys.astype(bf16)
    fresh_values = fresh_values.astype(bf16)
    token = lax.broadcasted_iota(jnp.int32, (512, 8), 0) >> 3
    fresh_at = lax.broadcasted_iota(jnp.int32, (1, 8), 1)
    fresh_pos = jnp.where(
        fresh_at == 0,
        shards[0],
        jnp.where(
            fresh_at == 1, shards[1], jnp.where(fresh_at == 2, shards[2], shards[3])
        ),
    )
    fresh_pos = fresh_pos * 16 + y * 2 + c
    fresh_ok = (fresh_at < NX) & (fresh_pos <= token)
    fresh_scores = jnp.where(fresh_ok, dot_nt(queries, fresh_keys), masked_score)

    scale = 1.0 / math.sqrt(HD)
    row_max = jnp.maximum(
        jnp.maximum(
            jnp.max(slab_scores, axis=-1, keepdims=True),
            jnp.max(cache_scores, axis=-1, keepdims=True),
        ),
        jnp.max(fresh_scores, axis=-1, keepdims=True),
    )
    shift = (row_max * scale).astype(bf16).astype(f32)

    def weigh(scores, values):
        weights = jnp.exp(scores * scale - shift).astype(bf16)
        wide = jnp.concatenate([values, jnp.ones_like(values)], axis=1)
        return dot_nn(weights, wide)

    merged = (
        weigh(slab_scores, new_values)
        + weigh(cache_scores, cache_values)
        + weigh(fresh_scores, fresh_values)
    )
    total = merged[:, HD:]
    high = total.astype(bf16).astype(f32)
    lanes = lax.broadcasted_iota(jnp.int32, (512, HD), 1)
    stats = jnp.where(lanes == 0, shift, jnp.where(lanes == 1, high, total - high))
    target = lax.broadcasted_iota(jnp.int32, (512, 1), 0)
    offset = (((target >> 1) & 3) + 4 - head) & 3
    at = jnp.where(
        offset == 0, 0, jnp.where(offset == 1, 2, jnp.where(offset == 2, 3, 1))
    )
    origin = (target & 1) * 256 + at * 64 + (target >> 3)
    spread = dot_nn(
        one_hot(origin, 512), jnp.concatenate([new_keys, new_values], axis=0)
    )
    out[:, 0:HD] = merged[:, 0:HD].astype(bf16)
    out[:, HD : 2 * HD] = stats.astype(bf16)
    out[:, 2 * HD :] = spread.astype(bf16)


def merge(parts, slab, attended):
    heads = []
    rebuilt = []
    for h in range(NX):
        block = parts[h * 128 : (h + 1) * 128, :]
        output = block[:, 0:HD].astype(f32).reshape(16, 8, HD)
        stats = block[:, HD : 2 * HD].astype(f32).reshape(16, 8, HD)
        rebuilt.append(block[:, 2 * HD :])
        shift = stats[:, :, 0:1]
        total = stats[:, :, 1:2] + stats[:, :, 2:3]
        largest = jnp.max(shift, axis=0, keepdims=True)
        factor = jnp.exp(shift - largest)
        merged_total = jnp.sum(factor * total, axis=0)
        merged_output = jnp.sum(factor * output, axis=0)
        heads.append(merged_output / merged_total)
    attended[...] = jnp.concatenate(heads, axis=0).astype(bf16)
    target = lax.broadcasted_iota(jnp.int32, (128, 1), 0)
    origin = (target & 15) * 8 + ((target >> 4) & 3) * 2 + (target >> 6)
    pick = one_hot(origin, 128)
    placed = dot_nn(pick, jnp.concatenate(rebuilt, axis=1)).astype(bf16)
    slab[:, 0:512] = placed[0:64, :]
    slab[:, 512:1024] = placed[64:128, :]


def shift_by(value, axis, step):
    size = lax.axis_size(axis)
    return lax.ppermute(value, axis, [(i, (i + step) % size) for i in range(size)])


def body(
    hidden_slab,
    projection,
    adapter_down,
    adapter_up,
    key_gain,
    cache_keys,
    cache_values,
    fresh_keys,
    fresh_values,
    queries,
    slab_length,
    cache_length,
):
    head = lax.axis_index("x")
    y = lax.axis_index("y")
    c = lax.axis_index("c")

    by_head = projection.reshape(10, 2, NX, HD).transpose(2, 1, 0, 3)
    count = jnp.broadcast_to(
        cache_length.astype(f32).astype(bf16).reshape(1, 1, 1), (NX, 1, HD)
    )
    bundle = jnp.concatenate(
        [
            by_head.reshape(NX, 20, HD),
            queries.reshape(NX, 8, HD),
            fresh_keys.reshape(NX, 1, HD),
            fresh_values.reshape(NX, 1, HD),
            count,
            jnp.zeros((NX, 1, HD), bf16),
        ],
        axis=1,
    )
    bundle = jnp.broadcast_to(bundle[:, None], (NX, NC, 32, HD))
    bundle = lax.all_to_all(
        bundle.reshape(NX * NC, 32, HD), ("x", "c"), 0, 0, tiled=True
    )
    weight = lax.dynamic_slice(bundle, (4 * c, 0, 0), (4, 20, HD))
    weight = weight.reshape(4, 2, 10, HD).transpose(0, 2, 1, 3).reshape(1, 40, 256)
    gathered = lax.all_to_all(
        jnp.broadcast_to(weight, (NY * NZ, 40, 256)), ("y", "z"), 0, 0, tiled=True
    )
    asked = bundle[:, 20:28].reshape(64, HD)
    asked = [asked] + [shift_by(asked, "y", d) for d in range(1, NY)]
    fresh = bundle[:, 20:32]

    rows = hidden_slab[0]
    own = lax.dynamic_slice(rows, (0, c * HALF), (64, HALF))
    other = lax.dynamic_slice(rows, (0, (1 - c) * HALF), (64, HALF))
    other = shift_by(other, "c", 1)
    mine = jnp.concatenate(
        [
            jnp.concatenate([own, other], axis=0),
            cache_keys[0],
            cache_values[0],
        ],
        axis=1,
    )
    left = shift_by(mine, "x", 1)
    right = shift_by(mine, "x", -1)
    far_a = shift_by(left[0:64], "x", 1)
    far_b = shift_by(right[64:128], "x", -1)

    down = lax.dynamic_slice(adapter_down[0], (c * HALF, 0), (HALF, 64))
    up = lax.dynamic_slice(adapter_up[0], (0, 0, head * HD), (2, 32, HD))
    empty = jnp.zeros((32, HD), bf16)
    up = jnp.concatenate(
        [
            jnp.concatenate([up[0], empty], axis=1),
            jnp.concatenate([empty, up[1]], axis=1),
        ],
        axis=0,
    )
    hidden_specs = [pl.BlockSpec((128, HALF), lambda i: (0, 0))] * 3
    hidden_specs += [pl.BlockSpec((64, HALF), lambda i: (0, 0))] * 2
    whole = pl.BlockSpec(memory_space=pltpu.VMEM)
    ring = (mine, left, right, far_a, far_b)
    keep, send = pl.pallas_call(
        project,
        grid=(1,),
        in_specs=hidden_specs + [whole] * 3,
        out_specs=[whole] * 2,
        out_shape=[
            jax.ShapeDtypeStruct((256, 256), f32),
            jax.ShapeDtypeStruct((256, 256), bf16),
        ],
        scratch_shapes=[pltpu.VMEM((HALF, 256), bf16)],
        compiler_params=pltpu.CompilerParams(vmem_limit_bytes=40 * 1024 * 1024),
    )(*ring, gathered.reshape(NY * NZ * 40, 256), down, up)
    taken = shift_by(send, "c", 1)

    place = jnp.stack([slab_length[0], head, y, c]).astype(jnp.int32)
    context = [a[:, HALF:] for a in ring]
    parts = pl.pallas_call(
        attend,
        in_specs=[pl.BlockSpec(memory_space=pltpu.SMEM)] + [whole] * (9 + NY),
        out_specs=whole,
        out_shape=jax.ShapeDtypeStruct((512, 384), bf16),
        scratch_shapes=[pltpu.VMEM((NY, NX, 16, HD), f32)],
        compiler_params=pltpu.CompilerParams(vmem_limit_bytes=40 * 1024 * 1024),
    )(place, keep, taken, key_gain.reshape(1, HD), *context, fresh, *asked)
    parts = lax.all_to_all(parts.reshape(64, 8, 384), CTX, 0, 0, tiled=True)
    slab, attended = pl.pallas_call(
        merge,
        out_shape=[
            jax.ShapeDtypeStruct((64, 1024), bf16),
            jax.ShapeDtypeStruct((32, HD), bf16),
        ],
        compiler_params=pltpu.CompilerParams(vmem_limit_bytes=32 * 1024 * 1024),
    )(parts.reshape(512, 384))
    return slab[None], attended.reshape(1, 1, 32 * HD)


def solution(mesh):
    fine = Mesh(mesh.devices.reshape(NX, NY, NC, NZ), ("x", "y", "c", "z"))
    return jax.shard_map(
        body,
        mesh=fine,
        in_specs=(
            P("z", CTX, None),
            P(CTX + ("z",), None),
            P("z", None, None),
            P("z", None, None, None),
            P(),
            P("z", CTX, None),
            P("z", CTX, None),
            P("z", CTX, None),
            P("z", CTX, None),
            P("z", CTX, None),
            P("z"),
            P("z", CTX),
        ),
        out_specs=(P("z", CTX, None), P("z", CTX, None)),
        check_vma=False,
    )
```

time: 132 us -> 146 us (1.11)
  starting transfers between devices: 14.7 us -> 71.1 us
  blocking collectives: 48.4 us -> 19.1 us
  waiting for transfers between devices: 37.9 us -> 24.3 us
  between operations: 15.5 us -> 2.37 us
  local copies, waits for them, and re-layouts: 6.95 us -> 17.3 us
  other arithmetic: 1.01 us -> 2.95 us
    ppermute x0 -> x13, starting transfers between devices: none -> 48.9 us  [shift_by(): lax.ppermute(value, axis, [(i, (i + step) % size) for i in range(size)])]
    all_to_all x2, waiting for transfers between devices: 37.9 us -> 4.87 us  [the longest x1 4.87 us: body(): lax.all_to_all(bundle.reshape(NX * NC, 32, HD), ('x', 'c'), 0, 0, tiled=T...]
    all_to_all x2 -> x0, blocking collectives: 22.8 us -> none  [the longest x1 14.4 us: body(): bundle = lax.all_to_all(bundle, ('x', 'c'), 0, 0, tiled=True)]
    ppermute x0 -> x13, waiting for transfers between devices: none -> 19.4 us  [shift_by(): lax.ppermute(value, axis, [(i, (i + step) % size) for i in range(size)])]
    all_to_all x2, starting transfers between devices: 14.7 us -> 22.2 us  [the longest x1 12.1 us: body(): lax.all_to_all(jnp.broadcast_to(weight, (NY * NZ, 40, 256)), ('y', 'z'),...]
    all_to_all x1, blocking collectives: 25.6 us -> 19.1 us  [body(): parts = lax.all_to_all(parts.reshape(64, 8, 384), CTX, 0, 0, tiled=True)]
    slice x0 -> x7, local copies, waits for them, and re-layouts: none -> 6.24 us  [the longest x4 3.77 us: body(): context = [a[:, HALF:] for a in ring]]
    unnamed x16 -> x36, local copies, waits for them, and re-layouts: 1.35 us -> 4.16 us
  transfers between devices with their start and end apart: 3 -> 15, of which waited for: 2 -> 3; matrix products, arithmetic and copies ran while one was open for 3% -> 7% of each run, Pallas kernels for 0% -> 3%
where the time goes in v2:
time: 146 us; the launch traced here: 145 us
  starting transfers between devices  71.1 us (49%)
  waiting for transfers between devices  24.3 us (17%)
  blocking collectives  19.1 us (13%)
  local copies, waits for them, and re-layouts  17.3 us (12%)
  Pallas kernels  7.91 us (5%)
  other arithmetic  2.95 us (2%)
  between operations  2.37 us (2%)
    ppermute x13, starting transfers between devices, shift_by(): lax.ppermute(value, axis, [(i, (i + step) % size) for i in range(size)])  48.9 us
    ppermute x13, waiting for transfers between devices, shift_by(): lax.ppermute(value, axis, [(i, (i + step) % size) for i in range(size)])  19.4 us
    all_to_all x1, blocking collectives, body(): parts = lax.all_to_all(parts.reshape(64, 8, 384), CTX, 0, 0, tiled=True)  19.1 us
    all_to_all x1, starting transfers between devices, body(): lax.all_to_all(jnp.broadcast_to(weight, (NY * NZ, 40, 256)), ('y', 'z'),...  12.1 us
    all_to_all x1, starting transfers between devices, body(): lax.all_to_all(bundle.reshape(NX * NC, 32, HD), ('x', 'c'), 0, 0, tiled=T...  10.1 us
    all_to_all x1, waiting for transfers between devices, body(): lax.all_to_all(bundle.reshape(NX * NC, 32, HD), ('x', 'c'), 0, 0, tiled=T...  4.87 us
    pallas_call x1, Pallas kernels, body(): pl.pallas_call(project, grid=(1,), in_specs=hidden_specs + [whole] * 3, o...  4.76 us
    unnamed x36, local copies, waits for them, and re-layouts  4.16 us
  transfers between devices with their start and end apart: 15, of which 3 were waited for; matrix products, arithmetic and copies ran while one was open for 7% of the time, Pallas kernels for 3%

profile of v2, /device:TPU:1, one launch (start us, length us, event | category | flops | bytes accessed | tf_op | source)
XLA Modules:
  0.0 145.0 jit_solution(4783402836440907501)
XLA Ops:
  0.6 0.8 reshape.58
  1.5 0.8 reduce
  2.3 0.7 reduce.1
  3.0 0.7 reduce.2
  4.4 0.6 broadcast_in_dim.30
  5.1 10.1 %all-to-all-start = ((bf16[8,32,128]{2,1,0:T(8,128)(2,1)}), bf16[8,32,128]{2,1,0:T(8,128)(2,1)S(1)}, u32[]{:S(2)}, u32[]{:S(2)}) async-start(bf16[8,32,128]{2,1,0:T(8,128)(2,1)} %bitcast.10), calls=%async_computation | async-start | bytes 131072 | tf_op jit(solution)/shard_map/all_to_all | solution.py:215
  15.2 4.9 %all-to-all-done = bf16[8,32,128]{2,1,0:T(8,128)(2,1)S(1)} async-done(((bf16[8,32,128]{2,1,0:T(8,128)(2,1)}), bf16[8,32,128]{2,1,0:T(8,128)(2,1)S(1)}, u32[]{:S(2)}, u32[]{:S(2)}) %all-to-all-start) | async-done | bytes 65568 | tf_op jit(solution)/shard_map/all_to_all | solution.py:215
  20.1 1.2 broadcast_in_dim.32
  21.3 12.1 %all-to-all-start.1 = ((bf16[64,40,256]{2,1,0:T(8,128)(2,1)}), bf16[64,40,256]{2,1,0:T(8,128)(2,1)S(1)}, u32[]{:S(2)}, u32[]{:S(2)}) async-start(bf16[64,40,256]{2,1,0:T(8,128)(2,1)} %broadcast_in_dim.32), calls=%async_computation.1 | async-start | bytes 2621440 | tf_op jit(solution)/shard_map/all_to_all | solution.py:220
  33.5 3.1 %collective-permute-start = (bf16[64,2560]{1,0:T(8,128)(2,1)S(1)}, bf16[64,2560]{1,0:T(8,128)(2,1)S(1)}, u32[]{:S(2)}, u32[]{:S(2)}) collective-permute-start(bf16[64,2560]{1,0:T(8,128)(2,1)S(1)} %get-tuple-element.11), channel_id=1, source_target_pairs={{0,8},{8,0},{1,9},{9,1},{2,10},{10,2},{3,11},{11,3},{4,12},{12,4},... | collective-permute-start | bytes 983048 | tf_op jit(solution)/shard_map/ppermute | solution.py:178
  36.6 1.2 collective-permute-done
  37.8 0.1 pad_maximum_fusion.mine
  37.9 2.2 %collective-permute-start.1 = (bf16[128,3584]{1,0:T(8,128)(2,1)S(1)}, bf16[128,3584]{1,0:T(8,128)(2,1)S(1)}, u32[]{:S(2)}, u32[]{:S(2)}) collective-permute-start(bf16[128,3584]{1,0:T(8,128)(2,1)S(1)} %pad_maximum_fusion.mine), channel_id=1, source_target_pairs={{0,128},{128,256},{256,384},{384,0},{1,129},{129,257},{257,385},{3... | collective-permute-start | bytes 2752520 | tf_op jit(solution)/shard_map/ppermute | solution.py:178
  40.1 4.3 %collective-permute-start.2 = (bf16[128,3584]{1,0:T(8,128)(2,1)S(1)}, bf16[128,3584]{1,0:T(8,128)(2,1)S(1)}, u32[]{:S(2)}, u32[]{:S(2)}) collective-permute-start(bf16[128,3584]{1,0:T(8,128)(2,1)S(1)} %pad_maximum_fusion.mine), channel_id=1, source_target_pairs={{0,384},{128,0},{256,128},{384,256},{1,385},{129,1},{257,129},{385... | collective-permute-start | bytes 2752520 | tf_op jit(solution)/shard_map/ppermute | solution.py:178
  44.4 18.2 %collective-permute-done.1.left = bf16[128,3584]{1,0:T(8,128)(2,1)S(1)} collective-permute-done((bf16[128,3584]{1,0:T(8,128)(2,1)S(1)}, bf16[128,3584]{1,0:T(8,128)(2,1)S(1)}, u32[]{:S(2)}, u32[]{:S(2)}) %collective-permute-start.1) | collective-permute-done | bytes 917536 | tf_op jit(solution)/shard_map/ppermute | solution.py:178
  62.6 0.9 slice.44
  63.4 1.9 %collective-permute-start.3 = (bf16[64,3584]{1,0:T(8,128)(2,1)}, bf16[64,3584]{1,0:T(8,128)(2,1)}, u32[]{:S(2)}, u32[]{:S(2)}) collective-permute-start(bf16[64,3584]{1,0:T(8,128)(2,1)} %slice.44), channel_id=1, source_target_pairs={{0,128},{128,256},{256,384},{384,0},{1,129},{129,257},{257,385},{3... | collective-permute-start | bytes 1376264 | tf_op jit(solution)/shard_map/ppermute | solution.py:178
  65.4 0.8 slice.45
  66.2 0.3 copy-done.3
  66.5 4.6 %collective-permute-start.4 = (bf16[64,3584]{1,0:T(8,128)(2,1)}, bf16[64,3584]{1,0:T(8,128)(2,1)}, u32[]{:S(2)}, u32[]{:S(2)}) collective-permute-start(bf16[64,3584]{1,0:T(8,128)(2,1)} %slice.45), channel_id=1, source_target_pairs={{0,384},{128,0},{256,128},{384,256},{1,385},{129,1},{257,129},{385... | collective-permute-start | bytes 1376264 | tf_op jit(solution)/shard_map/ppermute | solution.py:178
  71.0 0.8 constant_dynamic-slice_fusion
  71.8 1.3 copy.27
  73.1 0.7 dynamic-slice_bitcast_fusion.3
  73.8 0.6 fusion.2.up
  74.5 0.8 slice_bitcast_fusion.rest_0_
  75.2 3.2 %collective-permute-start.6 = (bf16[64,128]{1,0:T(8,128)(2,1)S(1)}, bf16[64,128]{1,0:T(8,128)(2,1)}, u32[]{:S(2)}, u32[]{:S(2)}) collective-permute-start(bf16[64,128]{1,0:T(8,128)(2,1)S(1)} %slice_bitcast_fusion.rest_0_), channel_id=1, source_target_pairs={{0,16},{16,32},{32,48},{48,64},{64,80},{80,96},{96,112},{112,0},{1... | collective-permute-start | bytes 49160 | tf_op jit(solution)/shard_map/ppermute | solution.py:178
  78.4 4.0 %collective-permute-start.7 = (bf16[64,128]{1,0:T(8,128)(2,1)S(1)}, bf16[64,128]{1,0:T(8,128)(2,1)}, u32[]{:S(2)}, u32[]{:S(2)}) collective-permute-start(bf16[64,128]{1,0:T(8,128)(2,1)S(1)} %slice_bitcast_fusion.rest_0_), channel_id=1, source_target_pairs={{0,32},{16,48},{32,64},{48,80},{64,96},{80,112},{96,0},{112,16},{1... | collective-permute-start | bytes 49160 | tf_op jit(solution)/shard_map/ppermute | solution.py:178
  82.5 4.5 %collective-permute-start.8 = (bf16[64,128]{1,0:T(8,128)(2,1)S(1)}, bf16[64,128]{1,0:T(8,128)(2,1)}, u32[]{:S(2)}, u32[]{:S(2)}) collective-permute-start(bf16[64,128]{1,0:T(8,128)(2,1)S(1)} %slice_bitcast_fusion.rest_0_), channel_id=1, source_target_pairs={{0,48},{16,64},{32,80},{48,96},{64,112},{80,0},{96,16},{112,32},{1... | collective-permute-start | bytes 49160 | tf_op jit(solution)/shard_map/ppermute | solution.py:178
  87.0 1.2 copy-done.2
  88.2 1.2 copy-done.4
  89.4 0.8 copy-done.7
  90.1 4.8 %shard_map.131 = (f32[256,256]{1,0:T(8,128)S(1)}, bf16[256,256]{1,0:T(8,128)(2,1)}) custom-call(bf16[128,3584]{1,0:T(8,128)(2,1)S(1)} %pad_maximum_fusion.mine, bf16[128,3584]{1,0:T(8,128)(2,1)S(1)} %copy-done.2, bf16[128,3584]{1,0:T(8,128)(2,1)S(1)} %copy-done.4, bf16[64,3584]{1,0:T(8,128)(2,1)} %collective-permute-done.3.far_a, ...), custom_call_target="tpu_custom_call" | custom-call | tf_op jit(solution)/shard_map/pallas_call | solution.py:258
  94.9 0.7 copy-done.5
  95.6 4.6 %collective-permute-start.5 = (bf16[256,256]{1,0:T(8,128)(2,1)}, bf16[256,256]{1,0:T(8,128)(2,1)S(1)}, u32[]{:S(2)}, u32[]{:S(2)}) collective-permute-start(bf16[256,256]{1,0:T(8,128)(2,1)} %get-tuple-element.7), channel_id=1, source_target_pairs={{0,8},{8,0},{1,9},{9,1},{2,10},{10,2},{3,11},{11,3},{4,12},{12,4},... | collective-permute-start | bytes 393224 | tf_op jit(solution)/shard_map/ppermute | solution.py:178
  100.9 3.8 %collective-permute-start.9 = (bf16[64,128]{1,0:T(8,128)(2,1)S(1)}, bf16[64,128]{1,0:T(8,128)(2,1)S(1)}, u32[]{:S(2)}, u32[]{:S(2)}) collective-permute-start(bf16[64,128]{1,0:T(8,128)(2,1)S(1)} %slice_bitcast_fusion.rest_0_), channel_id=1, source_target_pairs={{0,64},{16,80},{32,96},{48,112},{64,0},{80,16},{96,32},{112,48},{1... | collective-permute-start | bytes 49160 | tf_op jit(solution)/shard_map/ppermute | solution.py:178
  104.7 4.6 %collective-permute-start.10 = (bf16[64,128]{1,0:T(8,128)(2,1)S(1)}, bf16[64,128]{1,0:T(8,128)(2,1)S(1)}, u32[]{:S(2)}, u32[]{:S(2)}) collective-permute-start(bf16[64,128]{1,0:T(8,128)(2,1)S(1)} %slice_bitcast_fusion.rest_0_), channel_id=1, source_target_pairs={{0,80},{16,96},{32,112},{48,0},{64,16},{80,32},{96,48},{112,64},{1... | collective-permute-start | bytes 49160 | tf_op jit(solution)/shard_map/ppermute | solution.py:178
  109.3 5.1 %collective-permute-start.11 = (bf16[64,128]{1,0:T(8,128)(2,1)S(1)}, bf16[64,128]{1,0:T(8,128)(2,1)S(1)}, u32[]{:S(2)}, u32[]{:S(2)}) collective-permute-start(bf16[64,128]{1,0:T(8,128)(2,1)S(1)} %slice_bitcast_fusion.rest_0_), channel_id=1, source_target_pairs={{0,96},{16,112},{32,0},{48,16},{64,32},{80,48},{96,64},{112,80},{1... | collective-permute-start | bytes 49160 | tf_op jit(solution)/shard_map/ppermute | solution.py:178
  114.4 3.0 %collective-permute-start.12 = (bf16[64,128]{1,0:T(8,128)(2,1)S(1)}, bf16[64,128]{1,0:T(8,128)(2,1)S(1)}, u32[]{:S(2)}, u32[]{:S(2)}) collective-permute-start(bf16[64,128]{1,0:T(8,128)(2,1)S(1)} %slice_bitcast_fusion.rest_0_), channel_id=1, source_target_pairs={{0,112},{16,0},{32,16},{48,32},{64,48},{80,64},{96,80},{112,96},{1... | collective-permute-start | bytes 49160 | tf_op jit(solution)/shard_map/ppermute | solution.py:178
  117.4 0.1 pad_add_fusion.place
  117.5 0.8 slice.50.fresh
  118.3 1.0 slice.46.left
  119.3 1.0 slice.47.right
  120.2 0.9 slice.48.far_a
  121.2 0.9 slice.49.far_b
  122.1 2.1 %shard_map.132 = bf16[512,384]{1,0:T(8,128)(2,1)S(1)} custom-call(s32[4]{0:T(128)S(1)} %pad_add_fusion.place, f32[256,256]{1,0:T(8,128)S(1)} %copy-done.6, bf16[256,256]{1,0:T(8,128)(2,1)S(1)} %collective-permute-done.5.taken, f32[1,128]{1,0:T(1,128)S(1)} %bitcast.43, bf16[128,1024]{1,0:T(8,128)(2,1)S(1)} %pad_maximum_fusion.1.mine, ...), custom_call_target="tpu_custom_call" | custom-call | tf_op jit(solution)/shard_map/pallas_call | solution.py:274
  124.3 19.1 %all_to_all.15 = bf16[64,8,384]{2,1,0:T(8,128)(2,1)S(1)} all-to-all(bf16[64,8,384]{2,1,0:T(8,128)(2,1)S(1)} %bitcast.41), channel_id=1, replica_groups=mesh['x'=4,'y'=8,'c'=2,'z'=8] {'x','y','c'}, dimensions={0} | all-to-all | bytes 786432 | tf_op jit(solution)/shard_map/all_to_all | solution.py:282
  143.4 1.0 shard_map.133
  144.4 0.6 reshape.70
  (51 shorter events, 0.3 us)
Async XLA Ops:
  0.6 70.4 %copy-start = (bf16[1,5120,64]{1,2,0:T(8,128)(2,1)S(1)}, bf16[1,5120,64]{1,2,0:T(8,128)(2,1)}, u32[]{:S(2)}) copy-start(bf16[1,5120,64]{1,2,0:T(8,128)(2,1)} %param.14) | copy-start | bytes 1966084
  5.1 15.0 %all-to-all-start = ((bf16[8,32,128]{2,1,0:T(8,128)(2,1)}), bf16[8,32,128]{2,1,0:T(8,128)(2,1)S(1)}, u32[]{:S(2)}, u32[]{:S(2)}) async-start(bf16[8,32,128]{2,1,0:T(8,128)(2,1)} %bitcast.10), calls=%async_computation | async-start | bytes 131072 | tf_op jit(solution)/shard_map/all_to_all | solution.py:215
  20.1 1.2 copy-start.14
  21.3 12.1 %copy-start.9 = (bf16[1,64,5120]{2,1,0:T(8,128)(2,1)S(1)}, bf16[1,64,5120]{2,1,0:T(8,128)(2,1)}, u32[]{:S(2)}) copy-start(bf16[1,64,5120]{2,1,0:T(8,128)(2,1)} %param.12) | copy-start | bytes 1966084
  21.3 65.7 %all-to-all-start.1 = ((bf16[64,40,256]{2,1,0:T(8,128)(2,1)}), bf16[64,40,256]{2,1,0:T(8,128)(2,1)S(1)}, u32[]{:S(2)}, u32[]{:S(2)}) async-start(bf16[64,40,256]{2,1,0:T(8,128)(2,1)} %broadcast_in_dim.32), calls=%async_computation.1 | async-start | bytes 2621440 | tf_op jit(solution)/shard_map/all_to_all | solution.py:220
  33.4 4.4 %copy-start.10 = (bf16[1,128,512]{2,1,0:T(8,128)(2,1)S(1)}, bf16[1,128,512]{2,1,0:T(8,128)(2,1)}, u32[]{:S(2)}) copy-start(bf16[1,128,512]{2,1,0:T(8,128)(2,1)} %param.18) | copy-start | bytes 393220
  33.4 4.4 %copy-start.12 = (bf16[1,128,512]{2,1,0:T(8,128)(2,1)S(1)}, bf16[1,128,512]{2,1,0:T(8,128)(2,1)}, u32[]{:S(2)}) copy-start(bf16[1,128,512]{2,1,0:T(8,128)(2,1)} %param.17) | copy-start | bytes 393220
  33.5 4.3 %collective-permute-start = (bf16[64,2560]{1,0:T(8,128)(2,1)S(1)}, bf16[64,2560]{1,0:T(8,128)(2,1)S(1)}, u32[]{:S(2)}, u32[]{:S(2)}) collective-permute-start(bf16[64,2560]{1,0:T(8,128)(2,1)S(1)} %get-tuple-element.11), channel_id=1, source_target_pairs={{0,8},{8,0},{1,9},{9,1},{2,10},{10,2},{3,11},{11,3},{4,12},{12,4},... | collective-permute-start | bytes 983048 | tf_op jit(solution)/shard_map/ppermute | solution.py:178
  37.9 24.7 %collective-permute-start.1 = (bf16[128,3584]{1,0:T(8,128)(2,1)S(1)}, bf16[128,3584]{1,0:T(8,128)(2,1)S(1)}, u32[]{:S(2)}, u32[]{:S(2)}) collective-permute-start(bf16[128,3584]{1,0:T(8,128)(2,1)S(1)} %pad_maximum_fusion.mine), channel_id=1, source_target_pairs={{0,128},{128,256},{256,384},{384,0},{1,129},{129,257},{257,385},{3... | collective-permute-start | bytes 2752520 | tf_op jit(solution)/shard_map/ppermute | solution.py:178
  40.1 25.3 %collective-permute-start.2 = (bf16[128,3584]{1,0:T(8,128)(2,1)S(1)}, bf16[128,3584]{1,0:T(8,128)(2,1)S(1)}, u32[]{:S(2)}, u32[]{:S(2)}) collective-permute-start(bf16[128,3584]{1,0:T(8,128)(2,1)S(1)} %pad_maximum_fusion.mine), channel_id=1, source_target_pairs={{0,384},{128,0},{256,128},{384,256},{1,385},{129,1},{257,129},{385... | collective-permute-start | bytes 2752520 | tf_op jit(solution)/shard_map/ppermute | solution.py:178
  62.6 2.8 %copy-start.1 = (bf16[128,3584]{1,0:T(8,128)(2,1)}, bf16[128,3584]{1,0:T(8,128)(2,1)S(1)}, u32[]{:S(2)}) copy-start(bf16[128,3584]{1,0:T(8,128)(2,1)S(1)} %collective-permute-done.1.left) | copy-start | bytes 2752516
  63.4 23.5 %collective-permute-start.3 = (bf16[64,3584]{1,0:T(8,128)(2,1)}, bf16[64,3584]{1,0:T(8,128)(2,1)}, u32[]{:S(2)}, u32[]{:S(2)}) collective-permute-start(bf16[64,3584]{1,0:T(8,128)(2,1)} %slice.44), channel_id=1, source_target_pairs={{0,128},{128,256},{256,384},{384,0},{1,129},{129,257},{257,385},{3... | collective-permute-start | bytes 1376264 | tf_op jit(solution)/shard_map/ppermute | solution.py:178
  65.4 1.1 copy-start.3
  66.5 20.5 %collective-permute-start.4 = (bf16[64,3584]{1,0:T(8,128)(2,1)}, bf16[64,3584]{1,0:T(8,128)(2,1)}, u32[]{:S(2)}, u32[]{:S(2)}) collective-permute-start(bf16[64,3584]{1,0:T(8,128)(2,1)} %slice.45), channel_id=1, source_target_pairs={{0,384},{128,0},{256,128},{384,256},{1,385},{129,1},{257,129},{385... | collective-permute-start | bytes 1376264 | tf_op jit(solution)/shard_map/ppermute | solution.py:178
  75.2 29.5 %collective-permute-start.6 = (bf16[64,128]{1,0:T(8,128)(2,1)S(1)}, bf16[64,128]{1,0:T(8,128)(2,1)}, u32[]{:S(2)}, u32[]{:S(2)}) collective-permute-start(bf16[64,128]{1,0:T(8,128)(2,1)S(1)} %slice_bitcast_fusion.rest_0_), channel_id=1, source_target_pairs={{0,16},{16,32},{32,48},{48,64},{64,80},{80,96},{96,112},{112,0},{1... | collective-permute-start | bytes 49160 | tf_op jit(solution)/shard_map/ppermute | solution.py:178
  78.4 30.8 %collective-permute-start.7 = (bf16[64,128]{1,0:T(8,128)(2,1)S(1)}, bf16[64,128]{1,0:T(8,128)(2,1)}, u32[]{:S(2)}, u32[]{:S(2)}) collective-permute-start(bf16[64,128]{1,0:T(8,128)(2,1)S(1)} %slice_bitcast_fusion.rest_0_), channel_id=1, source_target_pairs={{0,32},{16,48},{32,64},{48,80},{64,96},{80,112},{96,0},{112,16},{1... | collective-permute-start | bytes 49160 | tf_op jit(solution)/shard_map/ppermute | solution.py:178
  82.5 31.9 %collective-permute-start.8 = (bf16[64,128]{1,0:T(8,128)(2,1)S(1)}, bf16[64,128]{1,0:T(8,128)(2,1)}, u32[]{:S(2)}, u32[]{:S(2)}) collective-permute-start(bf16[64,128]{1,0:T(8,128)(2,1)S(1)} %slice_bitcast_fusion.rest_0_), channel_id=1, source_target_pairs={{0,48},{16,64},{32,80},{48,96},{64,112},{80,0},{96,16},{112,32},{1... | collective-permute-start | bytes 49160 | tf_op jit(solution)/shard_map/ppermute | solution.py:178
  87.0 1.2 copy-start.2
  88.2 1.2 copy-start.4
  89.3 0.8 copy-start.7
  90.1 10.1 %copy-start.11 = (bf16[1,128,512]{2,1,0:T(8,128)(2,1)S(1)}, bf16[1,128,512]{2,1,0:T(8,128)(2,1)}, u32[]{:S(2)}) copy-start(bf16[1,128,512]{2,1,0:T(8,128)(2,1)} %param.18) | copy-start | bytes 393220
  90.1 10.1 %copy-start.13 = (bf16[1,128,512]{2,1,0:T(8,128)(2,1)S(1)}, bf16[1,128,512]{2,1,0:T(8,128)(2,1)}, u32[]{:S(2)}) copy-start(bf16[1,128,512]{2,1,0:T(8,128)(2,1)} %param.17) | copy-start | bytes 393220
  94.9 0.7 copy-start.5
  95.6 26.6 %copy-start.8 = (f32[128]{0:T(128)S(1)}, f32[128]{0:T(128)}, u32[]{:S(2)}) copy-start(f32[128]{0:T(128)} %param.16) | copy-start | bytes 1540
  95.6 26.6 %copy-start.6 = (f32[256,256]{1,0:T(8,128)S(1)}, f32[256,256]{1,0:T(8,128)}, u32[]{:S(2)}) copy-start(f32[256,256]{1,0:T(8,128)} %copy-done.5) | copy-start | bytes 786436
  95.6 26.6 %collective-permute-start.5 = (bf16[256,256]{1,0:T(8,128)(2,1)}, bf16[256,256]{1,0:T(8,128)(2,1)S(1)}, u32[]{:S(2)}, u32[]{:S(2)}) collective-permute-start(bf16[256,256]{1,0:T(8,128)(2,1)} %get-tuple-element.7), channel_id=1, source_target_pairs={{0,8},{8,0},{1,9},{9,1},{2,10},{10,2},{3,11},{11,3},{4,12},{12,4},... | collective-permute-start | bytes 393224 | tf_op jit(solution)/shard_map/ppermute | solution.py:178
  100.9 21.2 %collective-permute-start.9 = (bf16[64,128]{1,0:T(8,128)(2,1)S(1)}, bf16[64,128]{1,0:T(8,128)(2,1)S(1)}, u32[]{:S(2)}, u32[]{:S(2)}) collective-permute-start(bf16[64,128]{1,0:T(8,128)(2,1)S(1)} %slice_bitcast_fusion.rest_0_), channel_id=1, source_target_pairs={{0,64},{16,80},{32,96},{48,112},{64,0},{80,16},{96,32},{112,48},{1... | collective-permute-start | bytes 49160 | tf_op jit(solution)/shard_map/ppermute | solution.py:178
  104.7 17.4 %collective-permute-start.10 = (bf16[64,128]{1,0:T(8,128)(2,1)S(1)}, bf16[64,128]{1,0:T(8,128)(2,1)S(1)}, u32[]{:S(2)}, u32[]{:S(2)}) collective-permute-start(bf16[64,128]{1,0:T(8,128)(2,1)S(1)} %slice_bitcast_fusion.rest_0_), channel_id=1, source_target_pairs={{0,80},{16,96},{32,112},{48,0},{64,16},{80,32},{96,48},{112,64},{1... | collective-permute-start | bytes 49160 | tf_op jit(solution)/shard_map/ppermute | solution.py:178
  109.3 12.8 %collective-permute-start.11 = (bf16[64,128]{1,0:T(8,128)(2,1)S(1)}, bf16[64,128]{1,0:T(8,128)(2,1)S(1)}, u32[]{:S(2)}, u32[]{:S(2)}) collective-permute-start(bf16[64,128]{1,0:T(8,128)(2,1)S(1)} %slice_bitcast_fusion.rest_0_), channel_id=1, source_target_pairs={{0,96},{16,112},{32,0},{48,16},{64,32},{80,48},{96,64},{112,80},{1... | collective-permute-start | bytes 49160 | tf_op jit(solution)/shard_map/ppermute | solution.py:178
  114.4 7.7 %collective-permute-start.12 = (bf16[64,128]{1,0:T(8,128)(2,1)S(1)}, bf16[64,128]{1,0:T(8,128)(2,1)S(1)}, u32[]{:S(2)}, u32[]{:S(2)}) collective-permute-start(bf16[64,128]{1,0:T(8,128)(2,1)S(1)} %slice_bitcast_fusion.rest_0_), channel_id=1, source_target_pairs={{0,112},{16,0},{32,16},{48,32},{64,48},{80,64},{96,80},{112,96},{1... | collective-permute-start | bytes 49160 | tf_op jit(solution)/shard_map/ppermute | solution.py:178

commit v3 on v2

v3 whole, which is shorter than its diff:
```python
import math

import jax
import jax.numpy as jnp
from jax import lax
from jax.experimental import pallas as pl
from jax.experimental.pallas import tpu as pltpu
from jax.sharding import Mesh, PartitionSpec as P

adapter_scale = 0.5
norm_epsilon = 1e-06
masked_score = -1e30
HD = 128
NX, NY, NC, NZ = 4, 8, 2, 8
HALF = 2560
CTX = ("x", "y", "c")
bf16 = jnp.bfloat16
f32 = jnp.float32


def dot_nt(a, b):
    return lax.dot_general(a, b, (((1,), (1,)), ((), ())), preferred_element_type=f32)


def dot_nn(a, b):
    return lax.dot_general(a, b, (((1,), (0,)), ((), ())), preferred_element_type=f32)


def one_hot(origin, columns):
    lane = lax.broadcasted_iota(jnp.int32, (origin.shape[0], columns), 1)
    return jnp.where(lane == origin, 1.0, 0.0).astype(bf16)


def prepare(weight, asked, new_key, new_value, count, hidden, down, bundle, low):
    filled = jnp.broadcast_to(count[0].astype(f32), (1, HD))
    rows = weight[...].astype(f32)
    questions = asked[...].astype(f32)
    keys = new_key[...].astype(f32)
    values = new_value[...].astype(f32)
    for h in range(NX):
        lanes = slice(h * HD, (h + 1) * HD)
        pieces = [rows[:, lanes], rows[:, 512 + h * HD : 512 + (h + 1) * HD]]
        for g in range(8):
            start = (h * 8 + g) * HD
            pieces.append(questions[:, start : start + HD])
        pieces += [keys[:, lanes], values[:, lanes], filled, jnp.zeros((1, HD), f32)]
        block = jnp.concatenate(pieces, axis=0).astype(bf16)
        bundle[2 * h] = block
        bundle[2 * h + 1] = block
    own = dot_nt(hidden[...], down[...]).astype(bf16)
    low[...] = jnp.concatenate([own, jnp.zeros((64, 64), bf16)], axis=1)


def project(*refs):
    near, other, gathered = refs[0:4], refs[4:8], refs[8]
    keep, send, low = refs[9:12]
    near_rows, other_rows, arrived, weight, sems = refs[12:]
    copies = [pltpu.make_async_copy(gathered, arrived, sems.at[0])]
    for d in range(NX):
        copies.append(pltpu.make_async_copy(near[d], near_rows.at[d], sems.at[1 + d]))
        copies.append(pltpu.make_async_copy(other[d], other_rows.at[d], sems.at[5 + d]))
    for copy in copies:
        copy.start()
    target = lax.broadcasted_iota(jnp.int32, (320, 1), 0)
    s = (target >= 80).astype(jnp.int32)
    s = s + (target >= 160).astype(jnp.int32) + (target >= 240).astype(jnp.int32)
    within = target - 80 * s
    z = (within * 205) >> 11
    pick = one_hot(z * 40 + s * 10 + (within - 10 * z), 320)
    copies[0].wait()
    for y in range(NY):
        rows = dot_nn(pick, arrived[y * 320 : (y + 1) * 320, :]).astype(bf16)
        for x in range(2):
            start = x * 1280 + y * 160
            weight[start : start + 160, :] = rows[x * 160 : (x + 1) * 160, :]
    for copy in copies[1:]:
        copy.wait()
    for d in range(NX):
        low[d * 64 : (d + 1) * 64, :] = near_rows[d, :, HALF:]
    keep[...] = dot_nn(near_rows[:, :, 0:HALF].reshape(256, HALF), weight[...])
    send[...] = dot_nn(other_rows[...].reshape(256, HALF), weight[...])


def attend(place, keep, taken, low, up, gain, *rest):
    context, fresh, asked = rest[0:NX], rest[NX], rest[NX + 1 : NX + 5]
    out, ordered = rest[NX + 5 :]
    slab_length = place[0]
    head = place[1]
    y = place[2]
    c = place[3]
    for d in range(NY):
        part, row = [(0, 0), (1, 0), (2, 0), (2, 1), (3, 0), (3, 1), (3, 2), (3, 3)][d]
        block = asked[part][row * 64 : (row + 1) * 64, :]
        ordered[(y + NY - d) & 7] = block.astype(f32).reshape(NX, 16, HD)
    queries = jnp.stack([ordered[i] for i in range(NY)], axis=1)
    queries = queries.reshape(512, HD).astype(bf16)

    delta = dot_nn(low[:, 0:64], up[...])
    projected = keep[...] + taken[...] + adapter_scale * delta
    raw_keys = projected[:, 0:HD]
    mean = jnp.mean(raw_keys * raw_keys, axis=-1, keepdims=True)
    new_keys = (raw_keys * lax.rsqrt(mean + norm_epsilon) * gain[...]).astype(bf16)
    new_values = projected[:, HD:].astype(bf16)

    shards = [(head + NX - d) & 3 for d in range(NX)]

    def by_block(index):
        return jnp.where(
            index == 0,
            shards[0],
            jnp.where(index == 1, shards[1], jnp.where(index == 2, shards[2], shards[3])),
        )

    column = lax.broadcasted_iota(jnp.int32, (1, 256), 1)
    initial = by_block(column >> 6) * 1024 + (y * 2 + c) * 64 + (column & 63)
    slab_scores = jnp.where(
        initial < slab_length, dot_nt(queries, new_keys), masked_score
    )
    cache_keys = jnp.concatenate([a[0:128, :] for a in context], axis=0)
    cache_values = jnp.concatenate([a[128:256, :] for a in context], axis=0)
    lane = lax.broadcasted_iota(jnp.int32, (1, HD), 1).astype(f32)
    news = [fresh[2 * shard + c].astype(f32) for shard in shards]
    filled = jnp.concatenate(
        [jnp.where(lane < new[10:11, :], 1.0, 0.0) for new in news], axis=1
    )
    cache_scores = jnp.where(filled > 0.5, dot_nt(queries, cache_keys), masked_score)
    fresh_keys = jnp.concatenate([new[8:9, :] for new in news] * 2, axis=0)
    fresh_values = jnp.concatenate([new[9:10, :] for new in news] * 2, axis=0)
    fresh_keys = fresh_keys.astype(bf16)
    fresh_values = fresh_values.astype(bf16)
    token = lax.broadcasted_iota(jnp.int32, (512, 8), 0) >> 3
    fresh_at = lax.broadcasted_iota(jnp.int32, (1, 8), 1)
    fresh_pos = by_block(fresh_at) * 16 + y * 2 + c
    fresh_ok = (fresh_at < NX) & (fresh_pos <= token)
    fresh_scores = jnp.where(fresh_ok, dot_nt(queries, fresh_keys), masked_score)

    scale = 1.0 / math.sqrt(HD)
    row_max = jnp.maximum(
        jnp.maximum(
            jnp.max(slab_scores, axis=-1, keepdims=True),
            jnp.max(cache_scores, axis=-1, keepdims=True),
        ),
        jnp.max(fresh_scores, axis=-1, keepdims=True),
    )
    shift = (row_max * scale).astype(bf16).astype(f32)

    def weigh(scores, values):
        weights = jnp.exp(scores * scale - shift).astype(bf16)
        wide = jnp.concatenate([values, jnp.ones_like(values)], axis=1)
        return dot_nn(weights, wide)

    merged = (
        weigh(slab_scores, new_values)
        + weigh(cache_scores, cache_values)
        + weigh(fresh_scores, fresh_values)
    )
    total = merged[:, HD:]
    high = total.astype(bf16).astype(f32)
    lanes = lax.broadcasted_iota(jnp.int32, (512, HD), 1)
    stats = jnp.where(lanes == 0, shift, jnp.where(lanes == 1, high, total - high))
    target = lax.broadcasted_iota(jnp.int32, (512, 1), 0)
    at = (head + NX - ((target >> 1) & 3)) & 3
    origin = (target & 1) * 256 + at * 64 + (target >> 3)
    spread = dot_nn(
        one_hot(origin, 512), jnp.concatenate([new_keys, new_values], axis=0)
    )
    out[:, 0:HD] = merged[:, 0:HD].astype(bf16)
    out[:, HD : 2 * HD] = stats.astype(bf16)
    out[:, 2 * HD :] = spread.astype(bf16)


def merge(parts, slab, attended):
    heads = []
    rebuilt = []
    for h in range(NX):
        block = parts[h * 128 : (h + 1) * 128, :]
        output = block[:, 0:HD].astype(f32).reshape(16, 8, HD)
        stats = block[:, HD : 2 * HD].astype(f32).reshape(16, 8, HD)
        rebuilt.append(block[:, 2 * HD :])
        shift = stats[:, :, 0:1]
        total = stats[:, :, 1:2] + stats[:, :, 2:3]
        largest = jnp.max(shift, axis=0, keepdims=True)
        factor = jnp.exp(shift - largest)
        merged_total = jnp.sum(factor * total, axis=0)
        merged_output = jnp.sum(factor * output, axis=0)
        heads.append(merged_output / merged_total)
    for h in range(NX):
        for g in range(8):
            start = (h * 8 + g) * HD
            attended[:, start : start + HD] = heads[h][g : g + 1, :].astype(bf16)
    target = lax.broadcasted_iota(jnp.int32, (128, 1), 0)
    origin = (target & 15) * 8 + ((target >> 4) & 3) * 2 + (target >> 6)
    pick = one_hot(origin, 128)
    placed = dot_nn(pick, jnp.concatenate(rebuilt, axis=1)).astype(bf16)
    slab[:, 0:512] = placed[0:64, :]
    slab[:, 512:1024] = placed[64:128, :]


def shift_by(value, axis, step):
    size = lax.axis_size(axis)
    return lax.ppermute(value, axis, [(i, (i + step) % size) for i in range(size)])


def body(
    hidden_slab,
    projection,
    adapter_down,
    adapter_up,
    key_gain,
    cache_keys,
    cache_values,
    fresh_keys,
    fresh_values,
    queries,
    slab_length,
    cache_length,
):
    head = lax.axis_index("x")
    y = lax.axis_index("y")
    c = lax.axis_index("c")
    whole = pl.BlockSpec(memory_space=pltpu.VMEM)
    scalars = pl.BlockSpec(memory_space=pltpu.SMEM)
    anywhere = pl.BlockSpec(memory_space=pl.ANY)
    rows = hidden_slab[0]

    bundle, low = pl.pallas_call(
        prepare,
        in_specs=[whole] * 4 + [scalars] + [whole] * 2,
        out_specs=[whole] * 2,
        out_shape=[
            jax.ShapeDtypeStruct((NX * NC, 32, HD), bf16),
            jax.ShapeDtypeStruct((64, HD), bf16),
        ],
        compiler_params=pltpu.CompilerParams(vmem_limit_bytes=24 * 1024 * 1024),
    )(
        projection,
        queries[0],
        fresh_keys[0],
        fresh_values[0],
        cache_length[0],
        rows,
        adapter_down[0].T,
    )
    bundle = lax.all_to_all(bundle, ("x", "c"), 0, 0, tiled=True)
    weight = lax.dynamic_slice(bundle, (4 * c, 0, 0), (4, 20, HD))
    weight = weight.reshape(4, 2, 10, HD).transpose(0, 2, 1, 3).reshape(1, 40, 256)
    gathered = lax.all_to_all(
        jnp.broadcast_to(weight, (NY * NZ, 40, 256)), ("y", "z"), 0, 0, tiled=True
    )
    asked = [bundle[:, 20:28].reshape(64, HD)]
    asked.append(shift_by(asked[0], "y", 1))
    asked.append(shift_by(jnp.concatenate(asked, axis=0), "y", 2))
    asked.append(shift_by(jnp.concatenate(asked, axis=0), "y", 4))
    fresh = bundle[:, 20:32]

    own = lax.dynamic_slice(rows, (0, c * HALF), (64, HALF))
    own = jnp.concatenate([own, low], axis=1)
    other = lax.dynamic_slice(rows, (0, (1 - c) * HALF), (64, HALF))
    other = shift_by(other, "c", 1)
    near = [own, shift_by(own, "x", 1), None, shift_by(own, "x", -1)]
    others = [other, shift_by(other, "x", 1), None, shift_by(other, "x", -1)]
    near[2] = shift_by(near[1], "x", 1)
    others[2] = shift_by(others[3], "x", -1)

    by_head = jnp.concatenate([cache_keys[0], cache_values[0]], axis=0)
    by_head = by_head.reshape(256, NX, HD).transpose(1, 0, 2)
    context = []
    for d in range(NX):
        block = lax.dynamic_index_in_dim(by_head, (head + d) & 3, 0, keepdims=False)
        context.append(block if d == 0 else shift_by(block, "x", d))

    up = lax.dynamic_slice(adapter_up[0], (0, 0, head * HD), (2, 32, HD))
    empty = jnp.zeros((32, HD), bf16)
    up = jnp.concatenate(
        [
            jnp.concatenate([up[0], empty], axis=1),
            jnp.concatenate([empty, up[1]], axis=1),
        ],
        axis=0,
    )
    gathered, asked, context, up, fresh = lax.optimization_barrier(
        (gathered, asked, context, up, fresh)
    )
    keep, send, low = pl.pallas_call(
        project,
        in_specs=[anywhere] * 9,
        out_specs=[whole] * 3,
        out_shape=[
            jax.ShapeDtypeStruct((256, 256), f32),
            jax.ShapeDtypeStruct((256, 256), f32),
            jax.ShapeDtypeStruct((256, HD), bf16),
        ],
        scratch_shapes=[
            pltpu.VMEM((NX, 64, HALF + HD), bf16),
            pltpu.VMEM((NX, 64, HALF), bf16),
            pltpu.VMEM((HALF, 256), bf16),
            pltpu.VMEM((HALF, 256), bf16),
            pltpu.SemaphoreType.DMA((9,)),
        ],
        compiler_params=pltpu.CompilerParams(vmem_limit_bytes=32 * 1024 * 1024),
    )(*near, *others, gathered.reshape(HALF, 256))
    taken = shift_by(send, "c", 1)

    place = jnp.stack([slab_length[0], head, y, c]).astype(jnp.int32)
    parts = pl.pallas_call(
        attend,
        in_specs=[scalars] + [whole] * 14,
        out_specs=whole,
        out_shape=jax.ShapeDtypeStruct((512, 384), bf16),
        scratch_shapes=[pltpu.VMEM((NY, NX, 16, HD), f32)],
        compiler_params=pltpu.CompilerParams(vmem_limit_bytes=32 * 1024 * 1024),
    )(place, keep, taken, low, up, key_gain.reshape(1, HD), *context, fresh, *asked)
    parts = lax.all_to_all(parts.reshape(64, 8, 384), CTX, 0, 0, tiled=True)
    slab, attended = pl.pallas_call(
        merge,
        out_shape=[
            jax.ShapeDtypeStruct((64, 1024), bf16),
            jax.ShapeDtypeStruct((1, 32 * HD), bf16),
        ],
        compiler_params=pltpu.CompilerParams(vmem_limit_bytes=24 * 1024 * 1024),
    )(parts.reshape(512, 384))
    return slab[None], attended[None]


def solution(mesh):
    fine = Mesh(mesh.devices.reshape(NX, NY, NC, NZ), ("x", "y", "c", "z"))
    return jax.shard_map(
        body,
        mesh=fine,
        in_specs=(
            P("z", CTX, None),
            P(CTX + ("z",), None),
            P("z", None, None),
            P("z", None, None, None),
            P(),
            P("z", CTX, None),
            P("z", CTX, None),
            P("z", CTX, None),
            P("z", CTX, None),
            P("z", CTX, None),
            P("z"),
            P("z", CTX),
        ),
        out_specs=(P("z", CTX, None), P("z", CTX, None)),
        check_vma=False,
    )
```

time: 146 us -> 142 us (0.973)
  blocking collectives: 19.1 us -> 23.6 us
  waiting for transfers between devices: 24.3 us -> 20.4 us
  other arithmetic: 2.95 us -> 0.12 us
    unnamed x36 -> x46, local copies, waits for them, and re-layouts: 4.16 us -> 12.2 us
    slice x6 -> x0, local copies, waits for them, and re-layouts: 5.47 us -> none  [the longest x4 3.77 us: body(): context = [a[:, HALF:] for a in ring]]
    all_to_all x1, blocking collectives: 19.1 us -> 23.6 us  [body(): parts = lax.all_to_all(parts.reshape(64, 8, 384), CTX, 0, 0, tiled=True)]
    ppermute x13 -> x14, waiting for transfers between devices: 19.4 us -> 15.6 us  [shift_by(): lax.ppermute(value, axis, [(i, (i + step) % size) for i in range(size)])]
    reshape x4 -> x1, local copies, waits for them, and re-layouts: 2.23 us -> 0.01 us  [body(): asked = [bundle[:, 20:28].reshape(64, HD)]]
    unnamed x3 -> x0, other arithmetic: 2.17 us -> none
    dynamic_slice x3 -> x1, local copies, waits for them, and re-layouts: 2.12 us -> 0.05 us  [body(): other = lax.dynamic_slice(rows, (0, (1 - c) * HALF), (64, HALF))]
    ppermute x13 -> x14, starting transfers between devices: 48.9 us -> 47.5 us  [shift_by(): lax.ppermute(value, axis, [(i, (i + step) % size) for i in range(size)])]
  transfers between devices with their start and end apart: 15 -> 16, of which waited for: 3 -> 6; matrix products, arithmetic and copies ran while one was open for 7% -> 2% of each run, Pallas kernels for 3% -> 0%
where the time goes in v3:
time: 142 us; the launch traced here: 140 us
  starting transfers between devices  69.7 us (49%)
  blocking collectives  23.6 us (17%)
  waiting for transfers between devices  20.4 us (14%)
  local copies, waits for them, and re-layouts  16.6 us (12%)
  Pallas kernels  7.29 us (5%)
  between operations  2.33 us (2%)
    ppermute x14, starting transfers between devices, shift_by(): lax.ppermute(value, axis, [(i, (i + step) % size) for i in range(size)])  47.5 us
    all_to_all x1, blocking collectives, body(): parts = lax.all_to_all(parts.reshape(64, 8, 384), CTX, 0, 0, tiled=True)  23.6 us
    ppermute x14, waiting for transfers between devices, shift_by(): lax.ppermute(value, axis, [(i, (i + step) % size) for i in range(size)])  15.6 us
    unnamed x46, local copies, waits for them, and re-layouts  12.2 us
    all_to_all x1, starting transfers between devices, body(): lax.all_to_all(jnp.broadcast_to(weight, (NY * NZ, 40, 256)), ('y', 'z'),...  12.1 us
    all_to_all x1, starting transfers between devices, body(): bundle = lax.all_to_all(bundle, ('x', 'c'), 0, 0, tiled=True)  10.1 us
    all_to_all x1, waiting for transfers between devices, body(): bundle = lax.all_to_all(bundle, ('x', 'c'), 0, 0, tiled=True)  4.87 us
    pallas_call x1, Pallas kernels, body(): pl.pallas_call(project, in_specs=[anywhere] * 9, out_specs=[whole] * 3, o...  3.38 us
  transfers between devices with their start and end apart: 16, of which 6 were waited for; matrix products, arithmetic and copies ran while one was open for 2% of the time, Pallas kernels for 0%

profile of v3, /device:TPU:1, one launch (start us, length us, event | category | flops | bytes accessed | tf_op | source)
XLA Modules:
  0.0 140.2 jit_solution(6567687381302051464)
XLA Ops:
  1.3 1.1 copy-done
  2.4 1.1 copy-done.2
  3.5 0.8 copy-done.15
  4.2 0.7 copy-done.16
  4.9 0.7 copy-done.17
  5.6 0.7 copy-done.18
  6.3 0.8 shard_map.131
  7.1 10.1 %all-to-all-start = ((bf16[8,32,128]{2,1,0:T(8,128)(2,1)}), bf16[8,32,128]{2,1,0:T(8,128)(2,1)S(1)}, u32[]{:S(2)}, u32[]{:S(2)}) async-start(bf16[8,32,128]{2,1,0:T(8,128)(2,1)} %get-tuple-element.21), calls=%async_computation | async-start | bytes 131072 | tf_op jit(solution)/shard_map/all_to_all | solution.py:244
  17.3 4.9 %all-to-all-done = bf16[8,32,128]{2,1,0:T(8,128)(2,1)S(1)} async-done(((bf16[8,32,128]{2,1,0:T(8,128)(2,1)}), bf16[8,32,128]{2,1,0:T(8,128)(2,1)S(1)}, u32[]{:S(2)}, u32[]{:S(2)}) %all-to-all-start) | async-done | bytes 65568 | tf_op jit(solution)/shard_map/all_to_all | solution.py:244
  22.2 1.2 broadcast_in_dim.15
  23.4 12.1 %all-to-all-start.1 = ((bf16[64,40,256]{2,1,0:T(8,128)(2,1)}), bf16[64,40,256]{2,1,0:T(8,128)(2,1)S(1)}, u32[]{:S(2)}, u32[]{:S(2)}) async-start(bf16[64,40,256]{2,1,0:T(8,128)(2,1)} %broadcast_in_dim.15), calls=%async_computation.1 | async-start | bytes 2621440 | tf_op jit(solution)/shard_map/all_to_all | solution.py:247
  35.6 2.2 %collective-permute-start = (bf16[64,2688]{1,0:T(8,128)(2,1)S(1)}, bf16[64,2688]{1,0:T(8,128)(2,1)S(1)}, u32[]{:S(2)}, u32[]{:S(2)}) collective-permute-start(bf16[64,2688]{1,0:T(8,128)(2,1)S(1)} %pad_maximum_fusion.refs_0_), channel_id=1, source_target_pairs={{0,128},{128,256},{256,384},{384,0},{1,129},{129,257},{257,385},{3... | collective-permute-start | bytes 1032200 | tf_op jit(solution)/shard_map/ppermute | solution.py:201
  37.8 4.3 %collective-permute-start.2 = (bf16[64,2688]{1,0:T(8,128)(2,1)S(1)}, bf16[64,2688]{1,0:T(8,128)(2,1)S(1)}, u32[]{:S(2)}, u32[]{:S(2)}) collective-permute-start(bf16[64,2688]{1,0:T(8,128)(2,1)S(1)} %pad_maximum_fusion.refs_0_), channel_id=1, source_target_pairs={{0,384},{128,0},{256,128},{384,256},{1,385},{129,1},{257,129},{385... | collective-permute-start | bytes 1032200 | tf_op jit(solution)/shard_map/ppermute | solution.py:201
  42.1 3.5 %collective-permute-start.3 = (bf16[64,2560]{1,0:T(8,128)(2,1)S(1)}, bf16[64,2560]{1,0:T(8,128)(2,1)S(1)}, u32[]{:S(2)}, u32[]{:S(2)}) collective-permute-start(bf16[64,2560]{1,0:T(8,128)(2,1)S(1)} %get-tuple-element.38), channel_id=1, source_target_pairs={{0,8},{8,0},{1,9},{9,1},{2,10},{10,2},{3,11},{11,3},{4,12},{12,4},... | collective-permute-start | bytes 983048 | tf_op jit(solution)/shard_map/ppermute | solution.py:201
  45.7 0.9 concatenate.30
  46.7 0.2 collective-permute-done.3.refs_4_
  46.9 1.9 %collective-permute-start.5 = (bf16[64,2560]{1,0:T(8,128)(2,1)S(1)}, bf16[64,2560]{1,0:T(8,128)(2,1)S(1)}, u32[]{:S(2)}, u32[]{:S(2)}) collective-permute-start(bf16[64,2560]{1,0:T(8,128)(2,1)S(1)} %collective-permute-done.3.refs_4_), channel_id=1, source_target_pairs={{0,384},{128,0},{256,128},{384,256},{1,385},{129,1},{257,129},{385... | collective-permute-start | bytes 983048 | tf_op jit(solution)/shard_map/ppermute | solution.py:201
  48.8 3.2 %collective-permute-start.7 = (bf16[64,128]{1,0:T(8,128)(2,1)S(1)}, bf16[64,128]{1,0:T(8,128)(2,1)S(1)}, u32[]{:S(2)}, u32[]{:S(2)}) collective-permute-start(bf16[64,128]{1,0:T(8,128)(2,1)S(1)} %slice_bitcast_fusion.rest_5_), channel_id=1, source_target_pairs={{0,16},{16,32},{32,48},{48,64},{64,80},{80,96},{96,112},{112,0},{1... | collective-permute-start | bytes 49160 | tf_op jit(solution)/shard_map/ppermute | solution.py:201
  52.0 0.7 dynamic-slice_bitcast_fusion.2
  52.7 3.3 %collective-permute-start.10 = (bf16[256,128]{1,0:T(8,128)(2,1)}, bf16[256,128]{1,0:T(8,128)(2,1)S(1)}, u32[]{:S(2)}, u32[]{:S(2)}) collective-permute-start(bf16[256,128]{1,0:T(8,128)(2,1)} %get-tuple-element.42), channel_id=1, source_target_pairs={{0,128},{128,256},{256,384},{384,0},{1,129},{129,257},{257,385},{3... | collective-permute-start | bytes 196616 | tf_op jit(solution)/shard_map/ppermute | solution.py:201
  56.1 7.8 %collective-permute-done.7.rest_6_ = bf16[64,128]{1,0:T(8,128)(2,1)S(1)} collective-permute-done((bf16[64,128]{1,0:T(8,128)(2,1)S(1)}, bf16[64,128]{1,0:T(8,128)(2,1)S(1)}, u32[]{:S(2)}, u32[]{:S(2)}) %collective-permute-start.7) | collective-permute-done | bytes 16416 | tf_op jit(solution)/shard_map/ppermute | solution.py:201
  63.9 2.6 %collective-permute-start.11 = (bf16[256,128]{1,0:T(8,128)(2,1)}, bf16[256,128]{1,0:T(8,128)(2,1)S(1)}, u32[]{:S(2)}, u32[]{:S(2)}) collective-permute-start(bf16[256,128]{1,0:T(8,128)(2,1)} %get-tuple-element.41), channel_id=1, source_target_pairs={{0,256},{128,384},{256,0},{384,128},{1,257},{129,385},{257,1},{385... | collective-permute-start | bytes 196616 | tf_op jit(solution)/shard_map/ppermute | solution.py:201
  66.5 2.7 %collective-permute-start.1 = (bf16[64,2688]{1,0:T(8,128)(2,1)S(1)}, bf16[64,2688]{1,0:T(8,128)(2,1)S(1)}, u32[]{:S(2)}, u32[]{:S(2)}) collective-permute-start(bf16[64,2688]{1,0:T(8,128)(2,1)S(1)} %collective-permute-done.refs_1_), channel_id=1, source_target_pairs={{0,128},{128,256},{256,384},{384,0},{1,129},{129,257},{257,385},{3... | collective-permute-start | bytes 1032200 | tf_op jit(solution)/shard_map/ppermute | solution.py:201
  69.2 3.8 %collective-permute-start.8 = (bf16[128,128]{1,0:T(8,128)(2,1)S(1)}, bf16[128,128]{1,0:T(8,128)(2,1)S(1)}, u32[]{:S(2)}, u32[]{:S(2)}) collective-permute-start(bf16[128,128]{1,0:T(8,128)(2,1)S(1)} %pad_maximum_fusion.2), channel_id=1, source_target_pairs={{0,32},{16,48},{32,64},{48,80},{64,96},{80,112},{96,0},{112,16},{1... | collective-permute-start | bytes 98312 | tf_op jit(solution)/shard_map/ppermute | solution.py:201
  73.0 3.1 %collective-permute-start.4 = (bf16[64,2560]{1,0:T(8,128)(2,1)S(1)}, bf16[64,2560]{1,0:T(8,128)(2,1)}, u32[]{:S(2)}, u32[]{:S(2)}) collective-permute-start(bf16[64,2560]{1,0:T(8,128)(2,1)S(1)} %collective-permute-done.3.refs_4_), channel_id=1, source_target_pairs={{0,128},{128,256},{256,384},{384,0},{1,129},{129,257},{257,385},{3... | collective-permute-start | bytes 983048 | tf_op jit(solution)/shard_map/ppermute | solution.py:201
  76.2 3.4 %collective-permute-start.6 = (bf16[64,2560]{1,0:T(8,128)(2,1)S(1)}, bf16[64,2560]{1,0:T(8,128)(2,1)}, u32[]{:S(2)}, u32[]{:S(2)}) collective-permute-start(bf16[64,2560]{1,0:T(8,128)(2,1)S(1)} %collective-permute-done.5.refs_7_), channel_id=1, source_target_pairs={{0,384},{128,0},{256,128},{384,256},{1,385},{129,1},{257,129},{385... | collective-permute-start | bytes 983048 | tf_op jit(solution)/shard_map/ppermute | solution.py:201
  79.6 0.7 dynamic-slice_bitcast_fusion.7
  80.3 2.6 %collective-permute-start.12 = (bf16[256,128]{1,0:T(8,128)(2,1)}, bf16[256,128]{1,0:T(8,128)(2,1)S(1)}, u32[]{:S(2)}, u32[]{:S(2)}) collective-permute-start(bf16[256,128]{1,0:T(8,128)(2,1)} %get-tuple-element.40), channel_id=1, source_target_pairs={{0,384},{128,0},{256,128},{384,256},{1,385},{129,1},{257,129},{385... | collective-permute-start | bytes 196616 | tf_op jit(solution)/shard_map/ppermute | solution.py:201
  82.9 3.7 %collective-permute-done.12.rest_3_ = bf16[256,128]{1,0:T(8,128)(2,1)S(1)} collective-permute-done((bf16[256,128]{1,0:T(8,128)(2,1)}, bf16[256,128]{1,0:T(8,128)(2,1)S(1)}, u32[]{:S(2)}, u32[]{:S(2)}) %collective-permute-start.12) | collective-permute-done | bytes 65568 | tf_op jit(solution)/shard_map/ppermute | solution.py:201
  86.7 4.9 %collective-permute-start.9 = (bf16[256,128]{1,0:T(8,128)(2,1)S(1)}, bf16[256,128]{1,0:T(8,128)(2,1)S(1)}, u32[]{:S(2)}, u32[]{:S(2)}) collective-permute-start(bf16[256,128]{1,0:T(8,128)(2,1)S(1)} %pad_maximum_fusion.1), channel_id=1, source_target_pairs={{0,64},{16,80},{32,96},{48,112},{64,0},{80,16},{96,32},{112,48},{1... | collective-permute-start | bytes 196616 | tf_op jit(solution)/shard_map/ppermute | solution.py:201
  91.5 0.8 slice.19.rest_4_
  92.3 3.2 %collective-permute-done.9.rest_8_ = bf16[256,128]{1,0:T(8,128)(2,1)S(1)} collective-permute-done((bf16[256,128]{1,0:T(8,128)(2,1)S(1)}, bf16[256,128]{1,0:T(8,128)(2,1)S(1)}, u32[]{:S(2)}, u32[]{:S(2)}) %collective-permute-start.9) | collective-permute-done | bytes 65568 | tf_op jit(solution)/shard_map/ppermute | solution.py:201
  95.6 0.6 copy-done.11
  96.2 3.4 %shard_map.132 = (f32[256,256]{1,0:T(8,128)S(1)}, f32[256,256]{1,0:T(8,128)}, bf16[256,128]{1,0:T(8,128)(2,1)S(1)}) custom-call(bf16[64,2688]{1,0:T(8,128)(2,1)S(1)} %pad_maximum_fusion.refs_0_, bf16[64,2688]{1,0:T(8,128)(2,1)S(1)} %collective-permute-done.refs_1_, bf16[64,2688]{1,0:T(8,128)(2,1)S(1)} %collective-permute-done.1.refs_2_, ...), custom_call_target="tpu_custom_call" | custom-call | tf_op jit(solution)/shard_map/pallas_call | solution.py:284
  99.6 0.7 copy-done.3
  100.3 0.6 copy-done.13
  100.9 6.0 %collective-permute-start.13 = (f32[256,256]{1,0:T(8,128)}, f32[256,256]{1,0:T(8,128)S(1)}, u32[]{:S(2)}, u32[]{:S(2)}) collective-permute-start(f32[256,256]{1,0:T(8,128)} %get-tuple-element.24), channel_id=1, source_target_pairs={{0,8},{8,0},{1,9},{9,1},{2,10},{10,2},{3,11},{11,3},{4,12},{12,4},... | collective-permute-start | bytes 786440 | tf_op jit(solution)/shard_map/ppermute | solution.py:201
  107.6 0.1 pad_add_fusion.place
  107.7 0.6 collective-permute-done.13.taken
  108.3 0.9 copy-done.4
  109.2 0.8 copy-done.6
  110.1 0.8 copy-done.8
  110.9 0.8 copy-done.10
  111.8 0.8 copy-done.12
  112.6 0.8 copy-done.14
  113.4 2.1 %shard_map.133 = bf16[512,384]{1,0:T(8,128)(2,1)S(1)} custom-call(s32[4]{0:T(128)S(1)} %pad_add_fusion.place, f32[256,256]{1,0:T(8,128)S(1)} %copy-done.4, f32[256,256]{1,0:T(8,128)S(1)} %collective-permute-done.13.taken, bf16[256,128]{1,0:T(8,128)(2,1)S(1)} %copy-done.14, bf16[64,256]{1,0:T(8,128)(2,1)S(1)} %fusion.2.up, f32[1,128]{1,0:T(1,128)S(1)} %bitcast.52, ...), custom_call_target="tpu_custom_call" | custom-call | tf_op jit(solution)/shard_map/pallas_call | solution.py:305
  115.5 23.6 %all_to_all.15 = bf16[64,8,384]{2,1,0:T(8,128)(2,1)S(1)} all-to-all(bf16[64,8,384]{2,1,0:T(8,128)(2,1)S(1)} %bitcast.47), channel_id=1, replica_groups=mesh['x'=4,'y'=8,'c'=2,'z'=8] {'x','y','c'}, dimensions={0} | all-to-all | bytes 786432 | tf_op jit(solution)/shard_map/all_to_all | solution.py:313
  139.1 1.0 shard_map.134
  (52 shorter events, 0.3 us)
Async XLA Ops:
  1.3 1.1 copy-start
  2.4 1.1 copy-start.2
  3.5 0.8 copy-start.15
  4.2 0.7 copy-start.16
  4.9 0.7 copy-start.17
  5.6 0.7 copy-start.18
  7.1 15.0 %all-to-all-start = ((bf16[8,32,128]{2,1,0:T(8,128)(2,1)}), bf16[8,32,128]{2,1,0:T(8,128)(2,1)S(1)}, u32[]{:S(2)}, u32[]{:S(2)}) async-start(bf16[8,32,128]{2,1,0:T(8,128)(2,1)} %get-tuple-element.21), calls=%async_computation | async-start | bytes 131072 | tf_op jit(solution)/shard_map/all_to_all | solution.py:244
  22.1 26.7 %copy-start.20 = (bf16[8,32,128]{2,1,0:T(8,128)(2,1)}, bf16[8,32,128]{2,1,0:T(8,128)(2,1)S(1)}, u32[]{:S(2)}) copy-start(bf16[8,32,128]{2,1,0:T(8,128)(2,1)S(1)} %all-to-all-done) | copy-start | bytes 196612
  23.4 12.1 %copy-start.1 = (bf16[1,64,5120]{2,1,0:T(8,128)(2,1)S(1)}, bf16[1,64,5120]{2,1,0:T(8,128)(2,1)}, u32[]{:S(2)}) copy-start(bf16[1,64,5120]{2,1,0:T(8,128)(2,1)} %param.12) | copy-start | bytes 1966084
  23.4 72.8 %all-to-all-start.1 = ((bf16[64,40,256]{2,1,0:T(8,128)(2,1)}), bf16[64,40,256]{2,1,0:T(8,128)(2,1)S(1)}, u32[]{:S(2)}, u32[]{:S(2)}) async-start(bf16[64,40,256]{2,1,0:T(8,128)(2,1)} %broadcast_in_dim.15), calls=%async_computation.1 | async-start | bytes 2621440 | tf_op jit(solution)/shard_map/all_to_all | solution.py:247
  35.5 10.2 %copy-start.21 = (bf16[1,128,512]{2,1,0:T(8,128)(2,1)S(1)}, bf16[1,128,512]{2,1,0:T(8,128)(2,1)}, u32[]{:S(2)}) copy-start(bf16[1,128,512]{2,1,0:T(8,128)(2,1)} %param.17) | copy-start | bytes 393220
  35.6 30.9 %collective-permute-start = (bf16[64,2688]{1,0:T(8,128)(2,1)S(1)}, bf16[64,2688]{1,0:T(8,128)(2,1)S(1)}, u32[]{:S(2)}, u32[]{:S(2)}) collective-permute-start(bf16[64,2688]{1,0:T(8,128)(2,1)S(1)} %pad_maximum_fusion.refs_0_), channel_id=1, source_target_pairs={{0,128},{128,256},{256,384},{384,0},{1,129},{129,257},{257,385},{3... | collective-permute-start | bytes 1032200 | tf_op jit(solution)/shard_map/ppermute | solution.py:201
  37.8 58.4 %collective-permute-start.2 = (bf16[64,2688]{1,0:T(8,128)(2,1)S(1)}, bf16[64,2688]{1,0:T(8,128)(2,1)S(1)}, u32[]{:S(2)}, u32[]{:S(2)}) collective-permute-start(bf16[64,2688]{1,0:T(8,128)(2,1)S(1)} %pad_maximum_fusion.refs_0_), channel_id=1, source_target_pairs={{0,384},{128,0},{256,128},{384,256},{1,385},{129,1},{257,129},{385... | collective-permute-start | bytes 1032200 | tf_op jit(solution)/shard_map/ppermute | solution.py:201
  42.1 4.8 %collective-permute-start.3 = (bf16[64,2560]{1,0:T(8,128)(2,1)S(1)}, bf16[64,2560]{1,0:T(8,128)(2,1)S(1)}, u32[]{:S(2)}, u32[]{:S(2)}) collective-permute-start(bf16[64,2560]{1,0:T(8,128)(2,1)S(1)} %get-tuple-element.38), channel_id=1, source_target_pairs={{0,8},{8,0},{1,9},{9,1},{2,10},{10,2},{3,11},{11,3},{4,12},{12,4},... | collective-permute-start | bytes 983048 | tf_op jit(solution)/shard_map/ppermute | solution.py:201
  46.9 29.3 %collective-permute-start.5 = (bf16[64,2560]{1,0:T(8,128)(2,1)S(1)}, bf16[64,2560]{1,0:T(8,128)(2,1)S(1)}, u32[]{:S(2)}, u32[]{:S(2)}) collective-permute-start(bf16[64,2560]{1,0:T(8,128)(2,1)S(1)} %collective-permute-done.3.refs_4_), channel_id=1, source_target_pairs={{0,384},{128,0},{256,128},{384,256},{1,385},{129,1},{257,129},{385... | collective-permute-start | bytes 983048 | tf_op jit(solution)/shard_map/ppermute | solution.py:201
  48.8 15.1 %collective-permute-start.7 = (bf16[64,128]{1,0:T(8,128)(2,1)S(1)}, bf16[64,128]{1,0:T(8,128)(2,1)S(1)}, u32[]{:S(2)}, u32[]{:S(2)}) collective-permute-start(bf16[64,128]{1,0:T(8,128)(2,1)S(1)} %slice_bitcast_fusion.rest_5_), channel_id=1, source_target_pairs={{0,16},{16,32},{32,48},{48,64},{64,80},{80,96},{96,112},{112,0},{1... | collective-permute-start | bytes 49160 | tf_op jit(solution)/shard_map/ppermute | solution.py:201
  52.7 16.5 %collective-permute-start.10 = (bf16[256,128]{1,0:T(8,128)(2,1)}, bf16[256,128]{1,0:T(8,128)(2,1)S(1)}, u32[]{:S(2)}, u32[]{:S(2)}) collective-permute-start(bf16[256,128]{1,0:T(8,128)(2,1)} %get-tuple-element.42), channel_id=1, source_target_pairs={{0,128},{128,256},{256,384},{384,0},{1,129},{129,257},{257,385},{3... | collective-permute-start | bytes 196616 | tf_op jit(solution)/shard_map/ppermute | solution.py:201
  63.9 9.1 %collective-permute-start.11 = (bf16[256,128]{1,0:T(8,128)(2,1)}, bf16[256,128]{1,0:T(8,128)(2,1)S(1)}, u32[]{:S(2)}, u32[]{:S(2)}) collective-permute-start(bf16[256,128]{1,0:T(8,128)(2,1)} %get-tuple-element.41), channel_id=1, source_target_pairs={{0,256},{128,384},{256,0},{384,128},{1,257},{129,385},{257,1},{385... | collective-permute-start | bytes 196616 | tf_op jit(solution)/shard_map/ppermute | solution.py:201
  66.5 29.7 %collective-permute-start.1 = (bf16[64,2688]{1,0:T(8,128)(2,1)S(1)}, bf16[64,2688]{1,0:T(8,128)(2,1)S(1)}, u32[]{:S(2)}, u32[]{:S(2)}) collective-permute-start(bf16[64,2688]{1,0:T(8,128)(2,1)S(1)} %collective-permute-done.refs_1_), channel_id=1, source_target_pairs={{0,128},{128,256},{256,384},{384,0},{1,129},{129,257},{257,385},{3... | collective-permute-start | bytes 1032200 | tf_op jit(solution)/shard_map/ppermute | solution.py:201
  69.2 22.3 %copy-start.5 = (bf16[256,128]{1,0:T(8,128)(2,1)}, bf16[256,128]{1,0:T(8,128)(2,1)S(1)}, u32[]{:S(2)}) copy-start(bf16[256,128]{1,0:T(8,128)(2,1)S(1)} %collective-permute-done.10.rest_1_) | copy-start | bytes 196612
  69.2 11.1 %collective-permute-start.8 = (bf16[128,128]{1,0:T(8,128)(2,1)S(1)}, bf16[128,128]{1,0:T(8,128)(2,1)S(1)}, u32[]{:S(2)}, u32[]{:S(2)}) collective-permute-start(bf16[128,128]{1,0:T(8,128)(2,1)S(1)} %pad_maximum_fusion.2), channel_id=1, source_target_pairs={{0,32},{16,48},{32,64},{48,80},{64,96},{80,112},{96,0},{112,16},{1... | collective-permute-start | bytes 98312 | tf_op jit(solution)/shard_map/ppermute | solution.py:201
  73.0 19.3 %copy-start.7 = (bf16[256,128]{1,0:T(8,128)(2,1)}, bf16[256,128]{1,0:T(8,128)(2,1)S(1)}, u32[]{:S(2)}) copy-start(bf16[256,128]{1,0:T(8,128)(2,1)S(1)} %collective-permute-done.11.rest_2_) | copy-start | bytes 196612
  73.0 23.1 %collective-permute-start.4 = (bf16[64,2560]{1,0:T(8,128)(2,1)S(1)}, bf16[64,2560]{1,0:T(8,128)(2,1)}, u32[]{:S(2)}, u32[]{:S(2)}) collective-permute-start(bf16[64,2560]{1,0:T(8,128)(2,1)S(1)} %collective-permute-done.3.refs_4_), channel_id=1, source_target_pairs={{0,128},{128,256},{256,384},{384,0},{1,129},{129,257},{257,385},{3... | collective-permute-start | bytes 983048 | tf_op jit(solution)/shard_map/ppermute | solution.py:201
  76.2 20.0 %collective-permute-start.6 = (bf16[64,2560]{1,0:T(8,128)(2,1)S(1)}, bf16[64,2560]{1,0:T(8,128)(2,1)}, u32[]{:S(2)}, u32[]{:S(2)}) collective-permute-start(bf16[64,2560]{1,0:T(8,128)(2,1)S(1)} %collective-permute-done.5.refs_7_), channel_id=1, source_target_pairs={{0,384},{128,0},{256,128},{384,256},{1,385},{129,1},{257,129},{385... | collective-permute-start | bytes 983048 | tf_op jit(solution)/shard_map/ppermute | solution.py:201
  80.3 6.4 %collective-permute-start.12 = (bf16[256,128]{1,0:T(8,128)(2,1)}, bf16[256,128]{1,0:T(8,128)(2,1)S(1)}, u32[]{:S(2)}, u32[]{:S(2)}) collective-permute-start(bf16[256,128]{1,0:T(8,128)(2,1)} %get-tuple-element.40), channel_id=1, source_target_pairs={{0,384},{128,0},{256,128},{384,256},{1,385},{129,1},{257,129},{385... | collective-permute-start | bytes 196616 | tf_op jit(solution)/shard_map/ppermute | solution.py:201
  86.7 5.7 %copy-start.9 = (bf16[256,128]{1,0:T(8,128)(2,1)}, bf16[256,128]{1,0:T(8,128)(2,1)S(1)}, u32[]{:S(2)}) copy-start(bf16[256,128]{1,0:T(8,128)(2,1)S(1)} %collective-permute-done.12.rest_3_) | copy-start | bytes 196612
  86.7 8.9 %collective-permute-start.9 = (bf16[256,128]{1,0:T(8,128)(2,1)S(1)}, bf16[256,128]{1,0:T(8,128)(2,1)S(1)}, u32[]{:S(2)}, u32[]{:S(2)}) collective-permute-start(bf16[256,128]{1,0:T(8,128)(2,1)S(1)} %pad_maximum_fusion.1), channel_id=1, source_target_pairs={{0,64},{16,80},{32,96},{48,112},{64,0},{80,16},{96,32},{112,48},{1... | collective-permute-start | bytes 196616 | tf_op jit(solution)/shard_map/ppermute | solution.py:201
  95.6 0.6 copy-start.11
  96.2 12.1 %copy-start.19 = (f32[128]{0:T(128)S(1)}, f32[128]{0:T(128)}, u32[]{:S(2)}) copy-start(f32[128]{0:T(128)} %param.16) | copy-start | bytes 1540
  99.6 0.7 copy-start.3
  100.3 0.6 copy-start.13
  100.9 7.3 %collective-permute-start.13 = (f32[256,256]{1,0:T(8,128)}, f32[256,256]{1,0:T(8,128)S(1)}, u32[]{:S(2)}, u32[]{:S(2)}) collective-permute-start(f32[256,256]{1,0:T(8,128)} %get-tuple-element.24), channel_id=1, source_target_pairs={{0,8},{8,0},{1,9},{9,1},{2,10},{10,2},{3,11},{11,3},{4,12},{12,4},... | collective-permute-start | bytes 786440 | tf_op jit(solution)/shard_map/ppermute | solution.py:201
  108.3 1.0 copy-start.4
  109.2 0.8 copy-start.6
  110.1 0.8 copy-start.8
  110.9 0.8 copy-start.10
  111.8 0.8 copy-start.12
  112.6 0.8 copy-start.14

commit v4 on v3

v4 whole, which is shorter than its diff:
```python
import math

import jax
import jax.numpy as jnp
from jax import lax
from jax.experimental import pallas as pl
from jax.experimental.pallas import tpu as pltpu
from jax.sharding import Mesh, PartitionSpec as P

adapter_scale = 0.5
norm_epsilon = 1e-06
masked_score = -1e30
HD = 128
score_scale = 1.0 / math.sqrt(HD)
NX, NY, NC, NZ = 4, 8, 2, 8
HALF = 2560
CTX = ("x", "y", "c")
bf16 = jnp.bfloat16
f32 = jnp.float32


def dot_nt(a, b):
    return lax.dot_general(a, b, (((1,), (1,)), ((), ())), preferred_element_type=f32)


def dot_nn(a, b):
    return lax.dot_general(a, b, (((1,), (0,)), ((), ())), preferred_element_type=f32)


def one_hot(origin, columns):
    lane = lax.broadcasted_iota(jnp.int32, (origin.shape[0], columns), 1)
    return jnp.where(lane == origin, 1.0, 0.0).astype(bf16)


def fetch(pairs, sems):
    copies = [
        pltpu.make_async_copy(source, target, sems.at[i])
        for i, (source, target) in enumerate(pairs)
    ]
    for copy in copies:
        copy.start()
    return copies


def bundle_up(*refs):
    inputs, lengths, bundle, held, sems = refs[0:6], refs[6], refs[7], refs[8:14], refs[14]
    copies = fetch(list(zip(inputs, held)), sems)
    for copy in copies:
        copy.wait()
    weight, asked, new_key, new_value, keys, values = [ref[...] for ref in held]
    filled = jnp.broadcast_to(lengths[0].astype(f32), (1, HD))
    lane = lax.broadcasted_iota(jnp.int32, (1, HD), 1)
    live = jnp.where(lane < 64, lengths[1] >> 6, lengths[1] & 63).astype(f32)
    rows = weight.astype(f32)
    small = [ref.astype(f32) for ref in (new_key, new_value, asked)]
    for h in range(NX):
        lanes = slice(h * HD, (h + 1) * HD)
        pieces = [rows[:, lanes], rows[:, 512 + h * HD : 512 + (h + 1) * HD]]
        pieces += [small[0][:, lanes], small[1][:, lanes]]
        pieces += [filled, live]
        for g in range(8):
            start = (h * 8 + g) * HD
            pieces.append(small[2][:, start : start + HD])
        bundle[h, 0:32, :] = jnp.concatenate(pieces, axis=0).astype(bf16)
        bundle[h, 32:160, :] = keys[:, lanes]
        bundle[h, 160:288, :] = values[:, lanes]


def project(*refs):
    blocks, gathered, other, down_in, up_in, out = refs[0:5], *refs[5:10]
    rows, arrived, weight, down, up, sems = refs[10:]
    c = lax.axis_index("c")
    head = lax.axis_index("x")
    up_in = up_in.at[:, :, pl.ds(pl.multiple_of(head * HD, HD), HD)]
    pairs = [(gathered, arrived.at[0]), (other, arrived.at[1])]
    pairs += [(down_in, down), (up_in, up)]
    start = 0
    for block in blocks:
        size = block.shape[0]
        pairs.append((block, rows.at[start : start + size, :]))
        start += size
    copies = fetch(pairs, sems)
    target = lax.broadcasted_iota(jnp.int32, (320, 1), 0)
    x = (target >= 80).astype(jnp.int32)
    x = x + (target >= 160).astype(jnp.int32) + (target >= 240).astype(jnp.int32)
    within = target - 80 * x
    z = (within * 205) >> 11
    pick = one_hot(z * 40 + x * 10 + (within - 10 * z), 320)
    for side in range(NC):
        core = c if side == 0 else 1 - c
        copies[side].wait()
        for y in range(NY):
            block = arrived[side, y * 320 : (y + 1) * 320, :]
            picked = dot_nn(pick, block).astype(bf16)
            for x in range(NX):
                weight[x, y, core] = picked[x * 80 : (x + 1) * 80]
    for copy in copies[2:]:
        copy.wait()
    low = dot_nt(rows[...], down[...]).astype(bf16)
    base = dot_nn(rows[...], weight[...].reshape(2 * HALF, 256))
    out[:, 0:HD] = base[:, 0:HD] + adapter_scale * dot_nn(low[:, 0:32], up[0])
    out[:, HD:] = base[:, HD:] + adapter_scale * dot_nn(low[:, 32:64], up[1])


def attend(*refs):
    inputs, out, held, sems = refs[0:4], refs[4], refs[5:9], refs[9]
    copies = fetch(list(zip(inputs, held)), sems)
    asked, bundle, projected, gain = held
    head = lax.axis_index("x")
    y = lax.axis_index("y")
    c = lax.axis_index("c")
    copies[0].wait()
    queries = asked[...].astype(f32).reshape(NY * NC, NX, 8, HD)
    queries = jnp.stack([queries[:, i] for i in range(NX)], axis=0)
    queries = queries.reshape(512, HD).astype(bf16)

    copies[1].wait()
    cache_keys = bundle[:, 32:160, :].reshape(512, HD)
    cache_values = bundle[:, 160:288, :].reshape(512, HD)
    lane = lax.broadcasted_iota(jnp.int32, (1, HD), 1).astype(f32)
    news = [bundle[i, 16:32, :].astype(f32) for i in range(NX)]
    filled = jnp.concatenate(
        [jnp.where(lane < new[6:7, :], 1.0, 0.0) for new in news], axis=1
    )
    cache_scores = jnp.where(filled > 0.5, dot_nt(queries, cache_keys), masked_score)
    fresh_keys = jnp.concatenate([new[4:5, :] for new in news] * 2, axis=0)
    fresh_values = jnp.concatenate([new[5:6, :] for new in news] * 2, axis=0)
    fresh_keys = fresh_keys.astype(bf16)
    fresh_values = fresh_values.astype(bf16)
    token = lax.broadcasted_iota(jnp.int32, (512, 8), 0) >> 3
    fresh_at = lax.broadcasted_iota(jnp.int32, (1, 8), 1)
    fresh_ok = (fresh_at < NX) & (fresh_at * 16 + y * 2 + c <= token)
    fresh_scores = jnp.where(fresh_ok, dot_nt(queries, fresh_keys), masked_score)

    copies[2].wait()
    copies[3].wait()
    raw_keys = projected[:, 0:HD]
    mean = jnp.mean(raw_keys * raw_keys, axis=-1, keepdims=True)
    new_keys = (raw_keys * lax.rsqrt(mean + norm_epsilon) * gain[...]).astype(bf16)
    new_values = projected[:, HD:].astype(bf16)
    column = lax.broadcasted_iota(jnp.int32, (1, 256), 1)
    shard = (head + NX - (column >> 6)) & 3
    initial = shard * 1024 + (y * 2 + c) * 64 + (column & 63)
    slab_length = news[0][7:8, 0:1] * 64.0 + news[0][7:8, 64:65]
    live = initial.astype(f32) < slab_length
    slab_scores = jnp.where(
        live, dot_nt(queries, new_keys), masked_score
    )

    row_max = jnp.maximum(
        jnp.maximum(
            jnp.max(slab_scores, axis=-1, keepdims=True),
            jnp.max(cache_scores, axis=-1, keepdims=True),
        ),
        jnp.max(fresh_scores, axis=-1, keepdims=True),
    )
    shift = (row_max * score_scale).astype(bf16).astype(f32)

    def weigh(scores, values):
        weights = jnp.exp(scores * score_scale - shift).astype(bf16)
        wide = jnp.concatenate([values, jnp.ones_like(values)], axis=1)
        return dot_nn(weights, wide)

    merged = (
        weigh(slab_scores, new_values)
        + weigh(cache_scores, cache_values)
        + weigh(fresh_scores, fresh_values)
    )
    total = merged[:, HD:]
    high = total.astype(bf16).astype(f32)
    lanes = lax.broadcasted_iota(jnp.int32, (512, HD), 1)
    stats = jnp.where(lanes == 0, shift, jnp.where(lanes == 1, high, total - high))
    target = lax.broadcasted_iota(jnp.int32, (512, 1), 0)
    at = (head + NX - ((target >> 1) & 3)) & 3
    origin = (target & 1) * 256 + at * 64 + (target >> 3)
    spread = dot_nn(
        one_hot(origin, 512), jnp.concatenate([new_keys, new_values], axis=0)
    )
    out[:, 0:HD] = merged[:, 0:HD].astype(bf16)
    out[:, HD : 2 * HD] = stats.astype(bf16)
    out[:, 2 * HD :] = spread.astype(bf16)


def merge(parts, slab, attended):
    heads = []
    rebuilt = []
    for h in range(NX):
        block = parts[h * 128 : (h + 1) * 128, :]
        output = block[:, 0:HD].astype(f32).reshape(16, 8, HD)
        stats = block[:, HD : 2 * HD].astype(f32).reshape(16, 8, HD)
        rebuilt.append(block[:, 2 * HD :])
        shift = stats[:, :, 0:1]
        total = stats[:, :, 1:2] + stats[:, :, 2:3]
        largest = jnp.max(shift, axis=0, keepdims=True)
        factor = jnp.exp(shift - largest)
        merged_total = jnp.sum(factor * total, axis=0)
        merged_output = jnp.sum(factor * output, axis=0)
        heads.append(merged_output / merged_total)
    for h in range(NX):
        for g in range(8):
            start = (h * 8 + g) * HD
            attended[:, start : start + HD] = heads[h][g : g + 1, :].astype(bf16)
    target = lax.broadcasted_iota(jnp.int32, (128, 1), 0)
    origin = (target & 15) * 8 + ((target >> 4) & 3) * 2 + (target >> 6)
    pick = one_hot(origin, 128)
    placed = dot_nn(pick, jnp.concatenate(rebuilt, axis=1)).astype(bf16)
    slab[:, 0:512] = placed[0:64, :]
    slab[:, 512:1024] = placed[64:128, :]


def shift_by(value, axis, step):
    size = lax.axis_size(axis)
    return lax.ppermute(value, axis, [(i, (i + step) % size) for i in range(size)])


def body(
    hidden_slab,
    projection,
    adapter_down,
    adapter_up,
    key_gain,
    cache_keys,
    cache_values,
    fresh_keys,
    fresh_values,
    queries,
    slab_length,
    cache_length,
):
    c = lax.axis_index("c")
    whole = pl.BlockSpec(memory_space=pltpu.VMEM)
    scalars = pl.BlockSpec(memory_space=pltpu.SMEM)
    anywhere = pl.BlockSpec(memory_space=pl.ANY)
    rows = hidden_slab[0]

    inputs = [projection, queries[0], fresh_keys[0], fresh_values[0]]
    inputs += [cache_keys[0], cache_values[0]]
    bundle = pl.pallas_call(
        bundle_up,
        in_specs=[anywhere] * 6 + [scalars],
        out_specs=whole,
        out_shape=jax.ShapeDtypeStruct((NX, 288, HD), bf16),
        scratch_shapes=[pltpu.VMEM(a.shape, bf16) for a in inputs]
        + [pltpu.SemaphoreType.DMA((6,))],
        compiler_params=pltpu.CompilerParams(vmem_limit_bytes=56 * 1024 * 1024),
    )(*inputs, jnp.concatenate([cache_length[0], slab_length]))
    bundle = lax.all_to_all(bundle, "x", 0, 0, tiled=True)

    weight = bundle[:, 0:20].reshape(NX, 2, 10, HD)
    weight = weight.transpose(0, 2, 1, 3).reshape(1, 40, 256)
    gathered = lax.all_to_all(
        jnp.broadcast_to(weight, (NY * NZ, 40, 256)), ("y", "z"), 0, 0, tiled=True
    )
    left = shift_by(rows, "x", 1)
    right = shift_by(rows, "x", -1)
    far_a = shift_by(left[0:32], "x", 1)
    far_b = shift_by(right[32:64], "x", -1)
    asked = bundle[:, 24:32].reshape(1, 32, HD)
    asked = jnp.broadcast_to(asked, (NY * NC, 32, HD))

    gathered, asked, far_a, far_b = lax.optimization_barrier(
        (gathered.reshape(HALF, 256), asked, far_a, far_b)
    )
    other = shift_by(gathered, "c", 1)
    asked = lax.all_to_all(asked, ("y", "c"), 0, 0, tiled=True)
    projected = pl.pallas_call(
        project,
        in_specs=[anywhere] * 9,
        out_specs=whole,
        out_shape=jax.ShapeDtypeStruct((256, 256), f32),
        scratch_shapes=[
            pltpu.VMEM((256, 2 * HALF), bf16),
            pltpu.VMEM((NC, HALF, 256), bf16),
            pltpu.VMEM((NX, NY, NC, 80, 256), bf16),
            pltpu.VMEM((64, 2 * HALF), bf16),
            pltpu.VMEM((2, 32, HD), bf16),
            pltpu.SemaphoreType.DMA((9,)),
        ],
        compiler_params=pltpu.CompilerParams(vmem_limit_bytes=56 * 1024 * 1024),
        cost_estimate=pl.CostEstimate(
            flops=1400000000, bytes_accessed=8000000, transcendentals=0
        ),
    )(
        rows,
        left,
        far_a,
        far_b,
        right,
        gathered,
        other,
        adapter_down[0].T,
        adapter_up[0],
    )

    parts = pl.pallas_call(
        attend,
        in_specs=[anywhere] * 4,
        out_specs=whole,
        out_shape=jax.ShapeDtypeStruct((512, 384), bf16),
        scratch_shapes=[
            pltpu.VMEM((NY * NC, 32, HD), bf16),
            pltpu.VMEM((NX, 288, HD), bf16),
            pltpu.VMEM((256, 256), f32),
            pltpu.VMEM((1, HD), f32),
            pltpu.SemaphoreType.DMA((4,)),
        ],
        compiler_params=pltpu.CompilerParams(vmem_limit_bytes=56 * 1024 * 1024),
    )(asked, bundle, projected, key_gain.reshape(1, HD))
    parts = lax.all_to_all(parts.reshape(64, 8, 384), CTX, 0, 0, tiled=True)
    slab, attended = pl.pallas_call(
        merge,
        out_shape=[
            jax.ShapeDtypeStruct((64, 1024), bf16),
            jax.ShapeDtypeStruct((1, 32 * HD), bf16),
        ],
        compiler_params=pltpu.CompilerParams(vmem_limit_bytes=24 * 1024 * 1024),
    )(parts.reshape(512, 384))
    return slab[None], attended[None]


def solution(mesh):
    fine = Mesh(mesh.devices.reshape(NX, NY, NC, NZ), ("x", "y", "c", "z"))
    return jax.shard_map(
        body,
        mesh=fine,
        in_specs=(
            P("z", CTX, None),
            P(CTX + ("z",), None),
            P("z", None, None),
            P("z", None, None, None),
            P(),
            P("z", CTX, None),
            P("z", CTX, None),
            P("z", CTX, None),
            P("z", CTX, None),
            P("z", CTX, None),
            P("z"),
            P("z", CTX),
        ),
        out_specs=(P("z", CTX, None), P("z", CTX, None)),
        check_vma=False,
    )
```

time: 142 us -> 111 us (0.78); the launches traced: 140 us -> 111 us
  starting transfers between devices: 69.7 us -> 39.7 us
  local copies, waits for them, and re-layouts: 16.6 us -> 2.63 us
  blocking collectives: 23.6 us -> 29.9 us
  Pallas kernels: 7.29 us -> 12.3 us
  waiting for transfers between devices: 20.4 us -> 23.5 us
    ppermute x14 -> x5, starting transfers between devices: 47.5 us -> 17.9 us  [shift_by(): lax.ppermute(value, axis, [(i, (i + step) % size) for i in range(size)])]
    unnamed x46 -> x13, local copies, waits for them, and re-layouts: 12.2 us -> 0.68 us
    all_to_all x0 -> x1, blocking collectives: none -> 10.6 us  [body(): bundle = lax.all_to_all(bundle, 'x', 0, 0, tiled=True)]
    pallas_call x3, Pallas kernels: 6.27 us -> 11.3 us  [the longest x1 5.47 us: body(): pl.pallas_call(project, in_specs=[anywhere] * 9, out_specs=whole, out_sha...]
    all_to_all x1, starting transfers between devices: 10.1 us -> 5.38 us  [body(): asked = lax.all_to_all(asked, ('y', 'c'), 0, 0, tiled=True)]
    all_to_all x1, starting transfers between devices: 12.1 us -> 16.4 us  [body(): lax.all_to_all(jnp.broadcast_to(weight, (NY * NZ, 40, 256)), ('y', 'z'),...]
    all_to_all x1, blocking collectives: 23.6 us -> 19.4 us  [body(): parts = lax.all_to_all(parts.reshape(64, 8, 384), CTX, 0, 0, tiled=True)]
    ppermute x14 -> x5, waiting for transfers between devices: 15.6 us -> 18 us  [shift_by(): lax.ppermute(value, axis, [(i, (i + step) % size) for i in range(size)])]
  transfers between devices with their start and end apart: 16 -> 7, of which waited for: 6 -> 5; matrix products, arithmetic and copies ran while one was open for 2% -> 0% of each run, Pallas kernels for 0% -> 5%
where the time goes in v4:
time: 111 us
  starting transfers between devices  39.7 us (36%)
  blocking collectives  29.9 us (27%)
  waiting for transfers between devices  23.5 us (21%)
  Pallas kernels  12.3 us (11%)
  local copies, waits for them, and re-layouts  2.63 us (2%)
  between operations  2.1 us (2%)
    all_to_all x1, blocking collectives, body(): parts = lax.all_to_all(parts.reshape(64, 8, 384), CTX, 0, 0, tiled=True)  19.4 us
    ppermute x5, waiting for transfers between devices, shift_by(): lax.ppermute(value, axis, [(i, (i + step) % size) for i in range(size)])  18 us
    ppermute x5, starting transfers between devices, shift_by(): lax.ppermute(value, axis, [(i, (i + step) % size) for i in range(size)])  17.9 us
    all_to_all x1, starting transfers between devices, body(): lax.all_to_all(jnp.broadcast_to(weight, (NY * NZ, 40, 256)), ('y', 'z'),...  16.4 us
    all_to_all x1, blocking collectives, body(): bundle = lax.all_to_all(bundle, 'x', 0, 0, tiled=True)  10.6 us
    pallas_call x1, Pallas kernels, body(): pl.pallas_call(project, in_specs=[anywhere] * 9, out_specs=whole, out_sha...  5.47 us
    all_to_all x1, starting transfers between devices, body(): asked = lax.all_to_all(asked, ('y', 'c'), 0, 0, tiled=True)  5.38 us
    all_to_all x1, waiting for transfers between devices, body(): asked = lax.all_to_all(asked, ('y', 'c'), 0, 0, tiled=True)  3.65 us
  transfers between devices with their start and end apart: 7, of which 5 were waited for; matrix products, arithmetic and copies ran while one was open for 0% of the time, Pallas kernels for 5%

profile of v4, /device:TPU:1, one launch (start us, length us, event | category | flops | bytes accessed | tf_op | source)
XLA Modules:
  0.0 110.7 jit_solution(7281167520834038652)
XLA Ops:
  1.9 0.6 pad_add_fusion.refs_6_
  2.5 2.5 %shard_map.131 = bf16[4,288,128]{2,1,0:T(8,128)(2,1)} custom-call(bf16[10,1024]{1,0:T(8,128)(2,1)} %refs_0_.1, bf16[1,4096]{1,0:T(2,128)(2,1)} %bitcast.39, bf16[1,512]{1,0:T(2,128)(2,1)} %bitcast.40, bf16[1,512]{1,0:T(2,128)(2,1)} %bitcast.41, bf16[128,512]{1,0:T(8,128)(2,1)} %bitcast.33, bf16[128,512]{1,0:T(8,128)(2,1)} %bitcast.34, s32[2]{0:T(128)} %pad_add_fusion.refs_6_), custom_call_target="tpu_custom_call" | custom-call | tf_op jit(solution)/shard_map/pallas_call | solution.py:238
  5.0 10.6 %all_to_all.20.refs_1_ = bf16[4,288,128]{2,1,0:T(8,128)(2,1)S(1)} all-to-all(bf16[4,288,128]{2,1,0:T(8,128)(2,1)} %shard_map.131), channel_id=1, replica_groups=mesh['x'=4,'y'=8,'c'=2,'z'=8] {'x'}, dimensions={0} | all-to-all | bytes 589824 | tf_op jit(solution)/shard_map/all_to_all | solution.py:247
  15.6 0.0 copy-start.3
  15.6 1.2 %broadcast_in_dim.21 = bf16[64,40,256]{2,1,0:T(8,128)(2,1)} broadcast(bf16[40,256]{1,0:T(8,128)(2,1)S(1)} %bitcast.37), dimensions={1,2} | broadcast | bytes 1331200 | tf_op jit(solution)/shard_map/broadcast_in_dim | solution.py:252
  16.8 16.4 %all-to-all-start.1 = ((bf16[64,40,256]{2,1,0:T(8,128)(2,1)}), bf16[64,40,256]{2,1,0:T(8,128)(2,1)S(1)}, u32[]{:S(2)}, u32[]{:S(2)}) async-start(bf16[64,40,256]{2,1,0:T(8,128)(2,1)} %broadcast_in_dim.21), calls=%async_computation.1 | async-start | bytes 2621440 | tf_op jit(solution)/shard_map/all_to_all | solution.py:251
  33.2 2.8 %collective-permute-start.2 = (bf16[64,5120]{1,0:T(8,128)(2,1)}, bf16[64,5120]{1,0:T(8,128)(2,1)S(1)}, u32[]{:S(2)}, u32[]{:S(2)}) collective-permute-start(bf16[64,5120]{1,0:T(8,128)(2,1)} %bitcast.10.refs_0_), channel_id=1, source_target_pairs={{0,384},{128,0},{256,128},{384,256},{1,385},{129,1},{257,129},{385... | collective-permute-start | bytes 1966088 | tf_op jit(solution)/shard_map/ppermute | solution.py:213
  36.0 2.5 %collective-permute-start = (bf16[64,5120]{1,0:T(8,128)(2,1)}, bf16[64,5120]{1,0:T(8,128)(2,1)S(1)}, u32[]{:S(2)}, u32[]{:S(2)}) collective-permute-start(bf16[64,5120]{1,0:T(8,128)(2,1)} %bitcast.10.refs_0_), channel_id=1, source_target_pairs={{0,128},{128,256},{256,384},{384,0},{1,129},{129,257},{257,385},{3... | collective-permute-start | bytes 1966088 | tf_op jit(solution)/shard_map/ppermute | solution.py:213
  38.5 10.6 %collective-permute-done.2.refs_4_ = bf16[64,5120]{1,0:T(8,128)(2,1)S(1)} collective-permute-done((bf16[64,5120]{1,0:T(8,128)(2,1)}, bf16[64,5120]{1,0:T(8,128)(2,1)S(1)}, u32[]{:S(2)}, u32[]{:S(2)}) %collective-permute-start.2) | collective-permute-done | bytes 655392 | tf_op jit(solution)/shard_map/ppermute | solution.py:213
  49.1 0.0 copy-start.1
  49.1 4.0 %collective-permute-start.3 = (bf16[32,5120]{1,0:T(8,128)(2,1)S(1)}, bf16[32,5120]{1,0:T(8,128)(2,1)S(1)}, u32[]{:S(2)}, u32[]{:S(2)}) collective-permute-start(bf16[32,5120]{1,0:T(8,128)(2,1)S(1)} %slice.19), channel_id=1, source_target_pairs={{0,384},{128,0},{256,128},{384,256},{1,385},{129,1},{257,129},{385... | collective-permute-start | bytes 983048 | tf_op jit(solution)/shard_map/ppermute | solution.py:213
  53.1 0.0 collective-permute-done.refs_1_
  53.2 0.0 copy-start.2
  53.2 1.9 %collective-permute-start.1 = (bf16[32,5120]{1,0:T(8,128)(2,1)S(1)}, bf16[32,5120]{1,0:T(8,128)(2,1)}, u32[]{:S(2)}, u32[]{:S(2)}) collective-permute-start(bf16[32,5120]{1,0:T(8,128)(2,1)S(1)} %slice.18), channel_id=1, source_target_pairs={{0,128},{128,256},{256,384},{384,0},{1,129},{129,257},{257,385},{3... | collective-permute-start | bytes 983048 | tf_op jit(solution)/shard_map/ppermute | solution.py:213
  55.1 0.0 copy-done.3
  55.1 2.1 %collective-permute-done.3.refs_3_ = bf16[32,5120]{1,0:T(8,128)(2,1)S(1)} collective-permute-done((bf16[32,5120]{1,0:T(8,128)(2,1)S(1)}, bf16[32,5120]{1,0:T(8,128)(2,1)S(1)}, u32[]{:S(2)}, u32[]{:S(2)}) %collective-permute-start.3) | collective-permute-done | bytes 327712 | tf_op jit(solution)/shard_map/ppermute | solution.py:213
  57.2 0.0 copy-start.5
  57.2 5.3 %collective-permute-done.1.refs_2_ = bf16[32,5120]{1,0:T(8,128)(2,1)} collective-permute-done((bf16[32,5120]{1,0:T(8,128)(2,1)S(1)}, bf16[32,5120]{1,0:T(8,128)(2,1)}, u32[]{:S(2)}, u32[]{:S(2)}) %collective-permute-start.1) | collective-permute-done | bytes 327712 | tf_op jit(solution)/shard_map/ppermute | solution.py:213
  62.5 1.9 %all-to-all-done.1 = bf16[64,40,256]{2,1,0:T(8,128)(2,1)S(1)} async-done(((bf16[64,40,256]{2,1,0:T(8,128)(2,1)}), bf16[64,40,256]{2,1,0:T(8,128)(2,1)S(1)}, u32[]{:S(2)}, u32[]{:S(2)}) %all-to-all-start.1) | async-done | bytes 1310752 | tf_op jit(solution)/shard_map/all_to_all | solution.py:251
  64.4 0.0 copy-start
  64.4 0.7 broadcast_in_dim.23
  65.1 6.7 %collective-permute-start.4 = (bf16[2560,256]{1,0:T(8,128)(2,1)S(1)}, bf16[2560,256]{1,0:T(8,128)(2,1)}, u32[]{:S(2)}, u32[]{:S(2)}) collective-permute-start(bf16[2560,256]{1,0:T(8,128)(2,1)S(1)} %bitcast.29), channel_id=1, source_target_pairs={{0,8},{8,0},{1,9},{9,1},{2,10},{10,2},{3,11},{11,3},{4,12},{12,4},... | collective-permute-start | bytes 3932168 | tf_op jit(solution)/shard_map/ppermute | solution.py:213
  71.8 5.4 %all-to-all-start.2 = ((bf16[16,32,128]{2,1,0:T(8,128)(2,1)}), bf16[16,32,128]{2,1,0:T(8,128)(2,1)S(1)}, u32[]{:S(2)}, u32[]{:S(2)}) async-start(bf16[16,32,128]{2,1,0:T(8,128)(2,1)} %broadcast_in_dim.23), calls=%async_computation.2 | async-start | bytes 262144 | tf_op jit(solution)/shard_map/all_to_all | solution.py:265
  77.2 0.0 collective-permute-done.4.refs_6_
  77.2 0.0 copy-done.1
  77.2 0.0 copy-done.2
  77.2 0.0 copy-done.5
  77.2 0.0 copy-done
  77.2 5.5 %shard_map.132.refs_2_ = f32[256,256]{1,0:T(8,128)} custom-call(bf16[64,5120]{1,0:T(8,128)(2,1)} %bitcast.10.refs_0_, bf16[64,5120]{1,0:T(8,128)(2,1)} %copy-done.2, bf16[32,5120]{1,0:T(8,128)(2,1)} %collective-permute-done.1.refs_2_, bf16[32,5120]{1,0:T(8,128)(2,1)} %copy-done.5, bf16[64,5120]{1,0:T(8,128)(2,1)} %copy-done.1, bf16[2560,256]{1,0:T(8,128)(2,1)} %bitcast.30, ...), custom_call_target="tpu_custom_call" | custom-call | flops 1400000000 | bytes 8000000 | tf_op jit(solution)/shard_map/pallas_call | solution.py:266
  82.7 3.6 %all-to-all-done.2.refs_0_ = bf16[16,32,128]{2,1,0:T(8,128)(2,1)S(1)} async-done(((bf16[16,32,128]{2,1,0:T(8,128)(2,1)}), bf16[16,32,128]{2,1,0:T(8,128)(2,1)S(1)}, u32[]{:S(2)}, u32[]{:S(2)}) %all-to-all-start.2) | async-done | bytes 131104 | tf_op jit(solution)/shard_map/all_to_all | solution.py:265
  86.4 0.0 copy-start.4
  86.4 0.7 copy-done.4
  87.0 3.3 %shard_map.133 = bf16[512,384]{1,0:T(8,128)(2,1)} custom-call(bf16[16,32,128]{2,1,0:T(8,128)(2,1)} %copy-done.4, bf16[4,288,128]{2,1,0:T(8,128)(2,1)} %copy-done.3, f32[256,256]{1,0:T(8,128)} %shard_map.132.refs_2_, f32[1,128]{1,0:T(1,128)} %bitcast.42), custom_call_target="tpu_custom_call" | custom-call | tf_op jit(solution)/shard_map/pallas_call | solution.py:295
  90.3 19.4 %all_to_all.21 = bf16[64,8,384]{2,1,0:T(8,128)(2,1)S(1)} all-to-all(bf16[64,8,384]{2,1,0:T(8,128)(2,1)} %bitcast.31), channel_id=1, replica_groups=mesh['x'=4,'y'=8,'c'=2,'z'=8] {'x','y','c'}, dimensions={0} | all-to-all | bytes 786432 | tf_op jit(solution)/shard_map/all_to_all | solution.py:309
  109.7 1.0 shard_map.134
  (7 shorter events, 0.1 us)
Async XLA Ops:
  15.6 39.6 %copy-start.3 = (bf16[4,288,128]{2,1,0:T(8,128)(2,1)}, bf16[4,288,128]{2,1,0:T(8,128)(2,1)S(1)}, u32[]{:S(2)}) copy-start(bf16[4,288,128]{2,1,0:T(8,128)(2,1)S(1)} %all_to_all.20.refs_1_) | copy-start | bytes 884740
  16.8 47.6 %all-to-all-start.1 = ((bf16[64,40,256]{2,1,0:T(8,128)(2,1)}), bf16[64,40,256]{2,1,0:T(8,128)(2,1)S(1)}, u32[]{:S(2)}, u32[]{:S(2)}) async-start(bf16[64,40,256]{2,1,0:T(8,128)(2,1)} %broadcast_in_dim.21), calls=%async_computation.1 | async-start | bytes 2621440 | tf_op jit(solution)/shard_map/all_to_all | solution.py:251
  33.2 15.9 %collective-permute-start.2 = (bf16[64,5120]{1,0:T(8,128)(2,1)}, bf16[64,5120]{1,0:T(8,128)(2,1)S(1)}, u32[]{:S(2)}, u32[]{:S(2)}) collective-permute-start(bf16[64,5120]{1,0:T(8,128)(2,1)} %bitcast.10.refs_0_), channel_id=1, source_target_pairs={{0,384},{128,0},{256,128},{384,256},{1,385},{129,1},{257,129},{385... | collective-permute-start | bytes 1966088 | tf_op jit(solution)/shard_map/ppermute | solution.py:213
  36.0 17.1 %collective-permute-start = (bf16[64,5120]{1,0:T(8,128)(2,1)}, bf16[64,5120]{1,0:T(8,128)(2,1)S(1)}, u32[]{:S(2)}, u32[]{:S(2)}) collective-permute-start(bf16[64,5120]{1,0:T(8,128)(2,1)} %bitcast.10.refs_0_), channel_id=1, source_target_pairs={{0,128},{128,256},{256,384},{384,0},{1,129},{129,257},{257,385},{3... | collective-permute-start | bytes 1966088 | tf_op jit(solution)/shard_map/ppermute | solution.py:213
  49.1 28.1 %copy-start.1 = (bf16[64,5120]{1,0:T(8,128)(2,1)}, bf16[64,5120]{1,0:T(8,128)(2,1)S(1)}, u32[]{:S(2)}) copy-start(bf16[64,5120]{1,0:T(8,128)(2,1)S(1)} %collective-permute-done.2.refs_4_) | copy-start | bytes 1966084
  49.1 8.1 %collective-permute-start.3 = (bf16[32,5120]{1,0:T(8,128)(2,1)S(1)}, bf16[32,5120]{1,0:T(8,128)(2,1)S(1)}, u32[]{:S(2)}, u32[]{:S(2)}) collective-permute-start(bf16[32,5120]{1,0:T(8,128)(2,1)S(1)} %slice.19), channel_id=1, source_target_pairs={{0,384},{128,0},{256,128},{384,256},{1,385},{129,1},{257,129},{385... | collective-permute-start | bytes 983048 | tf_op jit(solution)/shard_map/ppermute | solution.py:213
  53.2 24.1 %copy-start.2 = (bf16[64,5120]{1,0:T(8,128)(2,1)}, bf16[64,5120]{1,0:T(8,128)(2,1)S(1)}, u32[]{:S(2)}) copy-start(bf16[64,5120]{1,0:T(8,128)(2,1)S(1)} %collective-permute-done.refs_1_) | copy-start | bytes 1966084
  53.2 9.3 %collective-permute-start.1 = (bf16[32,5120]{1,0:T(8,128)(2,1)S(1)}, bf16[32,5120]{1,0:T(8,128)(2,1)}, u32[]{:S(2)}, u32[]{:S(2)}) collective-permute-start(bf16[32,5120]{1,0:T(8,128)(2,1)S(1)} %slice.18), channel_id=1, source_target_pairs={{0,128},{128,256},{256,384},{384,0},{1,129},{129,257},{257,385},{3... | collective-permute-start | bytes 983048 | tf_op jit(solution)/shard_map/ppermute | solution.py:213
  57.2 20.0 %copy-start.5 = (bf16[32,5120]{1,0:T(8,128)(2,1)}, bf16[32,5120]{1,0:T(8,128)(2,1)S(1)}, u32[]{:S(2)}) copy-start(bf16[32,5120]{1,0:T(8,128)(2,1)S(1)} %collective-permute-done.3.refs_3_) | copy-start | bytes 983044
  64.4 12.8 %copy-start = (bf16[64,40,256]{2,1,0:T(8,128)(2,1)}, bf16[64,40,256]{2,1,0:T(8,128)(2,1)S(1)}, u32[]{:S(2)}) copy-start(bf16[64,40,256]{2,1,0:T(8,128)(2,1)S(1)} %all-to-all-done.1) | copy-start | bytes 3932164
  65.1 12.1 %collective-permute-start.4 = (bf16[2560,256]{1,0:T(8,128)(2,1)S(1)}, bf16[2560,256]{1,0:T(8,128)(2,1)}, u32[]{:S(2)}, u32[]{:S(2)}) collective-permute-start(bf16[2560,256]{1,0:T(8,128)(2,1)S(1)} %bitcast.29), channel_id=1, source_target_pairs={{0,8},{8,0},{1,9},{9,1},{2,10},{10,2},{3,11},{11,3},{4,12},{12,4},... | collective-permute-start | bytes 3932168 | tf_op jit(solution)/shard_map/ppermute | solution.py:213
  71.8 14.5 %all-to-all-start.2 = ((bf16[16,32,128]{2,1,0:T(8,128)(2,1)}), bf16[16,32,128]{2,1,0:T(8,128)(2,1)S(1)}, u32[]{:S(2)}, u32[]{:S(2)}) async-start(bf16[16,32,128]{2,1,0:T(8,128)(2,1)} %broadcast_in_dim.23), calls=%async_computation.2 | async-start | bytes 262144 | tf_op jit(solution)/shard_map/all_to_all | solution.py:265
  86.4 0.7 copy-start.4

commit v5 on v4

--- a/solution.py
+++ b/solution.py
@@ -43,14 +43,16 @@
 
 
 def bundle_up(*refs):
-    inputs, lengths, bundle, held, sems = refs[0:6], refs[6], refs[7], refs[8:14], refs[14]
+    inputs, bundle, held, sems = refs[0:8], refs[8], refs[9:17], refs[17]
     copies = fetch(list(zip(inputs, held)), sems)
     for copy in copies:
         copy.wait()
-    weight, asked, new_key, new_value, keys, values = [ref[...] for ref in held]
-    filled = jnp.broadcast_to(lengths[0].astype(f32), (1, HD))
+    weight, asked, new_key, new_value, keys, values, count, length = [
+        ref[...] for ref in held
+    ]
+    filled = jnp.broadcast_to(count.astype(f32), (1, HD))
     lane = lax.broadcasted_iota(jnp.int32, (1, HD), 1)
-    live = jnp.where(lane < 64, lengths[1] >> 6, lengths[1] & 63).astype(f32)
+    live = jnp.where(lane < 64, length >> 6, length & 63).astype(f32)
     rows = weight.astype(f32)
     small = [ref.astype(f32) for ref in (new_key, new_value, asked)]
     for h in range(NX):
@@ -66,46 +68,71 @@
         bundle[h, 160:288, :] = values[:, lanes]
 
 
+def fan_out(bundle, weight, asked, held, sems):
+    copy = pltpu.make_async_copy(bundle.at[:, 0:32, :], held, sems.at[0])
+    copy.start()
+    copy.wait()
+    rows = [held[x].astype(f32) for x in range(NX)]
+    block = jnp.concatenate([jnp.concatenate([a[0:10], a[10:20]], axis=1) for a in rows])
+    block = block.astype(bf16)
+    for i in range(NY * NZ):
+        weight[i] = block
+    block = jnp.concatenate([a[24:32] for a in rows], axis=0).astype(bf16)
+    for i in range(NY * NC):
+        asked[i] = block
+
+
 def project(*refs):
-    blocks, gathered, other, down_in, up_in, out = refs[0:5], *refs[5:10]
-    rows, arrived, weight, down, up, sems = refs[10:]
+    blocks, gathered, other, down_in, up_in, gain_in, out = refs[0:5], *refs[5:11]
+    rows, arrived, weight, down, up, gain, sems = refs[11:]
     c = lax.axis_index("c")
     head = lax.axis_index("x")
     up_in = up_in.at[:, :, pl.ds(pl.multiple_of(head * HD, HD), HD)]
     pairs = [(gathered, arrived.at[0]), (other, arrived.at[1])]
-    pairs += [(down_in, down), (up_in, up)]
+    pairs += [(down_in, down), (up_in, up), (gain_in, gain)]
     start = 0
     for block in blocks:
         size = block.shape[0]
         pairs.append((block, rows.at[start : start + size, :]))
         start += size
     copies = fetch(pairs, sems)
-    target = lax.broadcasted_iota(jnp.int32, (320, 1), 0)
-    x = (target >= 80).astype(jnp.int32)
-    x = x + (target >= 160).astype(jnp.int32) + (target >= 240).astype(jnp.int32)
-    within = target - 80 * x
+    target = lax.broadcasted_iota(jnp.int32, (160, 1), 0)
+    x = (target >= 40).astype(jnp.int32)
+    x = x + (target >= 80).astype(jnp.int32) + (target >= 120).astype(jnp.int32)
+    within = target - 40 * x
     z = (within * 205) >> 11
-    pick = one_hot(z * 40 + x * 10 + (within - 10 * z), 320)
+    pick = one_hot(z * 40 + x * 10 + (within - 10 * z), 160)
+    target = lax.broadcasted_iota(jnp.int32, (512, 1), 0)
+    at = (head + NX - ((target >> 1) & 3)) & 3
+    spread = one_hot((target & 1) * 256 + at * 64 + (target >> 3), 512)
     for side in range(NC):
         core = c if side == 0 else 1 - c
         copies[side].wait()
         for y in range(NY):
-            block = arrived[side, y * 320 : (y + 1) * 320, :]
-            picked = dot_nn(pick, block).astype(bf16)
+            picked = []
+            for half in range(2):
+                start = y * 320 + half * 160
+                picked.append(dot_nn(pick, arrived[side, start : start + 160, :]))
             for x in range(NX):
-                weight[x, y, core] = picked[x * 80 : (x + 1) * 80]
+                own = [a[x * 40 : (x + 1) * 40] for a in picked]
+                weight[x, y, core] = jnp.concatenate(own, axis=0).astype(bf16)
     for copy in copies[2:]:
         copy.wait()
     low = dot_nt(rows[...], down[...]).astype(bf16)
     base = dot_nn(rows[...], weight[...].reshape(2 * HALF, 256))
-    out[:, 0:HD] = base[:, 0:HD] + adapter_scale * dot_nn(low[:, 0:32], up[0])
-    out[:, HD:] = base[:, HD:] + adapter_scale * dot_nn(low[:, 32:64], up[1])
+    raw_keys = base[:, 0:HD] + adapter_scale * dot_nn(low[:, 0:32], up[0])
+    new_values = base[:, HD:] + adapter_scale * dot_nn(low[:, 32:64], up[1])
+    mean = jnp.mean(raw_keys * raw_keys, axis=-1, keepdims=True)
+    new_keys = raw_keys * lax.rsqrt(mean + norm_epsilon) * gain[...]
+    rebuilt = jnp.concatenate([new_keys, new_values], axis=0).astype(bf16)
+    out[:, 0:HD] = rebuilt
+    out[:, HD:] = dot_nn(spread, rebuilt).astype(bf16)
 
 
 def attend(*refs):
-    inputs, out, held, sems = refs[0:4], refs[4], refs[5:9], refs[9]
+    inputs, out, held, sems = refs[0:3], refs[3], refs[4:7], refs[7]
     copies = fetch(list(zip(inputs, held)), sems)
-    asked, bundle, projected, gain = held
+    asked, bundle, rebuilt = held
     head = lax.axis_index("x")
     y = lax.axis_index("y")
     c = lax.axis_index("c")
@@ -133,11 +160,8 @@
     fresh_scores = jnp.where(fresh_ok, dot_nt(queries, fresh_keys), masked_score)
 
     copies[2].wait()
-    copies[3].wait()
-    raw_keys = projected[:, 0:HD]
-    mean = jnp.mean(raw_keys * raw_keys, axis=-1, keepdims=True)
-    new_keys = (raw_keys * lax.rsqrt(mean + norm_epsilon) * gain[...]).astype(bf16)
-    new_values = projected[:, HD:].astype(bf16)
+    new_keys = rebuilt[0:256, 0:HD]
+    new_values = rebuilt[256:512, 0:HD]
     column = lax.broadcasted_iota(jnp.int32, (1, 256), 1)
     shard = (head + NX - (column >> 6)) & 3
     initial = shard * 1024 + (y * 2 + c) * 64 + (column & 63)
@@ -170,15 +194,9 @@
     high = total.astype(bf16).astype(f32)
     lanes = lax.broadcasted_iota(jnp.int32, (512, HD), 1)
     stats = jnp.where(lanes == 0, shift, jnp.where(lanes == 1, high, total - high))
-    target = lax.broadcasted_iota(jnp.int32, (512, 1), 0)
-    at = (head + NX - ((target >> 1) & 3)) & 3
-    origin = (target & 1) * 256 + at * 64 + (target >> 3)
-    spread = dot_nn(
-        one_hot(origin, 512), jnp.concatenate([new_keys, new_values], axis=0)
-    )
     out[:, 0:HD] = merged[:, 0:HD].astype(bf16)
     out[:, HD : 2 * HD] = stats.astype(bf16)
-    out[:, 2 * HD :] = spread.astype(bf16)
+    out[:, 2 * HD :] = rebuilt[:, HD:]
 
 
 def merge(parts, slab, attended):
@@ -229,52 +247,61 @@
 ):
     c = lax.axis_index("c")
     whole = pl.BlockSpec(memory_space=pltpu.VMEM)
-    scalars = pl.BlockSpec(memory_space=pltpu.SMEM)
     anywhere = pl.BlockSpec(memory_space=pl.ANY)
     rows = hidden_slab[0]
 
     inputs = [projection, queries[0], fresh_keys[0], fresh_values[0]]
     inputs += [cache_keys[0], cache_values[0]]
+    inputs += [cache_length, slab_length.reshape(1, 1)]
     bundle = pl.pallas_call(
         bundle_up,
-        in_specs=[anywhere] * 6 + [scalars],
+        in_specs=[anywhere] * 8,
         out_specs=whole,
         out_shape=jax.ShapeDtypeStruct((NX, 288, HD), bf16),
-        scratch_shapes=[pltpu.VMEM(a.shape, bf16) for a in inputs]
-        + [pltpu.SemaphoreType.DMA((6,))],
+        scratch_shapes=[pltpu.VMEM(a.shape, a.dtype) for a in inputs]
+        + [pltpu.SemaphoreType.DMA((8,))],
         compiler_params=pltpu.CompilerParams(vmem_limit_bytes=56 * 1024 * 1024),
-    )(*inputs, jnp.concatenate([cache_length[0], slab_length]))
+    )(*inputs)
     bundle = lax.all_to_all(bundle, "x", 0, 0, tiled=True)
 
-    weight = bundle[:, 0:20].reshape(NX, 2, 10, HD)
-    weight = weight.transpose(0, 2, 1, 3).reshape(1, 40, 256)
-    gathered = lax.all_to_all(
-        jnp.broadcast_to(weight, (NY * NZ, 40, 256)), ("y", "z"), 0, 0, tiled=True
-    )
+    weight, asked = pl.pallas_call(
+        fan_out,
+        in_specs=[anywhere],
+        out_specs=[whole] * 2,
+        out_shape=[
+            jax.ShapeDtypeStruct((NY * NZ, 40, 256), bf16),
+            jax.ShapeDtypeStruct((NY * NC, 32, HD), bf16),
+        ],
+        scratch_shapes=[
+            pltpu.VMEM((NX, 32, HD), bf16),
+            pltpu.SemaphoreType.DMA((1,)),
+        ],
+        compiler_params=pltpu.CompilerParams(vmem_limit_bytes=8 * 1024 * 1024),
+    )(bundle)
+    gathered = lax.all_to_all(weight, ("y", "z"), 0, 0, tiled=True)
     left = shift_by(rows, "x", 1)
     right = shift_by(rows, "x", -1)
     far_a = shift_by(left[0:32], "x", 1)
     far_b = shift_by(right[32:64], "x", -1)
-    asked = bundle[:, 24:32].reshape(1, 32, HD)
-    asked = jnp.broadcast_to(asked, (NY * NC, 32, HD))
 
     gathered, asked, far_a, far_b = lax.optimization_barrier(
         (gathered.reshape(HALF, 256), asked, far_a, far_b)
     )
     other = shift_by(gathered, "c", 1)
     asked = lax.all_to_all(asked, ("y", "c"), 0, 0, tiled=True)
-    projected = pl.pallas_call(
+    rebuilt = pl.pallas_call(
         project,
-        in_specs=[anywhere] * 9,
+        in_specs=[anywhere] * 10,
         out_specs=whole,
-        out_shape=jax.ShapeDtypeStruct((256, 256), f32),
+        out_shape=jax.ShapeDtypeStruct((512, 256), bf16),
         scratch_shapes=[
             pltpu.VMEM((256, 2 * HALF), bf16),
             pltpu.VMEM((NC, HALF, 256), bf16),
             pltpu.VMEM((NX, NY, NC, 80, 256), bf16),
             pltpu.VMEM((64, 2 * HALF), bf16),
             pltpu.VMEM((2, 32, HD), bf16),
-            pltpu.SemaphoreType.DMA((9,)),
+            pltpu.VMEM((1, HD), f32),
+            pltpu.SemaphoreType.DMA((10,)),
         ],
         compiler_params=pltpu.CompilerParams(vmem_limit_bytes=56 * 1024 * 1024),
         cost_estimate=pl.CostEstimate(
@@ -290,22 +317,22 @@
         other,
         adapter_down[0].T,
         adapter_up[0],
+        key_gain.reshape(1, HD),
     )
 
     parts = pl.pallas_call(
         attend,
-        in_specs=[anywhere] * 4,
+        in_specs=[anywhere] * 3,
         out_specs=whole,
         out_shape=jax.ShapeDtypeStruct((512, 384), bf16),
         scratch_shapes=[
             pltpu.VMEM((NY * NC, 32, HD), bf16),
             pltpu.VMEM((NX, 288, HD), bf16),
-            pltpu.VMEM((256, 256), f32),
-            pltpu.VMEM((1, HD), f32),
-            pltpu.SemaphoreType.DMA((4,)),
-        ],
-        compiler_params=pltpu.CompilerParams(vmem_limit_bytes=56 * 1024 * 1024),
-    )(asked, bundle, projected, key_gain.reshape(1, HD))
+            pltpu.VMEM((512, 256), bf16),
+            pltpu.SemaphoreType.DMA((3,)),
+        ],
+        compiler_params=pltpu.CompilerParams(vmem_limit_bytes=16 * 1024 * 1024),
+    )(asked, bundle, rebuilt)
     parts = lax.all_to_all(parts.reshape(64, 8, 384), CTX, 0, 0, tiled=True)
     slab, attended = pl.pallas_call(
         merge,
@@ -313,7 +340,7 @@
             jax.ShapeDtypeStruct((64, 1024), bf16),
             jax.ShapeDtypeStruct((1, 32 * HD), bf16),
         ],
-        compiler_params=pltpu.CompilerParams(vmem_limit_bytes=24 * 1024 * 1024),
+        compiler_params=pltpu.CompilerParams(vmem_limit_bytes=16 * 1024 * 1024),
     )(parts.reshape(512, 384))
     return slab[None], attended[None]
 

time: 111 us -> 108 us (0.973)
  local copies, waits for them, and re-layouts: 2.63 us -> 1.01 us
    broadcast_in_dim x3 -> x0, local copies, waits for them, and re-layouts: 1.88 us -> none  [the longest x1 1.16 us: body(): jnp.broadcast_to(weight, (NY * NZ, 40, 256))]
    pallas_call x3 -> x4, Pallas kernels: 11.3 us -> 10.1 us  [the longest x1 5.46 us: body(): pl.pallas_call(project, in_specs=[anywhere] * 10, out_specs=whole, out_sh...]
where the time goes in v5:
time: 108 us; the launch traced here: 107 us
  starting transfers between devices  39.7 us (37%)
  blocking collectives  29.7 us (28%)
  waiting for transfers between devices  23.5 us (22%)
  Pallas kernels  11.2 us (10%)
  between operations  2.07 us (2%)
    all_to_all x1, blocking collectives, body(): parts = lax.all_to_all(parts.reshape(64, 8, 384), CTX, 0, 0, tiled=True)  19.2 us
    ppermute x5, waiting for transfers between devices, shift_by(): lax.ppermute(value, axis, [(i, (i + step) % size) for i in range(size)])  18 us
    ppermute x5, starting transfers between devices, shift_by(): lax.ppermute(value, axis, [(i, (i + step) % size) for i in range(size)])  17.9 us
    all_to_all x1, starting transfers between devices, body(): gathered = lax.all_to_all(weight, ('y', 'z'), 0, 0, tiled=True)  16.4 us
    all_to_all x1, blocking collectives, body(): bundle = lax.all_to_all(bundle, 'x', 0, 0, tiled=True)  10.6 us
    pallas_call x1, Pallas kernels, body(): pl.pallas_call(project, in_specs=[anywhere] * 10, out_specs=whole, out_sh...  5.46 us
    all_to_all x1, starting transfers between devices, body(): asked = lax.all_to_all(asked, ('y', 'c'), 0, 0, tiled=True)  5.38 us
    all_to_all x1, waiting for transfers between devices, body(): asked = lax.all_to_all(asked, ('y', 'c'), 0, 0, tiled=True)  3.65 us
  transfers between devices with their start and end apart: 7, of which 5 were waited for; matrix products, arithmetic and copies ran while one was open for 0% of the time, Pallas kernels for 5%

profile of v5, /device:TPU:1, one launch (start us, length us, event | category | flops | bytes accessed | tf_op | source)
XLA Modules:
  0.0 107.2 jit_solution(9890625382367103502)
XLA Ops:
  1.9 1.9 %shard_map.131 = bf16[4,288,128]{2,1,0:T(8,128)(2,1)} custom-call(bf16[10,1024]{1,0:T(8,128)(2,1)} %refs_0_.1, bf16[1,4096]{1,0:T(2,128)(2,1)} %bitcast.26, bf16[1,512]{1,0:T(2,128)(2,1)} %bitcast.27, bf16[1,512]{1,0:T(2,128)(2,1)} %bitcast.28, bf16[128,512]{1,0:T(8,128)(2,1)} %bitcast.23, bf16[128,512]{1,0:T(8,128)(2,1)} %bitcast.24, ...), custom_call_target="tpu_custom_call" | custom-call | tf_op jit(solution)/shard_map/pallas_call | solution.py:256
  3.8 10.6 %all_to_all.20.bundle.refs_1_ = bf16[4,288,128]{2,1,0:T(8,128)(2,1)S(1)} all-to-all(bf16[4,288,128]{2,1,0:T(8,128)(2,1)} %shard_map.131), channel_id=1, replica_groups=mesh['x'=4,'y'=8,'c'=2,'z'=8] {'x'}, dimensions={0} | all-to-all | bytes 589824 | tf_op jit(solution)/shard_map/all_to_all | solution.py:265
  14.4 1.2 %shard_map.132 = (bf16[64,40,256]{2,1,0:T(8,128)(2,1)}, bf16[16,32,128]{2,1,0:T(8,128)(2,1)}) custom-call(bf16[4,288,128]{2,1,0:T(8,128)(2,1)S(1)} %all_to_all.20.bundle.refs_1_), custom_call_target="tpu_custom_call" | custom-call | tf_op jit(solution)/shard_map/pallas_call | solution.py:267
  15.6 16.4 %all-to-all-start.1 = ((bf16[64,40,256]{2,1,0:T(8,128)(2,1)}), bf16[64,40,256]{2,1,0:T(8,128)(2,1)S(1)}, u32[]{:S(2)}, u32[]{:S(2)}) async-start(bf16[64,40,256]{2,1,0:T(8,128)(2,1)} %get-tuple-element.10), calls=%async_computation.1 | async-start | bytes 2621440 | tf_op jit(solution)/shard_map/all_to_all | solution.py:281
  32.0 2.8 %collective-permute-start.2 = (bf16[64,5120]{1,0:T(8,128)(2,1)}, bf16[64,5120]{1,0:T(8,128)(2,1)S(1)}, u32[]{:S(2)}, u32[]{:S(2)}) collective-permute-start(bf16[64,5120]{1,0:T(8,128)(2,1)} %bitcast.7.refs_0_), channel_id=1, source_target_pairs={{0,384},{128,0},{256,128},{384,256},{1,385},{129,1},{257,129},{385... | collective-permute-start | bytes 1966088 | tf_op jit(solution)/shard_map/ppermute | solution.py:231
  34.8 2.5 %collective-permute-start = (bf16[64,5120]{1,0:T(8,128)(2,1)}, bf16[64,5120]{1,0:T(8,128)(2,1)S(1)}, u32[]{:S(2)}, u32[]{:S(2)}) collective-permute-start(bf16[64,5120]{1,0:T(8,128)(2,1)} %bitcast.7.refs_0_), channel_id=1, source_target_pairs={{0,128},{128,256},{256,384},{384,0},{1,129},{129,257},{257,385},{3... | collective-permute-start | bytes 1966088 | tf_op jit(solution)/shard_map/ppermute | solution.py:231
  37.3 10.6 %collective-permute-done.2.refs_4_ = bf16[64,5120]{1,0:T(8,128)(2,1)S(1)} collective-permute-done((bf16[64,5120]{1,0:T(8,128)(2,1)}, bf16[64,5120]{1,0:T(8,128)(2,1)S(1)}, u32[]{:S(2)}, u32[]{:S(2)}) %collective-permute-start.2) | collective-permute-done | bytes 655392 | tf_op jit(solution)/shard_map/ppermute | solution.py:231
  47.9 0.0 copy-start.2
  47.9 4.0 %collective-permute-start.3 = (bf16[32,5120]{1,0:T(8,128)(2,1)S(1)}, bf16[32,5120]{1,0:T(8,128)(2,1)S(1)}, u32[]{:S(2)}, u32[]{:S(2)}) collective-permute-start(bf16[32,5120]{1,0:T(8,128)(2,1)S(1)} %slice.9), channel_id=1, source_target_pairs={{0,384},{128,0},{256,128},{384,256},{1,385},{129,1},{257,129},{385... | collective-permute-start | bytes 983048 | tf_op jit(solution)/shard_map/ppermute | solution.py:231
  51.9 0.0 collective-permute-done.refs_1_
  52.0 0.0 copy-start.3
  52.0 1.9 %collective-permute-start.1 = (bf16[32,5120]{1,0:T(8,128)(2,1)S(1)}, bf16[32,5120]{1,0:T(8,128)(2,1)}, u32[]{:S(2)}, u32[]{:S(2)}) collective-permute-start(bf16[32,5120]{1,0:T(8,128)(2,1)S(1)} %slice.8), channel_id=1, source_target_pairs={{0,128},{128,256},{256,384},{384,0},{1,129},{129,257},{257,385},{3... | collective-permute-start | bytes 983048 | tf_op jit(solution)/shard_map/ppermute | solution.py:231
  53.9 2.1 %collective-permute-done.3.refs_3_ = bf16[32,5120]{1,0:T(8,128)(2,1)S(1)} collective-permute-done((bf16[32,5120]{1,0:T(8,128)(2,1)S(1)}, bf16[32,5120]{1,0:T(8,128)(2,1)S(1)}, u32[]{:S(2)}, u32[]{:S(2)}) %collective-permute-start.3) | collective-permute-done | bytes 327712 | tf_op jit(solution)/shard_map/ppermute | solution.py:231
  56.0 0.0 copy-start.4
  56.0 5.3 %collective-permute-done.1.refs_2_ = bf16[32,5120]{1,0:T(8,128)(2,1)} collective-permute-done((bf16[32,5120]{1,0:T(8,128)(2,1)S(1)}, bf16[32,5120]{1,0:T(8,128)(2,1)}, u32[]{:S(2)}, u32[]{:S(2)}) %collective-permute-start.1) | collective-permute-done | bytes 327712 | tf_op jit(solution)/shard_map/ppermute | solution.py:231
  61.3 1.9 %all-to-all-done.1 = bf16[64,40,256]{2,1,0:T(8,128)(2,1)S(1)} async-done(((bf16[64,40,256]{2,1,0:T(8,128)(2,1)}), bf16[64,40,256]{2,1,0:T(8,128)(2,1)S(1)}, u32[]{:S(2)}, u32[]{:S(2)}) %all-to-all-start.1) | async-done | bytes 1310752 | tf_op jit(solution)/shard_map/all_to_all | solution.py:281
  63.2 0.0 copy-start.1
  63.2 6.7 %collective-permute-start.4 = (bf16[2560,256]{1,0:T(8,128)(2,1)S(1)}, bf16[2560,256]{1,0:T(8,128)(2,1)}, u32[]{:S(2)}, u32[]{:S(2)}) collective-permute-start(bf16[2560,256]{1,0:T(8,128)(2,1)S(1)} %bitcast.20), channel_id=1, source_target_pairs={{0,8},{8,0},{1,9},{9,1},{2,10},{10,2},{3,11},{11,3},{4,12},{12,4},... | collective-permute-start | bytes 3932168 | tf_op jit(solution)/shard_map/ppermute | solution.py:231
  69.9 5.4 %all-to-all-start.2 = ((bf16[16,32,128]{2,1,0:T(8,128)(2,1)}), bf16[16,32,128]{2,1,0:T(8,128)(2,1)S(1)}, u32[]{:S(2)}, u32[]{:S(2)}) async-start(bf16[16,32,128]{2,1,0:T(8,128)(2,1)} %get-tuple-element.12), calls=%async_computation.2 | async-start | bytes 262144 | tf_op jit(solution)/shard_map/all_to_all | solution.py:291
  75.3 0.0 collective-permute-done.4.refs_6_
  75.3 0.0 copy-done.2
  75.3 0.0 copy-done.3
  75.3 0.0 copy-done.4
  75.3 0.0 copy-done.1
  75.3 5.5 %shard_map.133.refs_2_ = bf16[512,256]{1,0:T(8,128)(2,1)} custom-call(bf16[64,5120]{1,0:T(8,128)(2,1)} %bitcast.7.refs_0_, bf16[64,5120]{1,0:T(8,128)(2,1)} %copy-done.3, bf16[32,5120]{1,0:T(8,128)(2,1)} %collective-permute-done.1.refs_2_, bf16[32,5120]{1,0:T(8,128)(2,1)} %copy-done.4, bf16[64,5120]{1,0:T(8,128)(2,1)} %copy-done.2, ...), custom_call_target="tpu_custom_call" | custom-call | flops 1400000000 | bytes 8000000 | tf_op jit(solution)/shard_map/pallas_call | solution.py:292
  80.8 3.6 %all-to-all-done.2.refs_0_ = bf16[16,32,128]{2,1,0:T(8,128)(2,1)S(1)} async-done(((bf16[16,32,128]{2,1,0:T(8,128)(2,1)}), bf16[16,32,128]{2,1,0:T(8,128)(2,1)S(1)}, u32[]{:S(2)}, u32[]{:S(2)}) %all-to-all-start.2) | async-done | bytes 131104 | tf_op jit(solution)/shard_map/all_to_all | solution.py:291
  84.4 0.0 copy-start
  84.4 0.9 copy-done
  85.4 1.6 %shard_map.134 = bf16[512,384]{1,0:T(8,128)(2,1)S(1)} custom-call(bf16[16,32,128]{2,1,0:T(8,128)(2,1)S(1)} %all-to-all-done.2.refs_0_, bf16[4,288,128]{2,1,0:T(8,128)(2,1)S(1)} %all_to_all.20.bundle.refs_1_, bf16[512,256]{1,0:T(8,128)(2,1)S(1)} %copy-done), custom_call_target="tpu_custom_call" | custom-call | tf_op jit(solution)/shard_map/pallas_call | solution.py:323
  87.0 19.2 %all_to_all.21 = bf16[64,8,384]{2,1,0:T(8,128)(2,1)S(1)} all-to-all(bf16[64,8,384]{2,1,0:T(8,128)(2,1)S(1)} %bitcast.18), channel_id=1, replica_groups=mesh['x'=4,'y'=8,'c'=2,'z'=8] {'x','y','c'}, dimensions={0} | all-to-all | bytes 786432 | tf_op jit(solution)/shard_map/all_to_all | solution.py:336
  106.2 1.0 shard_map.135
  (2 shorter events, 0.0 us)
Async XLA Ops:
  15.6 47.6 %all-to-all-start.1 = ((bf16[64,40,256]{2,1,0:T(8,128)(2,1)}), bf16[64,40,256]{2,1,0:T(8,128)(2,1)S(1)}, u32[]{:S(2)}, u32[]{:S(2)}) async-start(bf16[64,40,256]{2,1,0:T(8,128)(2,1)} %get-tuple-element.10), calls=%async_computation.1 | async-start | bytes 2621440 | tf_op jit(solution)/shard_map/all_to_all | solution.py:281
  32.0 15.9 %collective-permute-start.2 = (bf16[64,5120]{1,0:T(8,128)(2,1)}, bf16[64,5120]{1,0:T(8,128)(2,1)S(1)}, u32[]{:S(2)}, u32[]{:S(2)}) collective-permute-start(bf16[64,5120]{1,0:T(8,128)(2,1)} %bitcast.7.refs_0_), channel_id=1, source_target_pairs={{0,384},{128,0},{256,128},{384,256},{1,385},{129,1},{257,129},{385... | collective-permute-start | bytes 1966088 | tf_op jit(solution)/shard_map/ppermute | solution.py:231
  34.8 17.1 %collective-permute-start = (bf16[64,5120]{1,0:T(8,128)(2,1)}, bf16[64,5120]{1,0:T(8,128)(2,1)S(1)}, u32[]{:S(2)}, u32[]{:S(2)}) collective-permute-start(bf16[64,5120]{1,0:T(8,128)(2,1)} %bitcast.7.refs_0_), channel_id=1, source_target_pairs={{0,128},{128,256},{256,384},{384,0},{1,129},{129,257},{257,385},{3... | collective-permute-start | bytes 1966088 | tf_op jit(solution)/shard_map/ppermute | solution.py:231
  47.9 27.4 %copy-start.2 = (bf16[64,5120]{1,0:T(8,128)(2,1)}, bf16[64,5120]{1,0:T(8,128)(2,1)S(1)}, u32[]{:S(2)}) copy-start(bf16[64,5120]{1,0:T(8,128)(2,1)S(1)} %collective-permute-done.2.refs_4_) | copy-start | bytes 1966084
  47.9 8.1 %collective-permute-start.3 = (bf16[32,5120]{1,0:T(8,128)(2,1)S(1)}, bf16[32,5120]{1,0:T(8,128)(2,1)S(1)}, u32[]{:S(2)}, u32[]{:S(2)}) collective-permute-start(bf16[32,5120]{1,0:T(8,128)(2,1)S(1)} %slice.9), channel_id=1, source_target_pairs={{0,384},{128,0},{256,128},{384,256},{1,385},{129,1},{257,129},{385... | collective-permute-start | bytes 983048 | tf_op jit(solution)/shard_map/ppermute | solution.py:231
  52.0 23.3 %copy-start.3 = (bf16[64,5120]{1,0:T(8,128)(2,1)}, bf16[64,5120]{1,0:T(8,128)(2,1)S(1)}, u32[]{:S(2)}) copy-start(bf16[64,5120]{1,0:T(8,128)(2,1)S(1)} %collective-permute-done.refs_1_) | copy-start | bytes 1966084
  52.0 9.3 %collective-permute-start.1 = (bf16[32,5120]{1,0:T(8,128)(2,1)S(1)}, bf16[32,5120]{1,0:T(8,128)(2,1)}, u32[]{:S(2)}, u32[]{:S(2)}) collective-permute-start(bf16[32,5120]{1,0:T(8,128)(2,1)S(1)} %slice.8), channel_id=1, source_target_pairs={{0,128},{128,256},{256,384},{384,0},{1,129},{129,257},{257,385},{3... | collective-permute-start | bytes 983048 | tf_op jit(solution)/shard_map/ppermute | solution.py:231
  56.0 19.3 %copy-start.4 = (bf16[32,5120]{1,0:T(8,128)(2,1)}, bf16[32,5120]{1,0:T(8,128)(2,1)S(1)}, u32[]{:S(2)}) copy-start(bf16[32,5120]{1,0:T(8,128)(2,1)S(1)} %collective-permute-done.3.refs_3_) | copy-start | bytes 983044
  63.2 12.1 %copy-start.1 = (bf16[64,40,256]{2,1,0:T(8,128)(2,1)}, bf16[64,40,256]{2,1,0:T(8,128)(2,1)S(1)}, u32[]{:S(2)}) copy-start(bf16[64,40,256]{2,1,0:T(8,128)(2,1)S(1)} %all-to-all-done.1) | copy-start | bytes 3932164
  63.2 12.1 %collective-permute-start.4 = (bf16[2560,256]{1,0:T(8,128)(2,1)S(1)}, bf16[2560,256]{1,0:T(8,128)(2,1)}, u32[]{:S(2)}, u32[]{:S(2)}) collective-permute-start(bf16[2560,256]{1,0:T(8,128)(2,1)S(1)} %bitcast.20), channel_id=1, source_target_pairs={{0,8},{8,0},{1,9},{9,1},{2,10},{10,2},{3,11},{11,3},{4,12},{12,4},... | collective-permute-start | bytes 3932168 | tf_op jit(solution)/shard_map/ppermute | solution.py:231
  69.9 14.5 %all-to-all-start.2 = ((bf16[16,32,128]{2,1,0:T(8,128)(2,1)}), bf16[16,32,128]{2,1,0:T(8,128)(2,1)S(1)}, u32[]{:S(2)}, u32[]{:S(2)}) async-start(bf16[16,32,128]{2,1,0:T(8,128)(2,1)} %get-tuple-element.12), calls=%async_computation.2 | async-start | bytes 262144 | tf_op jit(solution)/shard_map/all_to_all | solution.py:291
  84.4 1.0 copy-start

commit v6 on v5

--- a/solution.py
+++ b/solution.py
@@ -130,18 +130,14 @@
 
 
 def attend(*refs):
-    inputs, out, held, sems = refs[0:3], refs[3], refs[4:7], refs[7]
-    copies = fetch(list(zip(inputs, held)), sems)
-    asked, bundle, rebuilt = held
+    asked, bundle, rebuilt, out = refs
     head = lax.axis_index("x")
     y = lax.axis_index("y")
     c = lax.axis_index("c")
-    copies[0].wait()
     queries = asked[...].astype(f32).reshape(NY * NC, NX, 8, HD)
     queries = jnp.stack([queries[:, i] for i in range(NX)], axis=0)
     queries = queries.reshape(512, HD).astype(bf16)
 
-    copies[1].wait()
     cache_keys = bundle[:, 32:160, :].reshape(512, HD)
     cache_values = bundle[:, 160:288, :].reshape(512, HD)
     lane = lax.broadcasted_iota(jnp.int32, (1, HD), 1).astype(f32)
@@ -159,7 +155,6 @@
     fresh_ok = (fresh_at < NX) & (fresh_at * 16 + y * 2 + c <= token)
     fresh_scores = jnp.where(fresh_ok, dot_nt(queries, fresh_keys), masked_score)
 
-    copies[2].wait()
     new_keys = rebuilt[0:256, 0:HD]
     new_values = rebuilt[256:512, 0:HD]
     column = lax.broadcasted_iota(jnp.int32, (1, 256), 1)
@@ -322,15 +317,9 @@
 
     parts = pl.pallas_call(
         attend,
-        in_specs=[anywhere] * 3,
+        in_specs=[whole] * 3,
         out_specs=whole,
         out_shape=jax.ShapeDtypeStruct((512, 384), bf16),
-        scratch_shapes=[
-            pltpu.VMEM((NY * NC, 32, HD), bf16),
-            pltpu.VMEM((NX, 288, HD), bf16),
-            pltpu.VMEM((512, 256), bf16),
-            pltpu.SemaphoreType.DMA((3,)),
-        ],
         compiler_params=pltpu.CompilerParams(vmem_limit_bytes=16 * 1024 * 1024),
     )(asked, bundle, rebuilt)
     parts = lax.all_to_all(parts.reshape(64, 8, 384), CTX, 0, 0, tiled=True)

time: 108 us -> 107 us (level)
  no operation moved by 1% of the time
where the time goes in v6:
time: 107 us
  starting transfers between devices  39.7 us (37%)
  blocking collectives  29.7 us (28%)
  waiting for transfers between devices  23.5 us (22%)
  Pallas kernels  10.7 us (10%)
  between operations  2.07 us (2%)
    all_to_all x1, blocking collectives, body(): parts = lax.all_to_all(parts.reshape(64, 8, 384), CTX, 0, 0, tiled=True)  19.2 us
    ppermute x5, waiting for transfers between devices, shift_by(): lax.ppermute(value, axis, [(i, (i + step) % size) for i in range(size)])  18 us
    ppermute x5, starting transfers between devices, shift_by(): lax.ppermute(value, axis, [(i, (i + step) % size) for i in range(size)])  17.9 us
    all_to_all x1, starting transfers between devices, body(): gathered = lax.all_to_all(weight, ('y', 'z'), 0, 0, tiled=True)  16.4 us
    all_to_all x1, blocking collectives, body(): bundle = lax.all_to_all(bundle, 'x', 0, 0, tiled=True)  10.6 us
    pallas_call x1, Pallas kernels, body(): pl.pallas_call(project, in_specs=[anywhere] * 10, out_specs=whole, out_sh...  5.46 us
    all_to_all x1, starting transfers between devices, body(): asked = lax.all_to_all(asked, ('y', 'c'), 0, 0, tiled=True)  5.38 us
    all_to_all x1, waiting for transfers between devices, body(): asked = lax.all_to_all(asked, ('y', 'c'), 0, 0, tiled=True)  3.65 us
  transfers between devices with their start and end apart: 7, of which 5 were waited for; matrix products, arithmetic and copies ran while one was open for 0% of the time, Pallas kernels for 5%

profile of v6, /device:TPU:1, one launch (start us, length us, event | category | flops | bytes accessed | tf_op | source)
XLA Modules:
  0.0 106.8 jit_solution(4637265844907102355)
XLA Ops:
  1.9 1.9 %shard_map.131 = bf16[4,288,128]{2,1,0:T(8,128)(2,1)} custom-call(bf16[10,1024]{1,0:T(8,128)(2,1)} %refs_0_.1, bf16[1,4096]{1,0:T(2,128)(2,1)} %bitcast.26, bf16[1,512]{1,0:T(2,128)(2,1)} %bitcast.27, bf16[1,512]{1,0:T(2,128)(2,1)} %bitcast.28, bf16[128,512]{1,0:T(8,128)(2,1)} %bitcast.23, bf16[128,512]{1,0:T(8,128)(2,1)} %bitcast.24, ...), custom_call_target="tpu_custom_call" | custom-call | tf_op jit(solution)/shard_map/pallas_call | solution.py:251
  3.8 10.6 %all_to_all.20.bundle.refs_1_ = bf16[4,288,128]{2,1,0:T(8,128)(2,1)S(1)} all-to-all(bf16[4,288,128]{2,1,0:T(8,128)(2,1)} %shard_map.131), channel_id=1, replica_groups=mesh['x'=4,'y'=8,'c'=2,'z'=8] {'x'}, dimensions={0} | all-to-all | bytes 589824 | tf_op jit(solution)/shard_map/all_to_all | solution.py:260
  14.4 1.2 %shard_map.132 = (bf16[64,40,256]{2,1,0:T(8,128)(2,1)}, bf16[16,32,128]{2,1,0:T(8,128)(2,1)}) custom-call(bf16[4,288,128]{2,1,0:T(8,128)(2,1)S(1)} %all_to_all.20.bundle.refs_1_), custom_call_target="tpu_custom_call" | custom-call | tf_op jit(solution)/shard_map/pallas_call | solution.py:262
  15.6 16.4 %all-to-all-start.1 = ((bf16[64,40,256]{2,1,0:T(8,128)(2,1)}), bf16[64,40,256]{2,1,0:T(8,128)(2,1)S(1)}, u32[]{:S(2)}, u32[]{:S(2)}) async-start(bf16[64,40,256]{2,1,0:T(8,128)(2,1)} %get-tuple-element.10), calls=%async_computation.1 | async-start | bytes 2621440 | tf_op jit(solution)/shard_map/all_to_all | solution.py:276
  32.0 2.8 %collective-permute-start.2 = (bf16[64,5120]{1,0:T(8,128)(2,1)}, bf16[64,5120]{1,0:T(8,128)(2,1)S(1)}, u32[]{:S(2)}, u32[]{:S(2)}) collective-permute-start(bf16[64,5120]{1,0:T(8,128)(2,1)} %bitcast.7.refs_0_), channel_id=1, source_target_pairs={{0,384},{128,0},{256,128},{384,256},{1,385},{129,1},{257,129},{385... | collective-permute-start | bytes 1966088 | tf_op jit(solution)/shard_map/ppermute | solution.py:226
  34.8 2.5 %collective-permute-start = (bf16[64,5120]{1,0:T(8,128)(2,1)}, bf16[64,5120]{1,0:T(8,128)(2,1)S(1)}, u32[]{:S(2)}, u32[]{:S(2)}) collective-permute-start(bf16[64,5120]{1,0:T(8,128)(2,1)} %bitcast.7.refs_0_), channel_id=1, source_target_pairs={{0,128},{128,256},{256,384},{384,0},{1,129},{129,257},{257,385},{3... | collective-permute-start | bytes 1966088 | tf_op jit(solution)/shard_map/ppermute | solution.py:226
  37.3 10.6 %collective-permute-done.2.refs_4_ = bf16[64,5120]{1,0:T(8,128)(2,1)S(1)} collective-permute-done((bf16[64,5120]{1,0:T(8,128)(2,1)}, bf16[64,5120]{1,0:T(8,128)(2,1)S(1)}, u32[]{:S(2)}, u32[]{:S(2)}) %collective-permute-start.2) | collective-permute-done | bytes 655392 | tf_op jit(solution)/shard_map/ppermute | solution.py:226
  47.9 0.0 copy-start.2
  47.9 4.0 %collective-permute-start.3 = (bf16[32,5120]{1,0:T(8,128)(2,1)S(1)}, bf16[32,5120]{1,0:T(8,128)(2,1)S(1)}, u32[]{:S(2)}, u32[]{:S(2)}) collective-permute-start(bf16[32,5120]{1,0:T(8,128)(2,1)S(1)} %slice.9), channel_id=1, source_target_pairs={{0,384},{128,0},{256,128},{384,256},{1,385},{129,1},{257,129},{385... | collective-permute-start | bytes 983048 | tf_op jit(solution)/shard_map/ppermute | solution.py:226
  51.9 0.0 collective-permute-done.refs_1_
  52.0 0.0 copy-start.3
  52.0 1.9 %collective-permute-start.1 = (bf16[32,5120]{1,0:T(8,128)(2,1)S(1)}, bf16[32,5120]{1,0:T(8,128)(2,1)}, u32[]{:S(2)}, u32[]{:S(2)}) collective-permute-start(bf16[32,5120]{1,0:T(8,128)(2,1)S(1)} %slice.8), channel_id=1, source_target_pairs={{0,128},{128,256},{256,384},{384,0},{1,129},{129,257},{257,385},{3... | collective-permute-start | bytes 983048 | tf_op jit(solution)/shard_map/ppermute | solution.py:226
  53.9 2.1 %collective-permute-done.3.refs_3_ = bf16[32,5120]{1,0:T(8,128)(2,1)S(1)} collective-permute-done((bf16[32,5120]{1,0:T(8,128)(2,1)S(1)}, bf16[32,5120]{1,0:T(8,128)(2,1)S(1)}, u32[]{:S(2)}, u32[]{:S(2)}) %collective-permute-start.3) | collective-permute-done | bytes 327712 | tf_op jit(solution)/shard_map/ppermute | solution.py:226
  56.0 0.0 copy-start.4
  56.0 5.3 %collective-permute-done.1.refs_2_ = bf16[32,5120]{1,0:T(8,128)(2,1)} collective-permute-done((bf16[32,5120]{1,0:T(8,128)(2,1)S(1)}, bf16[32,5120]{1,0:T(8,128)(2,1)}, u32[]{:S(2)}, u32[]{:S(2)}) %collective-permute-start.1) | collective-permute-done | bytes 327712 | tf_op jit(solution)/shard_map/ppermute | solution.py:226
  61.3 1.9 %all-to-all-done.1 = bf16[64,40,256]{2,1,0:T(8,128)(2,1)S(1)} async-done(((bf16[64,40,256]{2,1,0:T(8,128)(2,1)}), bf16[64,40,256]{2,1,0:T(8,128)(2,1)S(1)}, u32[]{:S(2)}, u32[]{:S(2)}) %all-to-all-start.1) | async-done | bytes 1310752 | tf_op jit(solution)/shard_map/all_to_all | solution.py:276
  63.2 0.0 copy-start.1
  63.2 6.7 %collective-permute-start.4 = (bf16[2560,256]{1,0:T(8,128)(2,1)S(1)}, bf16[2560,256]{1,0:T(8,128)(2,1)}, u32[]{:S(2)}, u32[]{:S(2)}) collective-permute-start(bf16[2560,256]{1,0:T(8,128)(2,1)S(1)} %bitcast.20), channel_id=1, source_target_pairs={{0,8},{8,0},{1,9},{9,1},{2,10},{10,2},{3,11},{11,3},{4,12},{12,4},... | collective-permute-start | bytes 3932168 | tf_op jit(solution)/shard_map/ppermute | solution.py:226
  69.9 5.4 %all-to-all-start.2 = ((bf16[16,32,128]{2,1,0:T(8,128)(2,1)}), bf16[16,32,128]{2,1,0:T(8,128)(2,1)S(1)}, u32[]{:S(2)}, u32[]{:S(2)}) async-start(bf16[16,32,128]{2,1,0:T(8,128)(2,1)} %get-tuple-element.12), calls=%async_computation.2 | async-start | bytes 262144 | tf_op jit(solution)/shard_map/all_to_all | solution.py:286
  75.3 0.0 collective-permute-done.4.refs_6_
  75.3 0.0 copy-done.2
  75.3 0.0 copy-done.3
  75.3 0.0 copy-done.4
  75.3 0.0 copy-done.1
  75.3 5.5 %shard_map.133.refs_2_ = bf16[512,256]{1,0:T(8,128)(2,1)} custom-call(bf16[64,5120]{1,0:T(8,128)(2,1)} %bitcast.7.refs_0_, bf16[64,5120]{1,0:T(8,128)(2,1)} %copy-done.3, bf16[32,5120]{1,0:T(8,128)(2,1)} %collective-permute-done.1.refs_2_, bf16[32,5120]{1,0:T(8,128)(2,1)} %copy-done.4, bf16[64,5120]{1,0:T(8,128)(2,1)} %copy-done.2, ...), custom_call_target="tpu_custom_call" | custom-call | flops 1400000000 | bytes 8000000 | tf_op jit(solution)/shard_map/pallas_call | solution.py:287
  80.8 3.6 %all-to-all-done.2.refs_0_ = bf16[16,32,128]{2,1,0:T(8,128)(2,1)S(1)} async-done(((bf16[16,32,128]{2,1,0:T(8,128)(2,1)}), bf16[16,32,128]{2,1,0:T(8,128)(2,1)S(1)}, u32[]{:S(2)}, u32[]{:S(2)}) %all-to-all-start.2) | async-done | bytes 131104 | tf_op jit(solution)/shard_map/all_to_all | solution.py:286
  84.4 0.0 copy-start
  84.4 0.9 copy-done
  85.4 1.2 %shard_map.134 = bf16[512,384]{1,0:T(8,128)(2,1)S(1)} custom-call(bf16[16,32,128]{2,1,0:T(8,128)(2,1)S(1)} %all-to-all-done.2.refs_0_, bf16[4,288,128]{2,1,0:T(8,128)(2,1)S(1)} %all_to_all.20.bundle.refs_1_, bf16[512,256]{1,0:T(8,128)(2,1)S(1)} %copy-done), custom_call_target="tpu_custom_call" | custom-call | tf_op jit(solution)/shard_map/pallas_call | solution.py:318
  86.6 19.2 %all_to_all.21 = bf16[64,8,384]{2,1,0:T(8,128)(2,1)S(1)} all-to-all(bf16[64,8,384]{2,1,0:T(8,128)(2,1)S(1)} %bitcast.18), channel_id=1, replica_groups=mesh['x'=4,'y'=8,'c'=2,'z'=8] {'x','y','c'}, dimensions={0} | all-to-all | bytes 786432 | tf_op jit(solution)/shard_map/all_to_all | solution.py:325
  105.7 1.0 shard_map.135
  (2 shorter events, 0.0 us)
Async XLA Ops:
  15.6 47.6 %all-to-all-start.1 = ((bf16[64,40,256]{2,1,0:T(8,128)(2,1)}), bf16[64,40,256]{2,1,0:T(8,128)(2,1)S(1)}, u32[]{:S(2)}, u32[]{:S(2)}) async-start(bf16[64,40,256]{2,1,0:T(8,128)(2,1)} %get-tuple-element.10), calls=%async_computation.1 | async-start | bytes 2621440 | tf_op jit(solution)/shard_map/all_to_all | solution.py:276
  32.0 15.9 %collective-permute-start.2 = (bf16[64,5120]{1,0:T(8,128)(2,1)}, bf16[64,5120]{1,0:T(8,128)(2,1)S(1)}, u32[]{:S(2)}, u32[]{:S(2)}) collective-permute-start(bf16[64,5120]{1,0:T(8,128)(2,1)} %bitcast.7.refs_0_), channel_id=1, source_target_pairs={{0,384},{128,0},{256,128},{384,256},{1,385},{129,1},{257,129},{385... | collective-permute-start | bytes 1966088 | tf_op jit(solution)/shard_map/ppermute | solution.py:226
  34.8 17.1 %collective-permute-start = (bf16[64,5120]{1,0:T(8,128)(2,1)}, bf16[64,5120]{1,0:T(8,128)(2,1)S(1)}, u32[]{:S(2)}, u32[]{:S(2)}) collective-permute-start(bf16[64,5120]{1,0:T(8,128)(2,1)} %bitcast.7.refs_0_), channel_id=1, source_target_pairs={{0,128},{128,256},{256,384},{384,0},{1,129},{129,257},{257,385},{3... | collective-permute-start | bytes 1966088 | tf_op jit(solution)/shard_map/ppermute | solution.py:226
  47.9 27.4 %copy-start.2 = (bf16[64,5120]{1,0:T(8,128)(2,1)}, bf16[64,5120]{1,0:T(8,128)(2,1)S(1)}, u32[]{:S(2)}) copy-start(bf16[64,5120]{1,0:T(8,128)(2,1)S(1)} %collective-permute-done.2.refs_4_) | copy-start | bytes 1966084
  47.9 8.1 %collective-permute-start.3 = (bf16[32,5120]{1,0:T(8,128)(2,1)S(1)}, bf16[32,5120]{1,0:T(8,128)(2,1)S(1)}, u32[]{:S(2)}, u32[]{:S(2)}) collective-permute-start(bf16[32,5120]{1,0:T(8,128)(2,1)S(1)} %slice.9), channel_id=1, source_target_pairs={{0,384},{128,0},{256,128},{384,256},{1,385},{129,1},{257,129},{385... | collective-permute-start | bytes 983048 | tf_op jit(solution)/shard_map/ppermute | solution.py:226
  52.0 23.3 %copy-start.3 = (bf16[64,5120]{1,0:T(8,128)(2,1)}, bf16[64,5120]{1,0:T(8,128)(2,1)S(1)}, u32[]{:S(2)}) copy-start(bf16[64,5120]{1,0:T(8,128)(2,1)S(1)} %collective-permute-done.refs_1_) | copy-start | bytes 1966084
  52.0 9.3 %collective-permute-start.1 = (bf16[32,5120]{1,0:T(8,128)(2,1)S(1)}, bf16[32,5120]{1,0:T(8,128)(2,1)}, u32[]{:S(2)}, u32[]{:S(2)}) collective-permute-start(bf16[32,5120]{1,0:T(8,128)(2,1)S(1)} %slice.8), channel_id=1, source_target_pairs={{0,128},{128,256},{256,384},{384,0},{1,129},{129,257},{257,385},{3... | collective-permute-start | bytes 983048 | tf_op jit(solution)/shard_map/ppermute | solution.py:226
  56.0 19.3 %copy-start.4 = (bf16[32,5120]{1,0:T(8,128)(2,1)}, bf16[32,5120]{1,0:T(8,128)(2,1)S(1)}, u32[]{:S(2)}) copy-start(bf16[32,5120]{1,0:T(8,128)(2,1)S(1)} %collective-permute-done.3.refs_3_) | copy-start | bytes 983044
  63.2 12.1 %copy-start.1 = (bf16[64,40,256]{2,1,0:T(8,128)(2,1)}, bf16[64,40,256]{2,1,0:T(8,128)(2,1)S(1)}, u32[]{:S(2)}) copy-start(bf16[64,40,256]{2,1,0:T(8,128)(2,1)S(1)} %all-to-all-done.1) | copy-start | bytes 3932164
  63.2 12.1 %collective-permute-start.4 = (bf16[2560,256]{1,0:T(8,128)(2,1)S(1)}, bf16[2560,256]{1,0:T(8,128)(2,1)}, u32[]{:S(2)}, u32[]{:S(2)}) collective-permute-start(bf16[2560,256]{1,0:T(8,128)(2,1)S(1)} %bitcast.20), channel_id=1, source_target_pairs={{0,8},{8,0},{1,9},{9,1},{2,10},{10,2},{3,11},{11,3},{4,12},{12,4},... | collective-permute-start | bytes 3932168 | tf_op jit(solution)/shard_map/ppermute | solution.py:226
  69.9 14.5 %all-to-all-start.2 = ((bf16[16,32,128]{2,1,0:T(8,128)(2,1)}), bf16[16,32,128]{2,1,0:T(8,128)(2,1)S(1)}, u32[]{:S(2)}, u32[]{:S(2)}) async-start(bf16[16,32,128]{2,1,0:T(8,128)(2,1)} %get-tuple-element.12), calls=%async_computation.2 | async-start | bytes 262144 | tf_op jit(solution)/shard_map/all_to_all | solution.py:286
  84.4 1.0 copy-start

commit v7 on v6

--- a/solution.py
+++ b/solution.py
@@ -276,8 +276,8 @@
     gathered = lax.all_to_all(weight, ("y", "z"), 0, 0, tiled=True)
     left = shift_by(rows, "x", 1)
     right = shift_by(rows, "x", -1)
-    far_a = shift_by(left[0:32], "x", 1)
-    far_b = shift_by(right[32:64], "x", -1)
+    far_a = shift_by(left[0:16], "x", 1)
+    far_b = shift_by(right[16:64], "x", -1)
 
     gathered, asked, far_a, far_b = lax.optimization_barrier(
         (gathered.reshape(HALF, 256), asked, far_a, far_b)

time: 107 us -> 107 us (level)
    ppermute x5, waiting for transfers between devices: 18 us -> 16.2 us  [shift_by(): lax.ppermute(value, axis, [(i, (i + step) % size) for i in range(size)])]
    all_to_all x1, waiting for transfers between devices: 1.86 us -> 2.94 us  [body(): gathered = lax.all_to_all(weight, ('y', 'z'), 0, 0, tiled=True)]
  transfers between devices with their start and end apart: 7 -> 7, of which waited for: 5 -> 4; matrix products, arithmetic and copies ran while one was open for 0% -> 0% of each run, Pallas kernels for 5% -> 5%
where the time goes in v7:
time: 107 us
  starting transfers between devices  39.7 us (37%)
  blocking collectives  29.7 us (28%)
  waiting for transfers between devices  22.8 us (21%)
  Pallas kernels  10.7 us (10%)
  between operations  2.07 us (2%)
  local copies, waits for them, and re-layouts  1.68 us (2%)
    all_to_all x1, blocking collectives, body(): parts = lax.all_to_all(parts.reshape(64, 8, 384), CTX, 0, 0, tiled=True)  19.2 us
    ppermute x5, starting transfers between devices, shift_by(): lax.ppermute(value, axis, [(i, (i + step) % size) for i in range(size)])  17.9 us
    all_to_all x1, starting transfers between devices, body(): gathered = lax.all_to_all(weight, ('y', 'z'), 0, 0, tiled=True)  16.4 us
    ppermute x5, waiting for transfers between devices, shift_by(): lax.ppermute(value, axis, [(i, (i + step) % size) for i in range(size)])  16.2 us
    all_to_all x1, blocking collectives, body(): bundle = lax.all_to_all(bundle, 'x', 0, 0, tiled=True)  10.6 us
    pallas_call x1, Pallas kernels, body(): pl.pallas_call(project, in_specs=[anywhere] * 10, out_specs=whole, out_sh...  5.46 us
    all_to_all x1, starting transfers between devices, body(): asked = lax.all_to_all(asked, ('y', 'c'), 0, 0, tiled=True)  5.38 us
    all_to_all x1, waiting for transfers between devices, body(): asked = lax.all_to_all(asked, ('y', 'c'), 0, 0, tiled=True)  3.66 us
  transfers between devices with their start and end apart: 7, of which 4 were waited for; matrix products, arithmetic and copies ran while one was open for 0% of the time, Pallas kernels for 5%

profile of v7, /device:TPU:1, one launch (start us, length us, event | category | flops | bytes accessed | tf_op | source)
XLA Modules:
  0.0 106.8 jit_solution(16911917466049659824)
XLA Ops:
  1.9 1.9 %shard_map.131 = bf16[4,288,128]{2,1,0:T(8,128)(2,1)} custom-call(bf16[10,1024]{1,0:T(8,128)(2,1)} %refs_0_.1, bf16[1,4096]{1,0:T(2,128)(2,1)} %bitcast.26, bf16[1,512]{1,0:T(2,128)(2,1)} %bitcast.27, bf16[1,512]{1,0:T(2,128)(2,1)} %bitcast.28, bf16[128,512]{1,0:T(8,128)(2,1)} %bitcast.23, bf16[128,512]{1,0:T(8,128)(2,1)} %bitcast.24, ...), custom_call_target="tpu_custom_call" | custom-call | tf_op jit(solution)/shard_map/pallas_call | solution.py:251
  3.8 10.6 %all_to_all.20.bundle.refs_1_ = bf16[4,288,128]{2,1,0:T(8,128)(2,1)S(1)} all-to-all(bf16[4,288,128]{2,1,0:T(8,128)(2,1)} %shard_map.131), channel_id=1, replica_groups=mesh['x'=4,'y'=8,'c'=2,'z'=8] {'x'}, dimensions={0} | all-to-all | bytes 589824 | tf_op jit(solution)/shard_map/all_to_all | solution.py:260
  14.4 1.2 %shard_map.132 = (bf16[64,40,256]{2,1,0:T(8,128)(2,1)}, bf16[16,32,128]{2,1,0:T(8,128)(2,1)}) custom-call(bf16[4,288,128]{2,1,0:T(8,128)(2,1)S(1)} %all_to_all.20.bundle.refs_1_), custom_call_target="tpu_custom_call" | custom-call | tf_op jit(solution)/shard_map/pallas_call | solution.py:262
  15.6 16.4 %all-to-all-start.1 = ((bf16[64,40,256]{2,1,0:T(8,128)(2,1)}), bf16[64,40,256]{2,1,0:T(8,128)(2,1)S(1)}, u32[]{:S(2)}, u32[]{:S(2)}) async-start(bf16[64,40,256]{2,1,0:T(8,128)(2,1)} %get-tuple-element.10), calls=%async_computation.1 | async-start | bytes 2621440 | tf_op jit(solution)/shard_map/all_to_all | solution.py:276
  32.0 2.8 %collective-permute-start.2 = (bf16[64,5120]{1,0:T(8,128)(2,1)}, bf16[64,5120]{1,0:T(8,128)(2,1)S(1)}, u32[]{:S(2)}, u32[]{:S(2)}) collective-permute-start(bf16[64,5120]{1,0:T(8,128)(2,1)} %bitcast.7.refs_0_), channel_id=1, source_target_pairs={{0,384},{128,0},{256,128},{384,256},{1,385},{129,1},{257,129},{385... | collective-permute-start | bytes 1966088 | tf_op jit(solution)/shard_map/ppermute | solution.py:226
  34.8 2.5 %collective-permute-start = (bf16[64,5120]{1,0:T(8,128)(2,1)}, bf16[64,5120]{1,0:T(8,128)(2,1)S(1)}, u32[]{:S(2)}, u32[]{:S(2)}) collective-permute-start(bf16[64,5120]{1,0:T(8,128)(2,1)} %bitcast.7.refs_0_), channel_id=1, source_target_pairs={{0,128},{128,256},{256,384},{384,0},{1,129},{129,257},{257,385},{3... | collective-permute-start | bytes 1966088 | tf_op jit(solution)/shard_map/ppermute | solution.py:226
  37.3 10.6 %collective-permute-done.2.refs_4_ = bf16[64,5120]{1,0:T(8,128)(2,1)S(1)} collective-permute-done((bf16[64,5120]{1,0:T(8,128)(2,1)}, bf16[64,5120]{1,0:T(8,128)(2,1)S(1)}, u32[]{:S(2)}, u32[]{:S(2)}) %collective-permute-start.2) | collective-permute-done | bytes 655392 | tf_op jit(solution)/shard_map/ppermute | solution.py:226
  47.9 0.0 copy-start.2
  48.0 4.0 %collective-permute-start.3 = (bf16[48,5120]{1,0:T(8,128)(2,1)S(1)}, bf16[48,5120]{1,0:T(8,128)(2,1)S(1)}, u32[]{:S(2)}, u32[]{:S(2)}) collective-permute-start(bf16[48,5120]{1,0:T(8,128)(2,1)S(1)} %slice.9), channel_id=1, source_target_pairs={{0,384},{128,0},{256,128},{384,256},{1,385},{129,1},{257,129},{385... | collective-permute-start | bytes 1474568 | tf_op jit(solution)/shard_map/ppermute | solution.py:226
  52.0 0.0 collective-permute-done.refs_1_
  52.0 0.0 copy-start.3
  52.0 1.9 %collective-permute-start.1 = (bf16[16,5120]{1,0:T(8,128)(2,1)S(1)}, bf16[16,5120]{1,0:T(8,128)(2,1)S(1)}, u32[]{:S(2)}, u32[]{:S(2)}) collective-permute-start(bf16[16,5120]{1,0:T(8,128)(2,1)S(1)} %slice.8), channel_id=1, source_target_pairs={{0,128},{128,256},{256,384},{384,0},{1,129},{129,257},{257,385},{3... | collective-permute-start | bytes 491528 | tf_op jit(solution)/shard_map/ppermute | solution.py:226
  53.9 5.6 %collective-permute-done.1.refs_2_ = bf16[16,5120]{1,0:T(8,128)(2,1)S(1)} collective-permute-done((bf16[16,5120]{1,0:T(8,128)(2,1)S(1)}, bf16[16,5120]{1,0:T(8,128)(2,1)S(1)}, u32[]{:S(2)}, u32[]{:S(2)}) %collective-permute-start.1) | collective-permute-done | bytes 163872 | tf_op jit(solution)/shard_map/ppermute | solution.py:226
  59.6 0.0 copy-start.5
  59.6 0.7 copy-done.5
  60.2 0.0 collective-permute-done.3.refs_3_
  60.2 0.0 copy-start.4
  60.2 2.9 %all-to-all-done.1 = bf16[64,40,256]{2,1,0:T(8,128)(2,1)S(1)} async-done(((bf16[64,40,256]{2,1,0:T(8,128)(2,1)}), bf16[64,40,256]{2,1,0:T(8,128)(2,1)S(1)}, u32[]{:S(2)}, u32[]{:S(2)}) %all-to-all-start.1) | async-done | bytes 1310752 | tf_op jit(solution)/shard_map/all_to_all | solution.py:276
  63.2 0.0 copy-start.1
  63.2 6.7 %collective-permute-start.4 = (bf16[2560,256]{1,0:T(8,128)(2,1)S(1)}, bf16[2560,256]{1,0:T(8,128)(2,1)}, u32[]{:S(2)}, u32[]{:S(2)}) collective-permute-start(bf16[2560,256]{1,0:T(8,128)(2,1)S(1)} %bitcast.20), channel_id=1, source_target_pairs={{0,8},{8,0},{1,9},{9,1},{2,10},{10,2},{3,11},{11,3},{4,12},{12,4},... | collective-permute-start | bytes 3932168 | tf_op jit(solution)/shard_map/ppermute | solution.py:226
  69.9 5.4 %all-to-all-start.2 = ((bf16[16,32,128]{2,1,0:T(8,128)(2,1)}), bf16[16,32,128]{2,1,0:T(8,128)(2,1)S(1)}, u32[]{:S(2)}, u32[]{:S(2)}) async-start(bf16[16,32,128]{2,1,0:T(8,128)(2,1)} %get-tuple-element.12), calls=%async_computation.2 | async-start | bytes 262144 | tf_op jit(solution)/shard_map/all_to_all | solution.py:286
  75.3 0.0 collective-permute-done.4.refs_6_
  75.3 0.0 copy-done.2
  75.3 0.0 copy-done.3
  75.3 0.0 copy-done.4
  75.3 0.0 copy-done.1
  75.3 5.5 %shard_map.133.refs_2_ = bf16[512,256]{1,0:T(8,128)(2,1)} custom-call(bf16[64,5120]{1,0:T(8,128)(2,1)} %bitcast.7.refs_0_, bf16[64,5120]{1,0:T(8,128)(2,1)} %copy-done.3, bf16[16,5120]{1,0:T(8,128)(2,1)} %copy-done.5, bf16[48,5120]{1,0:T(8,128)(2,1)} %copy-done.4, bf16[64,5120]{1,0:T(8,128)(2,1)} %copy-done.2, bf16[2560,256]{1,0:T(8,128)(2,1)} %bitcast.21, ...), custom_call_target="tpu_custom_call" | custom-call | flops 1400000000 | bytes 8000000 | tf_op jit(solution)/shard_map/pallas_call | solution.py:287
  80.8 3.7 %all-to-all-done.2.refs_0_ = bf16[16,32,128]{2,1,0:T(8,128)(2,1)S(1)} async-done(((bf16[16,32,128]{2,1,0:T(8,128)(2,1)}), bf16[16,32,128]{2,1,0:T(8,128)(2,1)S(1)}, u32[]{:S(2)}, u32[]{:S(2)}) %all-to-all-start.2) | async-done | bytes 131104 | tf_op jit(solution)/shard_map/all_to_all | solution.py:286
  84.5 0.0 copy-start
  84.5 0.9 copy-done
  85.4 1.2 %shard_map.134 = bf16[512,384]{1,0:T(8,128)(2,1)S(1)} custom-call(bf16[16,32,128]{2,1,0:T(8,128)(2,1)S(1)} %all-to-all-done.2.refs_0_, bf16[4,288,128]{2,1,0:T(8,128)(2,1)S(1)} %all_to_all.20.bundle.refs_1_, bf16[512,256]{1,0:T(8,128)(2,1)S(1)} %copy-done), custom_call_target="tpu_custom_call" | custom-call | tf_op jit(solution)/shard_map/pallas_call | solution.py:318
  86.6 19.2 %all_to_all.21 = bf16[64,8,384]{2,1,0:T(8,128)(2,1)S(1)} all-to-all(bf16[64,8,384]{2,1,0:T(8,128)(2,1)S(1)} %bitcast.18), channel_id=1, replica_groups=mesh['x'=4,'y'=8,'c'=2,'z'=8] {'x','y','c'}, dimensions={0} | all-to-all | bytes 786432 | tf_op jit(solution)/shard_map/all_to_all | solution.py:325
  105.7 1.0 shard_map.135
  (2 shorter events, 0.0 us)
Async XLA Ops:
  15.6 47.6 %all-to-all-start.1 = ((bf16[64,40,256]{2,1,0:T(8,128)(2,1)}), bf16[64,40,256]{2,1,0:T(8,128)(2,1)S(1)}, u32[]{:S(2)}, u32[]{:S(2)}) async-start(bf16[64,40,256]{2,1,0:T(8,128)(2,1)} %get-tuple-element.10), calls=%async_computation.1 | async-start | bytes 2621440 | tf_op jit(solution)/shard_map/all_to_all | solution.py:276
  32.0 15.9 %collective-permute-start.2 = (bf16[64,5120]{1,0:T(8,128)(2,1)}, bf16[64,5120]{1,0:T(8,128)(2,1)S(1)}, u32[]{:S(2)}, u32[]{:S(2)}) collective-permute-start(bf16[64,5120]{1,0:T(8,128)(2,1)} %bitcast.7.refs_0_), channel_id=1, source_target_pairs={{0,384},{128,0},{256,128},{384,256},{1,385},{129,1},{257,129},{385... | collective-permute-start | bytes 1966088 | tf_op jit(solution)/shard_map/ppermute | solution.py:226
  34.8 17.1 %collective-permute-start = (bf16[64,5120]{1,0:T(8,128)(2,1)}, bf16[64,5120]{1,0:T(8,128)(2,1)S(1)}, u32[]{:S(2)}, u32[]{:S(2)}) collective-permute-start(bf16[64,5120]{1,0:T(8,128)(2,1)} %bitcast.7.refs_0_), channel_id=1, source_target_pairs={{0,128},{128,256},{256,384},{384,0},{1,129},{129,257},{257,385},{3... | collective-permute-start | bytes 1966088 | tf_op jit(solution)/shard_map/ppermute | solution.py:226
  47.9 27.4 %copy-start.2 = (bf16[64,5120]{1,0:T(8,128)(2,1)}, bf16[64,5120]{1,0:T(8,128)(2,1)S(1)}, u32[]{:S(2)}) copy-start(bf16[64,5120]{1,0:T(8,128)(2,1)S(1)} %collective-permute-done.2.refs_4_) | copy-start | bytes 1966084
  48.0 12.3 %collective-permute-start.3 = (bf16[48,5120]{1,0:T(8,128)(2,1)S(1)}, bf16[48,5120]{1,0:T(8,128)(2,1)S(1)}, u32[]{:S(2)}, u32[]{:S(2)}) collective-permute-start(bf16[48,5120]{1,0:T(8,128)(2,1)S(1)} %slice.9), channel_id=1, source_target_pairs={{0,384},{128,0},{256,128},{384,256},{1,385},{129,1},{257,129},{385... | collective-permute-start | bytes 1474568 | tf_op jit(solution)/shard_map/ppermute | solution.py:226
  52.0 23.3 %copy-start.3 = (bf16[64,5120]{1,0:T(8,128)(2,1)}, bf16[64,5120]{1,0:T(8,128)(2,1)S(1)}, u32[]{:S(2)}) copy-start(bf16[64,5120]{1,0:T(8,128)(2,1)S(1)} %collective-permute-done.refs_1_) | copy-start | bytes 1966084
  52.0 7.6 %collective-permute-start.1 = (bf16[16,5120]{1,0:T(8,128)(2,1)S(1)}, bf16[16,5120]{1,0:T(8,128)(2,1)S(1)}, u32[]{:S(2)}, u32[]{:S(2)}) collective-permute-start(bf16[16,5120]{1,0:T(8,128)(2,1)S(1)} %slice.8), channel_id=1, source_target_pairs={{0,128},{128,256},{256,384},{384,0},{1,129},{129,257},{257,385},{3... | collective-permute-start | bytes 491528 | tf_op jit(solution)/shard_map/ppermute | solution.py:226
  59.6 0.7 copy-start.5
  60.2 15.1 %copy-start.4 = (bf16[48,5120]{1,0:T(8,128)(2,1)}, bf16[48,5120]{1,0:T(8,128)(2,1)S(1)}, u32[]{:S(2)}) copy-start(bf16[48,5120]{1,0:T(8,128)(2,1)S(1)} %collective-permute-done.3.refs_3_) | copy-start | bytes 1474564
  63.2 12.1 %copy-start.1 = (bf16[64,40,256]{2,1,0:T(8,128)(2,1)}, bf16[64,40,256]{2,1,0:T(8,128)(2,1)S(1)}, u32[]{:S(2)}) copy-start(bf16[64,40,256]{2,1,0:T(8,128)(2,1)S(1)} %all-to-all-done.1) | copy-start | bytes 3932164
  63.2 12.1 %collective-permute-start.4 = (bf16[2560,256]{1,0:T(8,128)(2,1)S(1)}, bf16[2560,256]{1,0:T(8,128)(2,1)}, u32[]{:S(2)}, u32[]{:S(2)}) collective-permute-start(bf16[2560,256]{1,0:T(8,128)(2,1)S(1)} %bitcast.20), channel_id=1, source_target_pairs={{0,8},{8,0},{1,9},{9,1},{2,10},{10,2},{3,11},{11,3},{4,12},{12,4},... | collective-permute-start | bytes 3932168 | tf_op jit(solution)/shard_map/ppermute | solution.py:226
  69.9 14.5 %all-to-all-start.2 = ((bf16[16,32,128]{2,1,0:T(8,128)(2,1)}), bf16[16,32,128]{2,1,0:T(8,128)(2,1)S(1)}, u32[]{:S(2)}, u32[]{:S(2)}) async-start(bf16[16,32,128]{2,1,0:T(8,128)(2,1)} %get-tuple-element.12), calls=%async_computation.2 | async-start | bytes 262144 | tf_op jit(solution)/shard_map/all_to_all | solution.py:286
  84.5 1.0 copy-start

commit v8 on v6

--- a/solution.py
+++ b/solution.py
@@ -298,7 +298,7 @@
             pltpu.VMEM((1, HD), f32),
             pltpu.SemaphoreType.DMA((10,)),
         ],
-        compiler_params=pltpu.CompilerParams(vmem_limit_bytes=56 * 1024 * 1024),
+        compiler_params=pltpu.CompilerParams(vmem_limit_bytes=53 * 1024 * 1024),
         cost_estimate=pl.CostEstimate(
             flops=1400000000, bytes_accessed=8000000, transcendentals=0
         ),

time: 107 us -> 106 us (level)
  transfers between devices with their start and end apart: 7 -> 7, of which waited for: 5 -> 5; matrix products, arithmetic and copies ran while one was open for 0% -> 0% of each run, Pallas kernels for 5% -> 4%
where the time goes in v8:
time: 106 us; the launch traced here: 105 us
  starting transfers between devices  40 us (38%)
  blocking collectives  28.9 us (27%)
  waiting for transfers between devices  23.3 us (22%)
  Pallas kernels  9.92 us (9%)
  between operations  2.1 us (2%)
    all_to_all x1, blocking collectives, body(): parts = lax.all_to_all(parts.reshape(64, 8, 384), CTX, 0, 0, tiled=True)  18.4 us
    ppermute x5, starting transfers between devices, shift_by(): lax.ppermute(value, axis, [(i, (i + step) % size) for i in range(size)])  18 us
    ppermute x5, waiting for transfers between devices, shift_by(): lax.ppermute(value, axis, [(i, (i + step) % size) for i in range(size)])  17.8 us
    all_to_all x1, starting transfers between devices, body(): gathered = lax.all_to_all(weight, ('y', 'z'), 0, 0, tiled=True)  16.6 us
    all_to_all x1, blocking collectives, body(): bundle = lax.all_to_all(bundle, 'x', 0, 0, tiled=True)  10.6 us
    all_to_all x1, starting transfers between devices, body(): asked = lax.all_to_all(asked, ('y', 'c'), 0, 0, tiled=True)  5.38 us
    pallas_call x1, Pallas kernels, body(): pl.pallas_call(project, in_specs=[anywhere] * 10, out_specs=whole, out_sh...  4.64 us
    all_to_all x1, waiting for transfers between devices, body(): asked = lax.all_to_all(asked, ('y', 'c'), 0, 0, tiled=True)  4.47 us
  transfers between devices with their start and end apart: 7, of which 5 were waited for; matrix products, arithmetic and copies ran while one was open for 0% of the time, Pallas kernels for 4%

profile of v8, /device:TPU:1, one launch (start us, length us, event | category | flops | bytes accessed | tf_op | source)
XLA Modules:
  0.0 105.2 jit_solution(4464468715089939686)
XLA Ops:
  1.9 1.9 %shard_map.131 = bf16[4,288,128]{2,1,0:T(8,128)(2,1)} custom-call(bf16[10,1024]{1,0:T(8,128)(2,1)} %refs_0_.1, bf16[1,4096]{1,0:T(2,128)(2,1)} %bitcast.30, bf16[1,512]{1,0:T(2,128)(2,1)} %bitcast.31, bf16[1,512]{1,0:T(2,128)(2,1)} %bitcast.32, bf16[128,512]{1,0:T(8,128)(2,1)} %bitcast.28, bf16[128,512]{1,0:T(8,128)(2,1)} %bitcast.29, ...), custom_call_target="tpu_custom_call" | custom-call | tf_op jit(solution)/shard_map/pallas_call | solution.py:251
  3.8 10.6 %all_to_all.20.bundle.refs_1_ = bf16[4,288,128]{2,1,0:T(8,128)(2,1)S(1)} all-to-all(bf16[4,288,128]{2,1,0:T(8,128)(2,1)} %shard_map.131), channel_id=1, replica_groups=mesh['x'=4,'y'=8,'c'=2,'z'=8] {'x'}, dimensions={0} | all-to-all | bytes 589824 | tf_op jit(solution)/shard_map/all_to_all | solution.py:260
  14.4 1.2 %shard_map.132 = (bf16[64,40,256]{2,1,0:T(8,128)(2,1)}, bf16[16,32,128]{2,1,0:T(8,128)(2,1)}) custom-call(bf16[4,288,128]{2,1,0:T(8,128)(2,1)S(1)} %all_to_all.20.bundle.refs_1_), custom_call_target="tpu_custom_call" | custom-call | tf_op jit(solution)/shard_map/pallas_call | solution.py:262
  15.6 0.0 copy-start.5
  15.6 16.6 %all-to-all-start.1 = ((bf16[64,40,256]{2,1,0:T(8,128)(2,1)}), bf16[64,40,256]{2,1,0:T(8,128)(2,1)S(1)}, u32[]{:S(2)}, u32[]{:S(2)}) async-start(bf16[64,40,256]{2,1,0:T(8,128)(2,1)} %get-tuple-element.10), calls=%async_computation.1 | async-start | bytes 2621440 | tf_op jit(solution)/shard_map/all_to_all | solution.py:276
  32.2 0.0 copy-start
  32.2 0.0 copy-start.1
  32.2 0.0 copy-done.5
  32.2 2.9 %collective-permute-start.2 = (bf16[64,5120]{1,0:T(8,128)(2,1)S(1)}, bf16[64,5120]{1,0:T(8,128)(2,1)S(1)}, u32[]{:S(2)}, u32[]{:S(2)}) collective-permute-start(bf16[64,5120]{1,0:T(8,128)(2,1)S(1)} %bitcast.25), channel_id=1, source_target_pairs={{0,384},{128,0},{256,128},{384,256},{1,385},{129,1},{257,129},{385... | collective-permute-start | bytes 1966088 | tf_op jit(solution)/shard_map/ppermute | solution.py:226
  35.1 2.5 %collective-permute-start = (bf16[64,5120]{1,0:T(8,128)(2,1)S(1)}, bf16[64,5120]{1,0:T(8,128)(2,1)S(1)}, u32[]{:S(2)}, u32[]{:S(2)}) collective-permute-start(bf16[64,5120]{1,0:T(8,128)(2,1)S(1)} %bitcast.26), channel_id=1, source_target_pairs={{0,128},{128,256},{256,384},{384,0},{1,129},{129,257},{257,385},{3... | collective-permute-start | bytes 1966088 | tf_op jit(solution)/shard_map/ppermute | solution.py:226
  37.6 10.4 %collective-permute-done.2.refs_4_ = bf16[64,5120]{1,0:T(8,128)(2,1)S(1)} collective-permute-done((bf16[64,5120]{1,0:T(8,128)(2,1)S(1)}, bf16[64,5120]{1,0:T(8,128)(2,1)S(1)}, u32[]{:S(2)}, u32[]{:S(2)}) %collective-permute-start.2) | collective-permute-done | bytes 655392 | tf_op jit(solution)/shard_map/ppermute | solution.py:226
  48.0 0.0 copy-start.3
  48.0 4.0 %collective-permute-start.3 = (bf16[32,5120]{1,0:T(8,128)(2,1)S(1)}, bf16[32,5120]{1,0:T(8,128)(2,1)S(1)}, u32[]{:S(2)}, u32[]{:S(2)}) collective-permute-start(bf16[32,5120]{1,0:T(8,128)(2,1)S(1)} %slice.9), channel_id=1, source_target_pairs={{0,384},{128,0},{256,128},{384,256},{1,385},{129,1},{257,129},{385... | collective-permute-start | bytes 983048 | tf_op jit(solution)/shard_map/ppermute | solution.py:226
  52.1 0.0 collective-permute-done.refs_1_
  52.1 0.0 copy-start.4
  52.1 0.8 copy-done.4
  52.9 1.9 %collective-permute-start.1 = (bf16[32,5120]{1,0:T(8,128)(2,1)S(1)}, bf16[32,5120]{1,0:T(8,128)(2,1)S(1)}, u32[]{:S(2)}, u32[]{:S(2)}) collective-permute-start(bf16[32,5120]{1,0:T(8,128)(2,1)S(1)} %slice.8), channel_id=1, source_target_pairs={{0,128},{128,256},{256,384},{384,0},{1,129},{129,257},{257,385},{3... | collective-permute-start | bytes 983048 | tf_op jit(solution)/shard_map/ppermute | solution.py:226
  54.9 1.3 %collective-permute-done.3.refs_3_ = bf16[32,5120]{1,0:T(8,128)(2,1)S(1)} collective-permute-done((bf16[32,5120]{1,0:T(8,128)(2,1)S(1)}, bf16[32,5120]{1,0:T(8,128)(2,1)S(1)}, u32[]{:S(2)}, u32[]{:S(2)}) %collective-permute-start.3) | collective-permute-done | bytes 327712 | tf_op jit(solution)/shard_map/ppermute | solution.py:226
  56.2 0.0 copy-start.6
  56.2 6.1 %collective-permute-done.1.refs_2_ = bf16[32,5120]{1,0:T(8,128)(2,1)S(1)} collective-permute-done((bf16[32,5120]{1,0:T(8,128)(2,1)S(1)}, bf16[32,5120]{1,0:T(8,128)(2,1)S(1)}, u32[]{:S(2)}, u32[]{:S(2)}) %collective-permute-start.1) | collective-permute-done | bytes 327712 | tf_op jit(solution)/shard_map/ppermute | solution.py:226
  62.3 1.1 %all-to-all-done.1 = bf16[64,40,256]{2,1,0:T(8,128)(2,1)S(1)} async-done(((bf16[64,40,256]{2,1,0:T(8,128)(2,1)}), bf16[64,40,256]{2,1,0:T(8,128)(2,1)S(1)}, u32[]{:S(2)}, u32[]{:S(2)}) %all-to-all-start.1) | async-done | bytes 1310752 | tf_op jit(solution)/shard_map/all_to_all | solution.py:276
  63.3 0.0 copy-start.2
  63.3 6.7 %collective-permute-start.4 = (bf16[2560,256]{1,0:T(8,128)(2,1)S(1)}, bf16[2560,256]{1,0:T(8,128)(2,1)}, u32[]{:S(2)}, u32[]{:S(2)}) collective-permute-start(bf16[2560,256]{1,0:T(8,128)(2,1)S(1)} %bitcast.22), channel_id=1, source_target_pairs={{0,8},{8,0},{1,9},{9,1},{2,10},{10,2},{3,11},{11,3},{4,12},{12,4},... | collective-permute-start | bytes 3932168 | tf_op jit(solution)/shard_map/ppermute | solution.py:226
  70.1 5.4 %all-to-all-start.2 = ((bf16[16,32,128]{2,1,0:T(8,128)(2,1)}), bf16[16,32,128]{2,1,0:T(8,128)(2,1)S(1)}, u32[]{:S(2)}, u32[]{:S(2)}) async-start(bf16[16,32,128]{2,1,0:T(8,128)(2,1)} %get-tuple-element.12), calls=%async_computation.2 | async-start | bytes 262144 | tf_op jit(solution)/shard_map/all_to_all | solution.py:286
  75.4 0.0 collective-permute-done.4.refs_6_
  75.4 0.0 copy-done.3
  75.5 0.0 copy-done.6
  75.5 0.0 copy-done.2
  75.5 0.0 copy-done
  75.5 0.0 copy-done.1
  75.5 4.6 %shard_map.133.refs_2_ = bf16[512,256]{1,0:T(8,128)(2,1)S(1)} custom-call(bf16[64,5120]{1,0:T(8,128)(2,1)} %bitcast.24, bf16[64,5120]{1,0:T(8,128)(2,1)} %copy-done.4, bf16[32,5120]{1,0:T(8,128)(2,1)S(1)} %collective-permute-done.1.refs_2_, bf16[32,5120]{1,0:T(8,128)(2,1)} %copy-done.6, bf16[64,5120]{1,0:T(8,128)(2,1)} %copy-done.3, ...), custom_call_target="tpu_custom_call" | custom-call | flops 1400000000 | bytes 8000000 | tf_op jit(solution)/shard_map/pallas_call | solution.py:287
  80.1 4.5 %all-to-all-done.2.refs_0_ = bf16[16,32,128]{2,1,0:T(8,128)(2,1)S(1)} async-done(((bf16[16,32,128]{2,1,0:T(8,128)(2,1)}), bf16[16,32,128]{2,1,0:T(8,128)(2,1)S(1)}, u32[]{:S(2)}, u32[]{:S(2)}) %all-to-all-start.2) | async-done | bytes 131104 | tf_op jit(solution)/shard_map/all_to_all | solution.py:286
  84.6 1.2 %shard_map.134 = bf16[512,384]{1,0:T(8,128)(2,1)S(1)} custom-call(bf16[16,32,128]{2,1,0:T(8,128)(2,1)S(1)} %all-to-all-done.2.refs_0_, bf16[4,288,128]{2,1,0:T(8,128)(2,1)S(1)} %all_to_all.20.bundle.refs_1_, bf16[512,256]{1,0:T(8,128)(2,1)S(1)} %shard_map.133.refs_2_), custom_call_target="tpu_custom_call" | custom-call | tf_op jit(solution)/shard_map/pallas_call | solution.py:318
  85.8 18.4 %all_to_all.21 = bf16[64,8,384]{2,1,0:T(8,128)(2,1)S(1)} all-to-all(bf16[64,8,384]{2,1,0:T(8,128)(2,1)S(1)} %bitcast.18), channel_id=1, replica_groups=mesh['x'=4,'y'=8,'c'=2,'z'=8] {'x','y','c'}, dimensions={0} | all-to-all | bytes 786432 | tf_op jit(solution)/shard_map/all_to_all | solution.py:325
  104.1 1.0 shard_map.135
  (2 shorter events, 0.0 us)
Async XLA Ops:
  15.6 16.6 %copy-start.5 = (bf16[1,64,5120]{2,1,0:T(8,128)(2,1)S(1)}, bf16[1,64,5120]{2,1,0:T(8,128)(2,1)}, u32[]{:S(2)}) copy-start(bf16[1,64,5120]{2,1,0:T(8,128)(2,1)} %param.12) | copy-start | bytes 1966084
  15.6 47.7 %all-to-all-start.1 = ((bf16[64,40,256]{2,1,0:T(8,128)(2,1)}), bf16[64,40,256]{2,1,0:T(8,128)(2,1)S(1)}, u32[]{:S(2)}, u32[]{:S(2)}) async-start(bf16[64,40,256]{2,1,0:T(8,128)(2,1)} %get-tuple-element.10), calls=%async_computation.1 | async-start | bytes 2621440 | tf_op jit(solution)/shard_map/all_to_all | solution.py:276
  32.2 43.3 %copy-start = (bf16[1,2,32,512]{3,2,1,0:T(8,128)(2,1)S(1)}, bf16[1,2,32,512]{3,2,1,0:T(8,128)(2,1)}, u32[]{:S(2)}) copy-start(bf16[1,2,32,512]{3,2,1,0:T(8,128)(2,1)} %param.15) | copy-start | bytes 196612
  32.2 43.3 %copy-start.1 = (f32[128]{0:T(128)S(1)}, f32[128]{0:T(128)}, u32[]{:S(2)}) copy-start(f32[128]{0:T(128)} %param.16) | copy-start | bytes 1540
  32.2 15.8 %collective-permute-start.2 = (bf16[64,5120]{1,0:T(8,128)(2,1)S(1)}, bf16[64,5120]{1,0:T(8,128)(2,1)S(1)}, u32[]{:S(2)}, u32[]{:S(2)}) collective-permute-start(bf16[64,5120]{1,0:T(8,128)(2,1)S(1)} %bitcast.25), channel_id=1, source_target_pairs={{0,384},{128,0},{256,128},{384,256},{1,385},{129,1},{257,129},{385... | collective-permute-start | bytes 1966088 | tf_op jit(solution)/shard_map/ppermute | solution.py:226
  35.1 16.9 %collective-permute-start = (bf16[64,5120]{1,0:T(8,128)(2,1)S(1)}, bf16[64,5120]{1,0:T(8,128)(2,1)S(1)}, u32[]{:S(2)}, u32[]{:S(2)}) collective-permute-start(bf16[64,5120]{1,0:T(8,128)(2,1)S(1)} %bitcast.26), channel_id=1, source_target_pairs={{0,128},{128,256},{256,384},{384,0},{1,129},{129,257},{257,385},{3... | collective-permute-start | bytes 1966088 | tf_op jit(solution)/shard_map/ppermute | solution.py:226
  48.0 27.4 %copy-start.3 = (bf16[64,5120]{1,0:T(8,128)(2,1)}, bf16[64,5120]{1,0:T(8,128)(2,1)S(1)}, u32[]{:S(2)}) copy-start(bf16[64,5120]{1,0:T(8,128)(2,1)S(1)} %collective-permute-done.2.refs_4_) | copy-start | bytes 1966084
  48.0 8.1 %collective-permute-start.3 = (bf16[32,5120]{1,0:T(8,128)(2,1)S(1)}, bf16[32,5120]{1,0:T(8,128)(2,1)S(1)}, u32[]{:S(2)}, u32[]{:S(2)}) collective-permute-start(bf16[32,5120]{1,0:T(8,128)(2,1)S(1)} %slice.9), channel_id=1, source_target_pairs={{0,384},{128,0},{256,128},{384,256},{1,385},{129,1},{257,129},{385... | collective-permute-start | bytes 983048 | tf_op jit(solution)/shard_map/ppermute | solution.py:226
  52.1 0.9 copy-start.4
  52.9 9.3 %collective-permute-start.1 = (bf16[32,5120]{1,0:T(8,128)(2,1)S(1)}, bf16[32,5120]{1,0:T(8,128)(2,1)S(1)}, u32[]{:S(2)}, u32[]{:S(2)}) collective-permute-start(bf16[32,5120]{1,0:T(8,128)(2,1)S(1)} %slice.8), channel_id=1, source_target_pairs={{0,128},{128,256},{256,384},{384,0},{1,129},{129,257},{257,385},{3... | collective-permute-start | bytes 983048 | tf_op jit(solution)/shard_map/ppermute | solution.py:226
  56.2 19.3 %copy-start.6 = (bf16[32,5120]{1,0:T(8,128)(2,1)}, bf16[32,5120]{1,0:T(8,128)(2,1)S(1)}, u32[]{:S(2)}) copy-start(bf16[32,5120]{1,0:T(8,128)(2,1)S(1)} %collective-permute-done.3.refs_3_) | copy-start | bytes 983044
  63.3 12.1 %copy-start.2 = (bf16[64,40,256]{2,1,0:T(8,128)(2,1)}, bf16[64,40,256]{2,1,0:T(8,128)(2,1)S(1)}, u32[]{:S(2)}) copy-start(bf16[64,40,256]{2,1,0:T(8,128)(2,1)S(1)} %all-to-all-done.1) | copy-start | bytes 3932164
  63.3 12.1 %collective-permute-start.4 = (bf16[2560,256]{1,0:T(8,128)(2,1)S(1)}, bf16[2560,256]{1,0:T(8,128)(2,1)}, u32[]{:S(2)}, u32[]{:S(2)}) collective-permute-start(bf16[2560,256]{1,0:T(8,128)(2,1)S(1)} %bitcast.22), channel_id=1, source_target_pairs={{0,8},{8,0},{1,9},{9,1},{2,10},{10,2},{3,11},{11,3},{4,12},{12,4},... | collective-permute-start | bytes 3932168 | tf_op jit(solution)/shard_map/ppermute | solution.py:226
  70.1 14.5 %all-to-all-start.2 = ((bf16[16,32,128]{2,1,0:T(8,128)(2,1)}), bf16[16,32,128]{2,1,0:T(8,128)(2,1)S(1)}, u32[]{:S(2)}, u32[]{:S(2)}) async-start(bf16[16,32,128]{2,1,0:T(8,128)(2,1)} %get-tuple-element.12), calls=%async_computation.2 | async-start | bytes 262144 | tf_op jit(solution)/shard_map/all_to_all | solution.py:286
